TPU v7x, 32 devices: a whole 2x2x4 slice. The times are simulated.
32 devices in a mesh: section: 2 (over y), tensor: 4 (over x, core), dp: 4 (over z).
Axes of the slice: x: 2, y: 2, z: 4, core: 2. Of those that a mesh axis runs over, the one named last changes fastest.
Arguments:
- block_input: bfloat16 [2, 1024, 4, 767], P(None, 'tensor', 'dp'), may hold values from -6 to 6
- segments: int32 [2, 4, 1024], P(None, 'dp'), may hold values from 0 to 3, as said below
- cotangent: bfloat16 [2, 1024, 4, 767], P(None, 'tensor', 'dp'), may hold values from -6 to 6
- attn_gain: bfloat16 [2, 768], P('section'), may hold values from 0.5 to 1.5
- qkv_weight: bfloat16 [2, 768, 3, 768], P('section', None, None, 'tensor'), may hold values from -0.21875 to 0.21875
- qv_bias: bfloat16 [2, 2, 768], P('section', None, 'tensor'), may hold values from -0.59765625 to 0.59765625
- out_weight: bfloat16 [2, 768, 768], P('section', 'tensor'), may hold values from -1.25 to 1.25
- out_bias: bfloat16 [2, 768], P('section'), may hold values from -1.796875 to 1.796875
- mlp_gain: bfloat16 [2, 768], P('section'), may hold values from 0.5 to 1.5
- up_projection_weight: bfloat16 [2, 768, 3072], P('section', None, 'tensor'), may hold values from -0.21875 to 0.21875
- up_bias: bfloat16 [2, 3072], P('section', 'tensor'), may hold values from -1.796875 to 1.796875
- down_projection_weight: bfloat16 [2, 768, 3072], P('section', None, 'tensor'), may hold values from -0.109375 to 0.109375
- down_bias: bfloat16 [2, 768], P('section'), may hold values from -1.796875 to 1.796875
Outputs:
- activations: bfloat16 [2, 2, 1024, 4, 767], P('section', None, 'tensor', 'dp')
- entry_grads: float32 [2, 2, 1024, 4, 767], P('section', None, 'tensor', 'dp')
- attn_gain_grad: float32 [2, 768], P('section')
- qkv_weight_grad: float32 [2, 768, 3, 768], P('section', None, None, 'tensor')
- qv_bias_grad: float32 [2, 2, 768], P('section', None, 'tensor')
- out_weight_grad: float32 [2, 768, 768], P('section', 'tensor')
- out_bias_grad: float32 [2, 768], P('section')
- mlp_gain_grad: float32 [2, 768], P('section')
- up_weight_grad: float32 [2, 768, 3072], P('section', None, 'tensor')
- up_bias_grad: float32 [2, 3072], P('section', 'tensor')
- down_weight_grad: float32 [2, 768, 3072], P('section', None, 'tensor')
- down_bias_grad: float32 [2, 768], P('section')
Inputs may be any that keep to these rules, and one draw needn't show every extreme that they name: `segments`: along each packed row of 1024 positions the segment numbers start at 0, never fall, and rise by one at each document boundary.
All inputs are finite; a program needn't handle non-finite values.
Results may differ from a plain program's by a relative error of at most 0.035.
Values may be sent and summed in bfloat16 or wider, within the bound.
A program may use at most 192 MiB of HBM per device.

v0:
```python
import jax
import jax.numpy as jnp
from jax import lax
from jax.sharding import PartitionSpec as P

HD = 64


EPS = 1e-05
SCALE = 0.125
NEGATIVE = -1e30


def from_behind(array, axis, by):
    count = lax.axis_size(axis)
    pairs = [(i, i + by) for i in range(count) if 0 <= i + by < count]
    return lax.ppermute(array, axis, pairs)


def expand(residual):
    return jnp.concatenate([residual, -jnp.sum(residual, axis=-1, keepdims=True)], axis=-1)


def shrink(branch):
    return branch[..., :-1] - jnp.mean(branch, axis=-1, keepdims=True)


def shrink_back(grad):
    padded = jnp.concatenate([grad, jnp.zeros_like(grad[..., :1])], axis=-1)
    return padded - jnp.sum(grad, axis=-1, keepdims=True) / padded.shape[-1]


def crms(residual, gain):
    full = expand(residual)
    factor = lax.rsqrt(jnp.mean(full * full, axis=-1, keepdims=True) + EPS)
    return full * factor * gain


def gelu_tanh(value):
    return jax.nn.gelu(value, approximate=True)


def allowed_keys(segment):
    places = jnp.arange(segment.shape[-1])
    same = segment[:, :, None] == segment[:, None, :]
    causal = places[None, :] <= places[:, None]
    return (same & causal[None])[:, None]


def gather_rows(normed):
    return lax.all_gather(normed, "tensor", axis=0, tiled=True)


def sum_branch(term, row_count):
    return lax.psum_scatter(
        term(jnp.int32(0), lax.axis_size("tensor") * row_count).astype(jnp.bfloat16),
        "tensor",
        scatter_dimension=0,
        tiled=True,
    ).astype(jnp.float32)


def sum_normed(term, row_count):
    return lax.psum_scatter(
        term(jnp.int32(0), lax.axis_size("tensor") * row_count).astype(jnp.bfloat16),
        "tensor",
        scatter_dimension=0,
        tiled=True,
    ).astype(jnp.float32)


def fold_rows(grad, step_fn, initial):
    return step_fn(initial, lax.all_gather(grad, "tensor", axis=0, tiled=True), jnp.int32(0))


def masked_scores(query_heads, key_heads, segment):
    scores = (
        jnp.einsum("qshd,kshd->shqk", query_heads, key_heads, preferred_element_type=jnp.float32)
        * SCALE
    )
    return jnp.where(allowed_keys(segment), scores, NEGATIVE)


def run_layer(residual, segment, params):
    (
        attn_gain,
        qkv_weight,
        qv_bias,
        out_weight,
        out_bias,
        mlp_gain,
        up_projection_weight,
        up_bias,
        down_projection_weight,
        down_bias,
    ) = params
    share_rows = residual.shape[0]
    normed = crms(residual, attn_gain).astype(jnp.bfloat16)
    normed_all = gather_rows(normed)
    project = jnp.einsum(
        "lsd,dte->lste", normed_all, qkv_weight, preferred_element_type=jnp.float32
    )
    query = (project[:, :, 0] + qv_bias[0]).astype(jnp.bfloat16)
    keys = project[:, :, 1].astype(jnp.bfloat16)
    values = (project[:, :, 2] + qv_bias[1]).astype(jnp.bfloat16)
    length, seqs, width = query.shape
    head_shape = (length, seqs, width // HD, HD)
    masked = masked_scores(query.reshape(head_shape), keys.reshape(head_shape), segment)
    highest = jnp.max(masked, axis=-1, keepdims=True)
    powers = jnp.exp(masked - highest)
    totals = jnp.sum(powers, axis=-1, keepdims=True)
    probs = powers / totals
    logsum = highest + jnp.log(totals)
    context = (
        jnp.einsum(
            "shqk,kshd->qshd",
            probs.astype(jnp.bfloat16),
            values.reshape(head_shape),
            preferred_element_type=jnp.float32,
        )
        .reshape(length, seqs, width)
        .astype(jnp.bfloat16)
    )

    def out_term(start, count):
        return jnp.einsum("lse,ed->lsd", context, out_weight, preferred_element_type=jnp.float32)

    attn_out = sum_branch(out_term, share_rows) + out_bias
    middle = residual + shrink(attn_out)
    normed2 = crms(middle, mlp_gain).astype(jnp.bfloat16)
    second_normed_full = gather_rows(normed2)
    pre = (
        jnp.einsum(
            "eqi,in->eqn",
            second_normed_full,
            up_projection_weight,
            preferred_element_type=jnp.float32,
        )
        + up_bias
    )
    hidden_state = gelu_tanh(pre).astype(jnp.bfloat16)

    def down_term(start, count):
        return jnp.einsum(
            "gjt,ct->gjc", hidden_state, down_projection_weight, preferred_element_type=jnp.float32
        )

    mlp_out = sum_branch(down_term, share_rows) + down_bias
    result = middle + shrink(mlp_out)
    kept_state = (
        residual,
        normed_all,
        query,
        keys,
        values,
        logsum,
        context,
        middle,
        second_normed_full,
        pre,
        hidden_state,
    )
    return (result, kept_state)


def layer_back(grad_out, kept_state, segment, params):
    (
        attn_gain,
        qkv_weight,
        qv_bias,
        out_weight,
        out_bias,
        mlp_gain,
        up_projection_weight,
        up_bias,
        down_projection_weight,
        down_bias,
    ) = params
    (
        residual,
        normed_all,
        query,
        keys,
        values,
        logsum,
        context,
        middle,
        second_normed_full,
        pre,
        hidden_state,
    ) = kept_state
    share_rows = residual.shape[0]
    grad_mlp = shrink_back(grad_out).astype(jnp.bfloat16)
    down_bias_grad = jnp.sum(grad_mlp.astype(jnp.float32), axis=(0, 1))

    def down_step(carry, section_slice, start):
        part_rows = jnp.einsum(
            "eqi,in->eqn", section_slice, down_projection_weight, preferred_element_type=jnp.float32
        )
        weight_gradient = jnp.einsum(
            "aez,aec->zc", section_slice, hidden_state, preferred_element_type=jnp.float32
        )
        return (part_rows, weight_gradient)

    initial = (
        jnp.zeros(hidden_state.shape, jnp.float32),
        jnp.zeros(down_projection_weight.shape, jnp.float32),
    )
    grad_hidden, down_weight_grad = fold_rows(grad_mlp, down_step, initial)
    gradient_before_norm = jax.vjp(gelu_tanh, pre)[1](grad_hidden)[0].astype(jnp.bfloat16)
    up_bias_grad = jnp.sum(gradient_before_norm.astype(jnp.float32), axis=(0, 1))
    up_weight_grad = jnp.einsum(
        "aez,aec->zc", second_normed_full, gradient_before_norm, preferred_element_type=jnp.float32
    )

    def up_term(start, count):
        return jnp.einsum(
            "gjt,ct->gjc",
            gradient_before_norm,
            up_projection_weight,
            preferred_element_type=jnp.float32,
        )

    grad_normed2 = sum_normed(up_term, share_rows)
    middle_norm_grad, mlp_gain_grad = jax.vjp(crms, middle, mlp_gain)[1](grad_normed2)
    grad_middle = grad_out + middle_norm_grad
    grad_attn = shrink_back(grad_middle).astype(jnp.bfloat16)
    out_bias_grad = jnp.sum(grad_attn.astype(jnp.float32), axis=(0, 1))

    def out_step(carry, section_slice, start):
        part_rows = jnp.einsum(
            "lsd,ed->lse", section_slice, out_weight, preferred_element_type=jnp.float32
        )
        weight_gradient = jnp.einsum(
            "lse,lsd->ed", context, section_slice, preferred_element_type=jnp.float32
        )
        return (part_rows, weight_gradient)

    initial = (jnp.zeros(context.shape, jnp.float32), jnp.zeros(out_weight.shape, jnp.float32))
    grad_context, out_weight_grad = fold_rows(grad_attn, out_step, initial)
    length, seqs, width = query.shape
    head_shape = (length, seqs, width // HD, HD)
    query_heads = query.reshape(head_shape)
    key_heads = keys.reshape(head_shape)
    value_heads = values.reshape(head_shape)
    grad_heads = grad_context.astype(jnp.bfloat16).reshape(head_shape)
    probs = jnp.exp(masked_scores(query_heads, key_heads, segment) - logsum)
    value_grad = jnp.einsum(
        "shqk,qshd->kshd",
        probs.astype(jnp.bfloat16),
        grad_heads,
        preferred_element_type=jnp.float32,
    )
    grad_probs = jnp.einsum(
        "qshd,kshd->shqk", grad_heads, value_heads, preferred_element_type=jnp.float32
    )
    centre = jnp.sum(grad_probs * probs, axis=-1, keepdims=True)
    grad_scores = (probs * (grad_probs - centre)).astype(jnp.bfloat16)
    query_grad = (
        jnp.einsum("shqk,kshd->qshd", grad_scores, key_heads, preferred_element_type=jnp.float32)
        * SCALE
    )
    key_grad = (
        jnp.einsum("shqk,qshd->kshd", grad_scores, query_heads, preferred_element_type=jnp.float32)
        * SCALE
    )
    grad_qkv = jnp.stack(
        [
            query_grad.reshape(length, seqs, width),
            key_grad.reshape(length, seqs, width),
            value_grad.reshape(length, seqs, width),
        ],
        axis=2,
    ).astype(jnp.bfloat16)
    qv_bias_grad = jnp.sum(grad_qkv[:, :, 0::2].astype(jnp.float32), axis=(0, 1))
    qkv_weight_grad = jnp.einsum(
        "lsd,lste->dte", normed_all, grad_qkv, preferred_element_type=jnp.float32
    )

    def qkv_term(start, count):
        return jnp.einsum("lste,dte->lsd", grad_qkv, qkv_weight, preferred_element_type=jnp.float32)

    grad_normed = sum_normed(qkv_term, share_rows)
    residual_norm_grad, attn_gain_grad = jax.vjp(crms, residual, attn_gain)[1](grad_normed)
    grad_in = grad_middle + residual_norm_grad
    grads = (
        attn_gain_grad,
        qkv_weight_grad,
        qv_bias_grad,
        out_weight_grad,
        out_bias_grad,
        mlp_gain_grad,
        up_weight_grad,
        up_bias_grad,
        down_weight_grad,
        down_bias_grad,
    )
    return (grad_in, grads)


def per_device(
    block_input,
    segments,
    cotangent,
    attn_gain,
    qkv_weight,
    qv_bias,
    out_weight,
    out_bias,
    mlp_gain,
    up_projection_weight,
    up_bias,
    down_projection_weight,
    down_bias,
):
    section_index = lax.axis_index("section")
    first_section = section_index == 0
    micro_count = block_input.shape[0]
    up_whole = up_projection_weight[0]
    up_bias_whole = up_bias[0]
    down_whole = down_projection_weight[0]
    params = (
        attn_gain[0].astype(jnp.float32),
        qkv_weight[0],
        qv_bias[0].astype(jnp.float32),
        out_weight[0],
        out_bias[0].astype(jnp.float32),
        mlp_gain[0].astype(jnp.float32),
        up_whole,
        up_bias_whole.astype(jnp.float32),
        down_whole,
        down_bias[0].astype(jnp.float32),
    )
    received = jnp.zeros(block_input.shape[1:], jnp.bfloat16)
    layer_inputs = []
    layer_outputs = []
    kept_list = []
    for tick in range(micro_count + 1):
        own_input = block_input[min(tick, micro_count - 1)]
        segment = jnp.where(
            first_section, segments[min(tick, micro_count - 1)], segments[max(tick - 1, 0)]
        )
        layer_entry = jnp.where(first_section, own_input, received).astype(jnp.float32)
        result, kept_state = run_layer(layer_entry, segment, params)
        outgoing = result.astype(jnp.bfloat16)
        layer_inputs.append(layer_entry)
        layer_outputs.append(outgoing)
        kept_list.append(kept_state)
        if tick < micro_count:
            received = from_behind(outgoing, "section", 1)
    activations = jnp.stack(
        [
            jnp.where(first_section, layer_outputs[micro], layer_outputs[micro + 1])
            for micro in range(micro_count)
        ]
    )[None]
    totals = jax.tree.map(lambda leaf: jnp.zeros(leaf.shape, jnp.float32), params)
    arrived = jnp.zeros(block_input.shape[1:], jnp.bfloat16)
    grads_in = []
    for tick in range(micro_count + 1):
        later = min(tick, micro_count - 1)
        earlier = max(tick - 1, 0)
        active = jnp.where(first_section, tick >= 1, tick < micro_count).astype(jnp.float32)
        segment = jnp.where(first_section, segments[earlier], segments[later])
        grad_out = jnp.where(first_section, arrived, cotangent[later]).astype(jnp.float32)
        layer_entry = jnp.where(first_section, layer_inputs[earlier], layer_inputs[later + 1])
        kept_state = run_layer(layer_entry, segment, params)[1]
        grad_in, grads = layer_back(grad_out, kept_state, segment, params)
        totals = jax.tree.map(lambda total, grad: total + active * grad, totals, grads)
        grads_in.append(grad_in)
        if tick < micro_count:
            arrived = from_behind(grad_in.astype(jnp.bfloat16), "section", -1)
    entry_grads = jnp.stack(
        [
            jnp.where(
                first_section,
                grads_in[micro + 1],
                grads_in[micro].astype(jnp.bfloat16).astype(jnp.float32),
            )
            for micro in range(micro_count)
        ]
    )[None]
    (
        gain_one,
        qkv_total,
        qv_total,
        out_total,
        out_bias_total,
        gain_two,
        up_total,
        up_bias_total,
        down_total,
        down_bias_total,
    ) = totals
    qkv_total, qv_total, out_total, up_total, up_bias_total, down_total = (
        lax.psum(qkv_total.astype(jnp.bfloat16), "dp").astype(jnp.float32),
        lax.psum(qv_total.astype(jnp.bfloat16), "dp").astype(jnp.float32),
        lax.psum(out_total.astype(jnp.bfloat16), "dp").astype(jnp.float32),
        lax.psum(up_total.astype(jnp.bfloat16), "dp").astype(jnp.float32),
        lax.psum(up_bias_total.astype(jnp.bfloat16), "dp").astype(jnp.float32),
        lax.psum(down_total.astype(jnp.bfloat16), "dp").astype(jnp.float32),
    )
    gain_one, out_bias_total, gain_two, down_bias_total = lax.psum(
        (gain_one, out_bias_total, gain_two, down_bias_total), ("tensor", "dp")
    )
    return (
        activations,
        entry_grads,
        gain_one[None],
        qkv_total[None],
        qv_total[None],
        out_total[None],
        out_bias_total[None],
        gain_two[None],
        up_total[None],
        up_bias_total[None],
        down_total[None],
        down_bias_total[None],
    )


def solution(mesh):
    in_specs = (
        P(None, "tensor", "dp", None),
        P(None, "dp", None),
        P(None, "tensor", "dp", None),
        P("section", None),
        P("section", None, None, "tensor"),
        P("section", None, "tensor"),
        P("section", "tensor", None),
        P("section", None),
        P("section", None),
        P("section", None, "tensor"),
        P("section", "tensor"),
        P("section", None, "tensor"),
        P("section", None),
    )
    out_specs = (
        P("section", None, "tensor", "dp", None),
        P("section", None, "tensor", "dp", None),
        P("section", None),
        P("section", None, None, "tensor"),
        P("section", None, "tensor"),
        P("section", "tensor", None),
        P("section", None),
        P("section", None),
        P("section", None, "tensor"),
        P("section", "tensor"),
        P("section", None, "tensor"),
        P("section", None),
    )
    return jax.shard_map(
        per_device, mesh=mesh, in_specs=in_specs, out_specs=out_specs, check_vma=False
    )
```

profile of v0, /device:TPU:0, one launch (start us, length us, event | category | flops | bytes accessed | tf_op | source)
XLA Modules:
  0.0 1221.5 jit_solution(11711792966002891601)
XLA Ops:
  15.1 21.0 %all-gather.19.cloned.1.call-done = bf16[1024,1,768]{2,0,1:T(8,128)(2,1)} async-done(((bf16[256,1,768]{2,0,1:T(8,128)(2,1)}), bf16[1024,1,768]{2,0,1:T(8,128)(2,1)}) %all-gather.19.cloned.1.call-update) | async-done | bytes 1572880 | tf_op jit(solution)/shard_map/all_gather | solution.py:51
  59.0 28.2 %reduce-scatter.16.cloned.1.call-done = bf16[256,1,768]{2,0,1:T(8,128)(2,1)} async-done(((bf16[1024,1,768]{2,0,1:T(8,128)(2,1)}), bf16[256,1,768]{2,0,1:T(8,128)(2,1)}) %reduce-scatter.16.cloned.1.call-update) | async-done | bytes 393232 | tf_op jit(solution)/shard_map/reduce_scatter | solution.py:55
  90.2 19.5 %all-gather.21.cloned.1.call-done = bf16[1024,1,768]{2,0,1:T(8,128)(2,1)} async-done(((bf16[256,1,768]{2,0,1:T(8,128)(2,1)}), bf16[1024,1,768]{2,0,1:T(8,128)(2,1)}) %all-gather.21.cloned.1.call-update) | async-done | bytes 1572880 | tf_op jit(solution)/shard_map/all_gather | solution.py:51
  115.7 28.2 %reduce-scatter.18.cloned.1.call-done = bf16[256,1,768]{2,0,1:T(8,128)(2,1)} async-done(((bf16[1024,1,768]{2,0,1:T(8,128)(2,1)}), bf16[256,1,768]{2,0,1:T(8,128)(2,1)}) %reduce-scatter.18.cloned.1.call-update) | async-done | bytes 393232 | tf_op jit(solution)/shard_map/reduce_scatter | solution.py:55
  165.6 19.7 %all-gather.23.cloned.1.call-done = bf16[1024,1,768]{2,0,1:T(8,128)(2,1)} async-done(((bf16[256,1,768]{2,0,1:T(8,128)(2,1)}), bf16[1024,1,768]{2,0,1:T(8,128)(2,1)}) %all-gather.23.cloned.1.call-update) | async-done | bytes 1572880 | tf_op jit(solution)/shard_map/all_gather | solution.py:51
  208.4 27.9 %reduce-scatter.20.cloned.1.call-done = bf16[256,1,768]{2,0,1:T(8,128)(2,1)} async-done(((bf16[1024,1,768]{2,0,1:T(8,128)(2,1)}), bf16[256,1,768]{2,0,1:T(8,128)(2,1)}) %reduce-scatter.20.cloned.1.call-update) | async-done | bytes 393232 | tf_op jit(solution)/shard_map/reduce_scatter | solution.py:55
  239.1 19.8 %all-gather.25.cloned.1.call-done = bf16[1024,1,768]{2,0,1:T(8,128)(2,1)} async-done(((bf16[256,1,768]{2,0,1:T(8,128)(2,1)}), bf16[1024,1,768]{2,0,1:T(8,128)(2,1)}) %all-gather.25.cloned.1.call-update) | async-done | bytes 1572880 | tf_op jit(solution)/shard_map/all_gather | solution.py:51
  264.8 28.2 %reduce-scatter.22.cloned.1.call-done = bf16[256,1,768]{2,0,1:T(8,128)(2,1)} async-done(((bf16[1024,1,768]{2,0,1:T(8,128)(2,1)}), bf16[256,1,768]{2,0,1:T(8,128)(2,1)}) %reduce-scatter.22.cloned.1.call-update) | async-done | bytes 393232 | tf_op jit(solution)/shard_map/reduce_scatter | solution.py:55
  320.7 16.3 %all-gather.27.cloned.1.call-done = bf16[1024,1,768]{2,0,1:T(8,128)(2,1)} async-done(((bf16[256,1,768]{2,0,1:T(8,128)(2,1)}), bf16[1024,1,768]{2,0,1:T(8,128)(2,1)}) %all-gather.27.cloned.1.call-update) | async-done | bytes 1572880 | tf_op jit(solution)/shard_map/all_gather | solution.py:51
  431.8 31.3 %reduce-scatter.28.cloned.1.call-done = bf16[256,1,768]{2,0,1:T(8,128)(2,1)} async-done(((bf16[1024,1,768]{2,0,1:T(8,128)(2,1)}), bf16[256,1,768]{2,0,1:T(8,128)(2,1)}) %reduce-scatter.28.cloned.1.call-update) | async-done | bytes 393232 | tf_op jit(solution)/shard_map/reduce_scatter | solution.py:55
  463.1 31.1 %reduce-scatter.34.cloned.1.call-done = bf16[256,1,768]{2,0,1:T(8,128)(2,1)} async-done(((bf16[1024,1,768]{2,0,1:T(8,128)(2,1)}), bf16[256,1,768]{2,0,1:T(8,128)(2,1)}) %reduce-scatter.34.cloned.1.call-update) | async-done | bytes 393232 | tf_op jit(solution)/shard_map/reduce_scatter | solution.py:55
  494.2 31.3 %reduce-scatter.40.cloned.1.call-done = bf16[256,1,768]{2,0,1:T(8,128)(2,1)} async-done(((bf16[1024,1,768]{2,0,1:T(8,128)(2,1)}), bf16[256,1,768]{2,0,1:T(8,128)(2,1)}) %reduce-scatter.40.cloned.1.call-update) | async-done | bytes 393232 | tf_op jit(solution)/shard_map/reduce_scatter | solution.py:55
  564.3 17.2 %all-gather.31.cloned.1.call-done = bf16[1024,1,768]{2,0,1:T(8,128)(2,1)} async-done(((bf16[256,1,768]{2,0,1:T(8,128)(2,1)}), bf16[1024,1,768]{2,0,1:T(8,128)(2,1)}) %all-gather.31.cloned.1.call-update) | async-done | bytes 1572880 | tf_op jit(solution)/shard_map/all_gather | solution.py:73
  591.8 28.3 %reduce-scatter.30.cloned.1.call-done = bf16[256,1,768]{2,0,1:T(8,128)(2,1)} async-done(((bf16[1024,1,768]{2,0,1:T(8,128)(2,1)}), bf16[256,1,768]{2,0,1:T(8,128)(2,1)}) %reduce-scatter.30.cloned.1.call-update) | async-done | bytes 393232 | tf_op jit(solution)/shard_map/reduce_scatter | solution.py:64
  626.0 20.7 %all-gather.37.cloned.1.call-done = bf16[1024,1,768]{2,0,1:T(8,128)(2,1)} async-done(((bf16[256,1,768]{2,0,1:T(8,128)(2,1)}), bf16[1024,1,768]{2,0,1:T(8,128)(2,1)}) %all-gather.37.cloned.1.call-update) | async-done | bytes 1572880 | tf_op jit(solution)/shard_map/all_gather | solution.py:73
  676.5 27.6 %reduce-scatter.32.cloned.1.call-done = bf16[256,1,768]{2,0,1:T(8,128)(2,1)} async-done(((bf16[1024,1,768]{2,0,1:T(8,128)(2,1)}), bf16[256,1,768]{2,0,1:T(8,128)(2,1)}) %reduce-scatter.32.cloned.1.call-update) | async-done | bytes 393232 | tf_op jit(solution)/shard_map/reduce_scatter | solution.py:64
  729.7 17.4 %all-gather.39.cloned.1.call-done = bf16[1024,1,768]{2,0,1:T(8,128)(2,1)} async-done(((bf16[256,1,768]{2,0,1:T(8,128)(2,1)}), bf16[1024,1,768]{2,0,1:T(8,128)(2,1)}) %all-gather.39.cloned.1.call-update) | async-done | bytes 1572880 | tf_op jit(solution)/shard_map/all_gather | solution.py:73
  757.2 28.3 %reduce-scatter.36.cloned.1.call-done = bf16[256,1,768]{2,0,1:T(8,128)(2,1)} async-done(((bf16[1024,1,768]{2,0,1:T(8,128)(2,1)}), bf16[256,1,768]{2,0,1:T(8,128)(2,1)}) %reduce-scatter.36.cloned.1.call-update) | async-done | bytes 393232 | tf_op jit(solution)/shard_map/reduce_scatter | solution.py:64
  792.7 19.7 %all-gather.45.cloned.1.call-done = bf16[1024,1,768]{2,0,1:T(8,128)(2,1)} async-done(((bf16[256,1,768]{2,0,1:T(8,128)(2,1)}), bf16[1024,1,768]{2,0,1:T(8,128)(2,1)}) %all-gather.45.cloned.1.call-update) | async-done | bytes 1572880 | tf_op jit(solution)/shard_map/all_gather | solution.py:73
  842.1 27.7 %reduce-scatter.38.cloned.1.call-done = bf16[256,1,768]{2,0,1:T(8,128)(2,1)} async-done(((bf16[1024,1,768]{2,0,1:T(8,128)(2,1)}), bf16[256,1,768]{2,0,1:T(8,128)(2,1)}) %reduce-scatter.38.cloned.1.call-update) | async-done | bytes 393232 | tf_op jit(solution)/shard_map/reduce_scatter | solution.py:64
  895.9 17.3 %all-gather.47.cloned.1.call-done = bf16[1024,1,768]{2,0,1:T(8,128)(2,1)} async-done(((bf16[256,1,768]{2,0,1:T(8,128)(2,1)}), bf16[1024,1,768]{2,0,1:T(8,128)(2,1)}) %all-gather.47.cloned.1.call-update) | async-done | bytes 1572880 | tf_op jit(solution)/shard_map/all_gather | solution.py:73
  924.5 26.4 %reduce-scatter.42.cloned.1.call-done = bf16[256,1,768]{2,0,1:T(8,128)(2,1)} async-done(((bf16[1024,1,768]{2,0,1:T(8,128)(2,1)}), bf16[256,1,768]{2,0,1:T(8,128)(2,1)}) %reduce-scatter.42.cloned.1.call-update) | async-done | bytes 393232 | tf_op jit(solution)/shard_map/reduce_scatter | solution.py:64
  1078.6 62.3 %all-reduce.6 = (f32[1,768]{1,0:T(1,128)}, f32[1,768]{1,0:T(1,128)}, f32[1,768]{1,0:T(1,128)}, f32[1,768]{1,0:T(1,128)}) all-reduce(f32[1,768]{1,0:T(1,128)S(1)} %broadcast_in_dim.153, f32[1,768]{1,0:T(1,128)S(1)} %broadcast_in_dim.160, ...), channel_id=1, replica_groups=mesh['section'=2,'tensor'=4,'dp'=4] {'tensor','dp'}, use_global_device_ids=true, to_apply=%region_78.79 | all-reduce | flops 3072 | bytes 24576 | tf_op jit(solution)/shard_map/psum | solution.py:403
  1140.9 66.4 %all-reduce.11.cloned.1.call-done = (bf16[1,768,3,192]{1,3,2,0:T(8,128)(2,1)}, bf16[1,192,768]{2,1,0:T(8,128)(2,1)}, bf16[1,768,768]{2,1,0:T(8,128)(2,1)}, bf16[1,768,768]{2,1,0:T(8,128)(2,1)}) async-done(((bf16[1,768,3,192]{1,3,2,0:T(8,128)(2,1)}, bf16[1,192,768]{2,1,0:T(8,128)(2,1)}, bf16[1,768,768]{2,1,0:T(8,128)(2,1)}, bf16[1,768,768]{2,1,0:T(8,128)(2,1)}), (bf16[1,768,3,192]{1,3,2,0:T(8,128)(2,1)}, ...) | async-done | bytes 3538960 | tf_op jit(solution)/shard_map/psum | solution.py:396
  (740 shorter events, 542.1 us)
Async XLA Ops:
  13.6 73.7 %reduce-scatter.16.cloned.1.call-start = ((), (), s32[]{:S(2)}) async-start(), calls=%async_computation.16 | async-start | bytes 1966080 | tf_op jit(solution)/shard_map/reduce_scatter | solution.py:55
  115.6 69.6 %all-gather.23.cloned.1.call-start = ((), (), s32[]{:S(2)}) async-start(), calls=%async_computation.19 | async-start | bytes 1966080 | tf_op jit(solution)/shard_map/all_gather | solution.py:51
  163.4 72.9 %reduce-scatter.20.cloned.1.call-start = ((), (), s32[]{:S(2)}) async-start(), calls=%async_computation.20 | async-start | bytes 1966080 | tf_op jit(solution)/shard_map/reduce_scatter | solution.py:55
  264.8 72.2 %all-gather.27.cloned.1.call-start = ((), (), s32[]{:S(2)}) async-start(), calls=%async_computation.23 | async-start | bytes 1966080 | tf_op jit(solution)/shard_map/all_gather | solution.py:51
  316.5 63.4 %all-gather.41.cloned.1.call-start = ((), (), s32[]{:S(2)}) async-start(), calls=%async_computation.35 | async-start | bytes 1966080 | tf_op jit(solution)/shard_map/all_gather | solution.py:51
  317.3 83.8 %all-gather.49.cloned.1.call-start = ((), (), s32[]{:S(2)}) async-start(), calls=%async_computation.42 | async-start | bytes 1966080 | tf_op jit(solution)/shard_map/all_gather | solution.py:51
  320.5 111.3 %reduce-scatter.24.cloned.1.call-start = ((), (), s32[]{:S(2)}) async-start(), calls=%async_computation.24 | async-start | bytes 1966080 | tf_op jit(solution)/shard_map/reduce_scatter | solution.py:55
  359.8 103.2 %reduce-scatter.28.cloned.1.call-start = ((), (), s32[]{:S(2)}) async-start(), calls=%async_computation.29 | async-start | bytes 1966080 | tf_op jit(solution)/shard_map/reduce_scatter | solution.py:55
  376.7 117.5 %reduce-scatter.34.cloned.1.call-start = ((), (), s32[]{:S(2)}) async-start(), calls=%async_computation.36 | async-start | bytes 1966080 | tf_op jit(solution)/shard_map/reduce_scatter | solution.py:55
  396.5 129.0 %reduce-scatter.40.cloned.1.call-start = ((), (), s32[]{:S(2)}) async-start(), calls=%async_computation.43 | async-start | bytes 1966080 | tf_op jit(solution)/shard_map/reduce_scatter | solution.py:55
  418.0 141.9 %all-gather.35.cloned.1.call-start = ((), (), s32[]{:S(2)}) async-start(), calls=%async_computation.30 | async-start | bytes 1966080 | tf_op jit(solution)/shard_map/all_gather | solution.py:51
  548.0 72.1 %reduce-scatter.30.cloned.1.call-start = ((), (), s32[]{:S(2)}) async-start(), calls=%async_computation.31 | async-start | bytes 1966080 | tf_op jit(solution)/shard_map/reduce_scatter | solution.py:64
  591.7 55.0 %all-gather.37.cloned.1.call-start = ((), (), s32[]{:S(2)}) async-start(), calls=%async_computation.32 | async-start | bytes 1966080 | tf_op jit(solution)/shard_map/all_gather | solution.py:73
  625.9 78.1 %reduce-scatter.32.cloned.1.call-start = ((), (), s32[]{:S(2)}) async-start(), calls=%async_computation.33 | async-start | bytes 1966080 | tf_op jit(solution)/shard_map/reduce_scatter | solution.py:64
  676.4 70.7 %all-gather.39.cloned.1.call-start = ((), (), s32[]{:S(2)}) async-start(), calls=%async_computation.34 | async-start | bytes 1966080 | tf_op jit(solution)/shard_map/all_gather | solution.py:73
  724.0 61.5 %reduce-scatter.36.cloned.1.call-start = ((), (), s32[]{:S(2)}) async-start(), calls=%async_computation.38 | async-start | bytes 1966080 | tf_op jit(solution)/shard_map/reduce_scatter | solution.py:64
  757.2 55.2 %all-gather.45.cloned.1.call-start = ((), (), s32[]{:S(2)}) async-start(), calls=%async_computation.39 | async-start | bytes 1966080 | tf_op jit(solution)/shard_map/all_gather | solution.py:73
  792.6 77.1 %reduce-scatter.38.cloned.1.call-start = ((), (), s32[]{:S(2)}) async-start(), calls=%async_computation.40 | async-start | bytes 1966080 | tf_op jit(solution)/shard_map/reduce_scatter | solution.py:64
  842.0 71.3 %all-gather.47.cloned.1.call-start = ((), (), s32[]{:S(2)}) async-start(), calls=%async_computation.41 | async-start | bytes 1966080 | tf_op jit(solution)/shard_map/all_gather | solution.py:73
  888.4 62.6 %reduce-scatter.42.cloned.1.call-start = ((), (), s32[]{:S(2)}) async-start(), calls=%async_computation.45 | async-start | bytes 1966080 | tf_op jit(solution)/shard_map/reduce_scatter | solution.py:64
  957.7 67.3 %all-gather.29.cloned.1.call-start = ((), (), s32[]{:S(2)}) async-start(), calls=%async_computation.25 | async-start | bytes 1966080 | tf_op jit(solution)/shard_map/all_gather | solution.py:51
  963.2 100.9 %reduce-scatter.44.cloned.1.call-start = ((), (), s32[]{:S(2)}) async-start(), calls=%async_computation.47 | async-start | bytes 1966080 | tf_op jit(solution)/shard_map/reduce_scatter | solution.py:64
  1007.2 67.1 %reduce-scatter.26.cloned.1.call-start = ((), (), s32[]{:S(2)}) async-start(), calls=%async_computation.26 | async-start | bytes 1966080 | tf_op jit(solution)/shard_map/reduce_scatter | solution.py:55
  1030.9 176.4 %all-reduce.11.cloned.1.call-start = ((), (), s32[]{:S(2)}) async-start(), calls=%async_computation.48 | async-start | bytes 7077888 | tf_op jit(solution)/shard_map/psum | solution.py:396
  (204 other events, 3207.5 us)
Sparse Core Ops, SparseCore 0:
  13.7 22.3 all-gather.18
  59.0 28.1 reduce-scatter.15
  115.8 28.1 reduce-scatter.17
  163.5 21.7 all-gather.22
  208.1 28.1 reduce-scatter.19
  264.9 28.1 reduce-scatter.21
  316.1 20.8 all-gather.26
  360.2 19.6 all-gather.40
  403.6 28.1 reduce-scatter.23
  434.9 28.1 reduce-scatter.27
  466.0 28.1 reduce-scatter.33
  497.3 28.1 reduce-scatter.39
  540.2 19.6 all-gather.34
  591.8 28.1 reduce-scatter.29
  626.1 20.6 all-gather.36
  675.8 28.1 reduce-scatter.31
  757.3 28.1 reduce-scatter.35
  841.5 28.1 reduce-scatter.37
  871.7 19.6 all-gather.50
  922.8 28.1 reduce-scatter.41
  979.7 19.6 all-gather.28
  1007.3 28.1 reduce-scatter.43
  1037.9 28.2 reduce-scatter.25
  1070.1 137.1 all-reduce.10
  (10 shorter events, 196.0 us)
where the time goes:
time: 1230 us; the launch traced here: 1220 us
  waiting for transfers between devices  685 us (56%)
  matrix products  243 us (20%)
  other arithmetic  119 us (10%)
  blocking collectives  74.1 us (6%)
  local copies, waits for them, and re-layouts  67.5 us (5%)
  between operations  17.5 us (1%)
  starting transfers between devices  14.6 us (1%)
    reduce_scatter x9, waiting for transfers between devices, sum_branch(): lax.psum_scatter(term(jnp.int32(0), lax.axis_size('tensor') * row_count)....  220 us
    reduce_scatter x6, waiting for transfers between devices, sum_normed(): lax.psum_scatter(term(jnp.int32(0), lax.axis_size('tensor') * row_count)....  138 us
    all_gather x12, waiting for transfers between devices, gather_rows(): return lax.all_gather(normed, 'tensor', axis=0, tiled=True)  119 us
    all_gather x6, waiting for transfers between devices, fold_rows(): lax.all_gather(grad, 'tensor', axis=0, tiled=True)  107 us
    psum x1, waiting for transfers between devices, per_device(): lax.psum(qkv_total.astype(jnp.bfloat16), 'dp').astype(jnp.float32)  66.4 us
    psum x1, blocking collectives, per_device(): lax.psum((gain_one, out_bias_total, gain_two, down_bias_total), ('tensor'...  62.3 us
    unnamed x386, local copies, waits for them, and re-layouts  52.5 us
    ppermute x4, waiting for transfers between devices, from_behind(): return lax.ppermute(array, axis, pairs)  32.6 us
  transfers between devices with their start and end apart: 38, of which 34 were waited for; matrix products, arithmetic and copies ran while one was open for 15% of the time, Pallas kernels for 0%

commit v1 on v0

v1 whole, which is shorter than its diff:
```python
import jax
import jax.numpy as jnp
from jax import lax
from jax.experimental import pallas as pl
from jax.experimental.pallas import tpu as pltpu
from jax.sharding import PartitionSpec as P

HD = 64
EPS = 1e-05
SCALE = 0.125
NEGATIVE = -1e30
CHUNK = 128
MESH = pl.DeviceIdType.MESH
F32 = jnp.float32
BF16 = jnp.bfloat16
NN = (((1,), (0,)), ((), ()))
NT = (((1,), (1,)), ((), ()))
TN = (((0,), (0,)), ((), ()))
GELU_C = 0.7978845608028654
GELU_A = 0.044715


def dot(left, right, dims=NN):
    return lax.dot_general(left, right, dims, preferred_element_type=F32)


def lane_sum(value):
    return jnp.sum(value, axis=-1, keepdims=True)


def row_sum(value):
    return jnp.sum(value, axis=0, keepdims=True)


def expanded(block):
    value = block.astype(F32)
    lane = lax.broadcasted_iota(jnp.int32, value.shape, 1)
    return jnp.where(lane == value.shape[1] - 1, -lane_sum(value), value)


def norm_factor(full):
    return lax.rsqrt(lane_sum(full * full) * (1.0 / full.shape[1]) + EPS)


def centred(value):
    return value - lane_sum(value) * (1.0 / value.shape[1])


def norm_back(grad, full, gain):
    factor = norm_factor(full)
    weighted = grad * gain
    inner = lane_sum(weighted * full) * (1.0 / full.shape[1])
    gain_grad = row_sum(grad * full * factor)
    return centred(factor * weighted - full * (factor * factor * factor * inner)), gain_grad


def make_kernel(names, count):
    def kernel(*refs):
        r = dict(zip(names, refs, strict=True))
        xin, cot = r["xin"], r["cot"]
        vec, segc, segr = r["vec"], r["segc"], r["segr"]
        act, eg, grads, small = r["act"], r["eg"], r["grads"], r["small"]
        wq, wo, wu, wd, bc, ub = r["wq"], r["wo"], r["wu"], r["wd"], r["bc"], r["ub"]
        xbuf, cotb, hop, resb = r["xbuf"], r["cotb"], r["hop"], r["resb"]
        pool, nrm, n2t = r["pool"], r["nrm"], r["n2t"]
        qt, kt, vt, ctx, lse = r["qt"], r["kt"], r["vt"], r["ctx"], r["lse"]
        gp, hid, gpre, gmt, gat = r["gp"], r["hid"], r["gpre"], r["gmt"], r["gat"]
        dot_, dqkv, dk, dv = r["dot"], r["dqkv"], r["dk"], r["dv"]
        ex, xrec, cin, fin = r["ex"], r["xrec"], r["cin"], r["fin"]
        sown, soth, srec, scin, sfin = r["sown"], r["soth"], r["srec"], r["scin"], r["sfin"]
        sl, sg, se, sh, so, sr, sc, ss, credit = (
            r["sl"], r["sg"], r["se"], r["sh"], r["so"], r["sr"], r["sc"], r["ss"], r["credit"])
        blocks, rows, width = xbuf.shape
        length = blocks * rows
        slots, hs = wq.shape[0], wo.shape[1] // HD
        heads = slots * hs
        part = wo.shape[1]
        units = wu.shape[2]

        s = lax.axis_index("section")
        t = lax.axis_index("tensor")
        d = lax.axis_index("dp")
        core, xh = lax.rem(t, 2), lax.div(t, 2)
        t_core = 2 * xh + 1 - core
        t_x = 2 * (1 - xh) + core
        to_core = (s, t_core, d)
        to_x = (s, t_x, d)
        to_y = (1 - s, t, d)
        parity = lax.rem(d, 2)
        to_pair = (s, t, d + 1 - 2 * parity)
        left, right = (s, t, d - 1), (s, t, d + 1)

        def send(src, dst, sems, at, device):
            return pltpu.make_async_remote_copy(
                src_ref=src, dst_ref=dst, send_sem=sems.at[(0, *at)], recv_sem=sems.at[(1, *at)],
                device_id=device, device_id_type=MESH)

        def loop(stop, body):
            def step(i, carry):
                body(i)
                return carry

            lax.fori_loop(0, stop, step, 0)

        barrier = pltpu.get_barrier_semaphore()
        for device in (to_core, to_x, to_y):
            pl.semaphore_signal(barrier, inc=1, device_id=device, device_id_type=MESH)

        @pl.when(d > 0)
        def _():
            pl.semaphore_signal(barrier, inc=1, device_id=left, device_id_type=MESH)

        @pl.when(d < count - 1)
        def _():
            pl.semaphore_signal(barrier, inc=1, device_id=right, device_id_type=MESH)

        ends = jnp.where(d > 0, 1, 0) + jnp.where(d < count - 1, 1, 0)
        pl.semaphore_wait(barrier, 3 + ends)

        def rows_in(source, target, which):
            return (
                pltpu.make_async_copy(source.at[xh], target.at[t], sl.at[which]),
                send(source.at[1 - xh], target.at[t], sg, (which,), to_x),
                send(source.at[xh], target.at[t], sg, (which + 2,), to_core),
                send(target.at[t_x], target.at[t_x], sg, (which + 4,), to_core),
            )

        def rows_wait(copies):
            local, across, core_own, core_other = copies
            local.wait()
            across.wait_recv()
            core_other.start()
            core_own.wait()
            core_other.wait()
            across.wait_send()

        x_copies = rows_in(xin, xbuf, 0)
        cot_copies = rows_in(cot, cotb, 1)
        for copy in x_copies[:3]:
            copy.start()

        bias_copies = []
        for which, (source, target) in enumerate(((r["bch"], bc), (r["ubh"], ub))):
            bias_copies.append(pltpu.make_async_copy(source, target.at[0], sl.at[2 + which]))
            bias_copies.append(send(source, target.at[1], sg, (6 + which,), to_x))
        weights = []
        for which, (source, target) in enumerate(((r["wqh"], wq), (r["woh"], wo), (r["wuh"], wu), (r["wdh"], wd))):
            half = source.shape[0] // 2
            mine = pl.ds(pl.multiple_of(parity * half, 16), half)
            weights.append((
                pltpu.make_async_copy(source, target.at[0], sl.at[4 + which]),
                send(source.at[mine], target.at[1, mine], sg, (8 + which,), to_x),
                send(target.at[1, mine], target.at[1, mine], sg, (12 + which,), to_pair),
            ))
        for copy in bias_copies:
            copy.start()
        for local, across, _ in weights:
            local.start()
            across.start()
        for copy in cot_copies[:3]:
            copy.start()

        def pass_on(which):
            _, across, pair = weights[which]
            across.wait_recv()
            pair.start()

        def have(which):
            local, across, pair = weights[which]
            local.wait()
            across.wait_send()
            pair.wait()

        sown[...] = jnp.zeros_like(sown)
        soth[...] = jnp.zeros_like(soth)

        attn_gain, mlp_gain, out_bias, down_bias = (vec[i : i + 1, :] for i in range(4))

        def at_row(i):
            return pl.ds(pl.multiple_of(i * rows, rows), rows)

        def mid_at(i):
            return at_row(i)

        def grad_at(i):
            return pl.ds(pl.multiple_of(length + i * rows, rows), rows)

        def ex_at(kind, i):
            return pl.ds(pl.multiple_of(kind * length + i * rows, rows), rows)

        def pair_copy(kind, i):
            return send(ex.at[ex_at(2 * kind, i)], ex.at[ex_at(2 * kind + 1, i)], se, (kind, i), to_core)

        def pair_send(kind, i, value):
            ex[ex_at(2 * kind, i), :] = value.astype(BF16)
            pair_copy(kind, i).start()

        def pair_sum(kind, i):
            pair_copy(kind, i).wait()
            return ex[ex_at(2 * kind, i), :].astype(F32) + ex[ex_at(2 * kind + 1, i), :].astype(F32)

        half_rows = rows // 2
        own_half = pl.ds(pl.multiple_of(core * half_rows, half_rows), half_rows)

        def hop_copy(i):
            return send(resb.at[i, own_half], hop.at[i, own_half], sh, (0, i), to_y)

        def hop_core(i):
            return send(hop.at[i, own_half], hop.at[i, own_half], sh, (1, i), to_core)

        def hop_receive():
            def first(i):
                hop_copy(i).wait_recv()
                hop_core(i).start()

            def second(i):
                hop_copy(i).wait_send()
                hop_core(i).wait()

            loop(blocks, first)
            loop(blocks, second)

        def masked(scores, i, j0, j1, diagonal):
            same = segc[j0:j1, :]
            same = jnp.concatenate([same] * (rows // same.shape[1]), axis=1)
            allowed = same == segr[0:1, i * rows : (i + 1) * rows]
            if diagonal:
                key = lax.broadcasted_iota(jnp.int32, scores.shape, 0)
                query = lax.broadcasted_iota(jnp.int32, scores.shape, 1)
                allowed = allowed & (key <= query)
            return jnp.where(allowed, scores, NEGATIVE)

        def key_parts(i):
            parts = [(i * rows, (i + 1) * rows, True)]
            if i > 0:
                parts.append((0, i * rows, False))
            return parts

        def forward(p):
            @pl.when(p == 0)
            def _():
                rows_wait(x_copies)

            @pl.when(p == 1)
            def _():
                hop_receive()

                @pl.when(s == 1)
                def _():
                    xbuf[...] = hop[...]

                pl.semaphore_signal(credit, inc=1, device_id=to_y, device_id_type=MESH)

            def norm_rows(i):
                full = expanded(xbuf[i])
                nrm[i] = (full * norm_factor(full) * attn_gain).astype(BF16)

            loop(blocks, norm_rows)

            @pl.when(p == 0)
            def _():
                pass_on(0)
                for copy in bias_copies:
                    copy.wait()
                have(0)

            def project(i):
                normed = nrm[i]
                cols = at_row(i)
                for slot in range(slots):
                    three = dot(wq[slot], normed, NT)
                    bias = bc[slot].astype(F32)
                    bias = jnp.concatenate([bias] * (rows // bias.shape[1]), axis=1)
                    query = (three[:part] + bias[:part]).astype(BF16) * SCALE
                    key = three[part : 2 * part].astype(BF16)
                    value = (three[2 * part :] + bias[part:]).astype(BF16)
                    for h in range(hs):
                        at = slice(h * HD, (h + 1) * HD)
                        qt[i, slot * hs + h] = query[at].astype(BF16)
                        kt[slot * hs + h, :, cols] = key[at]
                        vt[slot * hs + h, :, cols] = value[at]

            loop(blocks, project)

            @pl.when(p == 0)
            def _():
                pass_on(1)
                pass_on(2)

            def attend(h):
                key = kt[h].astype(F32).T.astype(BF16)
                for i in range(blocks):
                    cols = slice(i * rows, (i + 1) * rows)
                    parts = key_parts(i)
                    query = qt[i, h]
                    scores = [masked(dot(key[a:b], query), i, a, b, g) for a, b, g in parts]
                    highest = scores[0].max(axis=0, keepdims=True)
                    for score in scores[1:]:
                        highest = jnp.maximum(highest, score.max(axis=0, keepdims=True))
                    total, context = 0.0, 0.0
                    for score, (a, b, _) in zip(scores, parts, strict=True):
                        power = jnp.exp(score - highest)
                        total = total + row_sum(power)
                        context = context + dot(vt[h, :, a:b], power.astype(BF16))
                    ctx[h, :, cols] = (context / total).astype(BF16)
                    lse[i, h] = highest + jnp.log(total)

            loop(heads, attend)

            @pl.when(p == 0)
            def _():
                pass_on(3)
                have(1)

            def out_rows(i):
                context = ctx[:, :, at_row(i)].reshape(heads * HD, rows)
                pair_send(0, i, dot(context, wo[...].reshape(heads * HD, width), TN))

            loop(blocks, out_rows)

            @pl.when(p == 0)
            def _():
                have(2)

            def up_rows(i):
                branch = pair_sum(0, i) + out_bias
                middle = expanded(xbuf[i]) + centred(branch)
                pool[mid_at(i), :] = middle
                normed = middle * norm_factor(middle) * mlp_gain
                n2t[:, at_row(i)] = normed.T.astype(BF16)
                normed = normed.astype(BF16)
                for slot in range(slots):
                    pre = dot(normed, wu[slot]) + ub[slot, 0:1, :].astype(F32)
                    square = pre * pre
                    bend = jnp.tanh(GELU_C * pre * (1.0 + GELU_A * square))
                    grow = 0.5 * (1.0 + bend)
                    hid[slot, i] = (pre * grow).astype(BF16)
                    slope = GELU_C * (1.0 + 3.0 * GELU_A * square)
                    gp[slot, i] = (grow + 0.5 * pre * (1.0 - bend * bend) * slope).astype(BF16)

            loop(blocks, up_rows)

            @pl.when(p == 0)
            def _():
                have(3)

            def down_rows(i):
                branch = dot(hid[0, i], wd[0], NT)
                for slot in range(1, slots):
                    branch = branch + dot(hid[slot, i], wd[slot], NT)
                pair_send(1, i, branch)

            loop(blocks, down_rows)

            def result_rows(i):
                result = pool[mid_at(i), :] + centred(pair_sum(1, i) + down_bias)
                lane = lax.broadcasted_iota(jnp.int32, result.shape, 1)
                resb[i] = jnp.where(lane == width - 1, 0.0, result).astype(BF16)

                @pl.when(p == 0)
                def _():
                    hop_copy(i).start()

            loop(blocks, result_rows)

        def rows_out(target, which):
            return (
                pltpu.make_async_copy(resb.at[t], target.at[xh], sl.at[8 + which]),
                send(resb.at[t_x], target.at[xh], so, (which,), to_x),
            )

        loop(2, forward)
        act_copies = rows_out(act, 0)
        for copy in act_copies:
            copy.start()
        rows_wait(cot_copies)

        def backward(p):
            @pl.when(p == 0)
            def _():
                pl.semaphore_wait(credit, 1)

            @pl.when(p == 1)
            def _():
                hop_receive()

                @pl.when(s == 0)
                def _():
                    cotb[...] = hop[...]

            sown[...] = jnp.zeros_like(sown)
            soth[...] = jnp.zeros_like(soth)

            def down_back(i):
                grad = centred(cotb[i].astype(F32))
                pool[grad_at(i), :] = grad
                gmt[:, at_row(i)] = grad.T.astype(BF16)
                grad = grad.astype(BF16)
                sown[3:4, :] += row_sum(grad.astype(F32))
                branch = 0.0
                for slot, sums in ((0, sown), (1, soth)):
                    before = (dot(grad, wd[slot]) * gp[slot, i].astype(F32)).astype(BF16)
                    gpre[slot, i] = before
                    sums[4:5, :] += row_sum(before.astype(F32))
                    branch = branch + dot(before, wu[slot], NT)
                pair_send(0, i, branch)

            loop(blocks, down_back)

            def out_back(i):
                grad, gain_grad = norm_back(pair_sum(0, i), pool[mid_at(i), :], mlp_gain)
                sown[2:3, :] += gain_grad
                grad = grad + pool[grad_at(i), :]
                pool[grad_at(i), :] = grad
                grad = grad.astype(BF16)
                gat[i] = grad
                sown[1:2, :] += row_sum(grad.astype(F32))
                back = dot(wo[...].reshape(heads * HD, width), grad, NT).astype(BF16)
                for h in range(heads):
                    dot_[i, h] = back[h * HD : (h + 1) * HD]

            loop(blocks, out_back)

            def attend_back(h):
                key_t = kt[h]
                key = key_t.astype(F32).T.astype(BF16)
                value = vt[h].astype(F32).T.astype(BF16)
                slot, place = lax.div(h, hs), lax.rem(h, hs)
                for i in reversed(range(blocks)):
                    query, back = qt[i, h], dot_[i, h]
                    parts = key_parts(i)
                    probs, g_probs = [], []
                    centre = 0.0
                    for a, b, g in parts:
                        prob = jnp.exp(masked(dot(key[a:b], query), i, a, b, g) - lse[i, h])
                        g_prob = dot(value[a:b], back)
                        centre = centre + row_sum(prob * g_prob)
                        probs.append(prob)
                        g_probs.append(g_prob)
                    g_query = 0.0
                    for prob, g_prob, (a, b, _) in zip(probs, g_probs, parts, strict=True):
                        g_score = (prob * (g_prob - centre)).astype(BF16)
                        g_value = dot(back, prob.astype(BF16), NT)
                        g_key = dot(query, g_score, NT)
                        g_query = g_query + dot(key_t[:, a:b], g_score)
                        if i == blocks - 1:
                            dv[:, a:b] = g_value
                            dk[:, a:b] = g_key
                        else:
                            dv[:, a:b] += g_value
                            dk[:, a:b] += g_key
                    dqkv[slot, 0, place, :, i * rows : (i + 1) * rows] = (g_query * SCALE).astype(BF16)
                dqkv[slot, 1, place] = dk[...].astype(BF16)
                dqkv[slot, 2, place] = dv[...].astype(BF16)

            loop(heads, attend_back)

            def qkv_back(i):
                branch = 0.0
                for slot in range(slots):
                    three = dqkv[slot, :, :, :, at_row(i)].reshape(3 * part, rows)
                    branch = branch + dot(three, wq[slot], TN)
                pair_send(1, i, branch)

            loop(blocks, qkv_back)

            @pl.when(p == 0)
            def _():
                for copy in act_copies:
                    copy.wait()

            def in_back(i):
                grad, gain_grad = norm_back(pair_sum(1, i), expanded(xbuf[i]), attn_gain)
                sown[0:1, :] += gain_grad
                grad = grad + pool[grad_at(i), :]
                resb[i] = (grad - grad[:, width - 1 :]).astype(BF16)

                @pl.when(p == 0)
                def _():
                    hop_copy(i).start()

            loop(blocks, in_back)

        loop(2, backward)
        eg_copies = rows_out(eg, 1)
        for copy in eg_copies:
            copy.start()

        chunks = grads.shape[0]

        def x_copy(k):
            return send(ex.at[pl.ds(pl.multiple_of(k * CHUNK, CHUNK), CHUNK)], xrec.at[k], sr, (k,), to_x)

        ones = jnp.ones((8, length), BF16)
        sown[5:6, : 3 * part] = dot(ones, dqkv[0].reshape(3 * part, length), NT)[0:1]
        soth[5:6, : 3 * part] = dot(ones, dqkv[1].reshape(3 * part, length), NT)[0:1]
        soth[0:4, :] = sown[0:4, :]
        small_x = send(soth, srec, ss, (0,), to_x)
        small_x.start()

        def weight_grads(turn):
            slot = 1 - turn

            def put(at, value):
                @pl.when(turn == 0)
                def _():
                    ex[at, :] = value.astype(BF16)

                @pl.when(turn == 1)
                def _():
                    pool[at, :] = value

            def start(first, number):
                @pl.when(turn == 0)
                def _():
                    loop(number, lambda k: x_copy(first + k).start())

            tile = 256
            tiles = width // tile

            def down_part(k):
                at = pl.ds(pl.multiple_of(k * tile, tile), tile)
                put(at, dot(gmt[at, :], hid[slot].reshape(length, units)))

            loop(tiles, down_part)
            start(0, width // CHUNK)

            def up_part(k):
                at = pl.ds(pl.multiple_of(k * tile, tile), tile)
                here = pl.ds(pl.multiple_of(width + k * tile, tile), tile)
                put(here, dot(n2t[at, :], gpre[slot].reshape(length, units)))

            loop(tiles, up_part)
            start(width // CHUNK, width // CHUNK)

            def qkv_part(k):
                here = pl.ds(pl.multiple_of(2 * width + k * part, 64), part)
                put(here, dot(dqkv[slot, k].reshape(part, length), nrm[...].reshape(length, width)))

            loop(3, qkv_part)
            here = pl.ds(2 * width + 3 * part, part)
            context = ctx[pl.ds(slot * hs, hs)].reshape(part, length)
            put(here, dot(context, gat[...].reshape(length, width)))
            start(2 * (width // CHUNK), chunks - 2 * (width // CHUNK))

        loop(2, weight_grads)

        middle = count // 2
        on_left = d < middle
        depth = jnp.where(on_left, d, count - 1 - d)
        has_outer = depth > 0
        is_mid = depth == middle - 1
        side = jnp.where(on_left, 0, 1)
        inner = (s, t, jnp.where(on_left, d + 1, d - 1))
        outer = (s, t, jnp.where(on_left, d - 1, d + 1))
        lag = 2
        lag_in = lag * depth
        lag_mid = lag * middle
        lag_out = lag_mid + lag * (middle - depth)
        lag_all = lag_mid + lag * middle

        def in_copy(k):
            return send(xrec.at[k], cin.at[k], sc, (0, k), inner)

        def cross_copy(k):
            return send(xrec.at[k], fin.at[k], sc, (1, k), inner)

        def back_copy(k):
            return send(fin.at[k], fin.at[k], sc, (2, k), inner)

        def out_copy(k):
            return send(fin.at[k], fin.at[k], sc, (3, k), outer)

        def grads_copy(k):
            return pltpu.make_async_copy(fin.at[k], grads.at[k], so.at[0, 2 + k])

        def reduce(it):
            @pl.when(it < chunks)
            def _():
                k = it
                x_copy(k).wait()
                here = pl.ds(pl.multiple_of(k * CHUNK, CHUNK), CHUNK)
                xrec[k] = (pool[here, :] + xrec[k].astype(F32)).astype(BF16)

            k_in = it - lag_in

            @pl.when((k_in >= 0) & (k_in < chunks))
            def _():
                k = k_in
                owner = lax.rem(k, 2) == side

                @pl.when(has_outer)
                def _():
                    in_copy(k).wait_recv()
                    xrec[k] = (xrec[k].astype(F32) + cin[k].astype(F32)).astype(BF16)

                @pl.when(jnp.logical_not(is_mid))
                def _():
                    in_copy(k).start()

                @pl.when(is_mid & jnp.logical_not(owner))
                def _():
                    cross_copy(k).start()

            k_mid = it - lag_mid

            @pl.when((k_mid >= 0) & (k_mid < chunks) & is_mid)
            def _():
                k = k_mid

                @pl.when(lax.rem(k, 2) == side)
                def _():
                    cross_copy(k).wait_recv()
                    fin[k] = (xrec[k].astype(F32) + fin[k].astype(F32)).astype(BF16)
                    back_copy(k).start()

                    @pl.when(has_outer)
                    def _():
                        out_copy(k).start()

                    grads_copy(k).start()

            k_out = it - lag_out

            @pl.when((k_out >= 0) & (k_out < chunks))
            def _():
                k = k_out
                owner = lax.rem(k, 2) == side

                @pl.when(is_mid & jnp.logical_not(owner))
                def _():
                    back_copy(k).wait_recv()

                @pl.when(jnp.logical_not(is_mid))
                def _():
                    out_copy(k).wait_recv()

                @pl.when(jnp.logical_not(is_mid & owner))
                def _():
                    @pl.when(has_outer)
                    def _():
                        out_copy(k).start()

                    grads_copy(k).start()

        loop(chunks + lag_all, reduce)

        small_x.wait()
        sown[...] = sown[...] + srec[...]
        s_in = send(sown, scin, ss, (1,), inner)
        s_cross = send(sown, sfin, ss, (2,), inner)
        s_back = send(sfin, sfin, ss, (3,), inner)
        s_out = send(sfin, sfin, ss, (4,), outer)
        owner = side == 0

        @pl.when(has_outer)
        def _():
            s_in.wait_recv()
            sown[...] = sown[...] + scin[...]

        @pl.when(jnp.logical_not(is_mid))
        def _():
            s_in.start()
            s_in.wait_send()
            s_out.wait_recv()

        @pl.when(is_mid & jnp.logical_not(owner))
        def _():
            s_cross.start()
            s_cross.wait_send()
            s_back.wait_recv()

        @pl.when(is_mid & owner)
        def _():
            s_cross.wait_recv()
            sfin[...] = sfin[...] + sown[...]
            s_back.start()
            s_back.wait_send()

        @pl.when(has_outer)
        def _():
            s_out.start()
            s_out.wait_send()

        small[...] = sfin[...]

        def drain(k):
            owner = lax.rem(k, 2) == side

            @pl.when(jnp.logical_not(is_mid))
            def _():
                in_copy(k).wait_send()

            @pl.when(is_mid & jnp.logical_not(owner))
            def _():
                cross_copy(k).wait_send()

            @pl.when(is_mid & owner)
            def _():
                back_copy(k).wait_send()

            @pl.when(has_outer)
            def _():
                out_copy(k).wait_send()

            grads_copy(k).wait()

        loop(chunks, drain)
        for copy in eg_copies:
            copy.wait()

    return kernel


def per_device(
    block_input,
    segments,
    cotangent,
    attn_gain,
    qkv_weight,
    qv_bias,
    out_weight,
    out_bias,
    mlp_gain,
    up_projection_weight,
    up_bias,
    down_projection_weight,
    down_bias,
):
    micros, rows, _, kept = block_input.shape
    width = qkv_weight.shape[1]
    part = qkv_weight.shape[3]
    units = up_projection_weight.shape[2]
    blocks = lax.axis_size("tensor")
    count = lax.axis_size("dp")
    length = blocks * rows
    slots = 2
    hs = part // HD
    heads = slots * hs
    chunks = (2 * width + 4 * part) // CHUNK

    def padded(array):
        return jnp.pad(array[:, :, 0, :], ((0, 0), (0, 0), (0, width - kept)))

    micro = lax.axis_index("tensor") // 2
    segment = lax.dynamic_index_in_dim(segments[:, 0, :], micro, 0, keepdims=False)
    vec = jnp.concatenate([attn_gain, mlp_gain, out_bias, down_bias] * 2).astype(F32)
    inputs = {
        "xin": padded(block_input),
        "cot": padded(cotangent),
        "wqh": qkv_weight[0].transpose(1, 2, 0).reshape(3 * part, width),
        "woh": out_weight[0],
        "wuh": up_projection_weight[0],
        "wdh": down_projection_weight[0],
        "bch": jnp.broadcast_to(qv_bias[0].reshape(2 * part, 1), (2 * part, 128)),
        "ubh": jnp.broadcast_to(up_bias, (16, units)),
        "vec": vec,
        "segc": jnp.broadcast_to(segment[:, None], (length, 128)),
        "segr": jnp.broadcast_to(segment[None, :], (8, length)),
    }
    outputs = {
        "act": ((micros, rows, width), BF16),
        "eg": ((micros, rows, width), BF16),
        "grads": ((chunks, CHUNK, width), BF16),
        "small": ((8, width), F32),
    }
    scratch = {
        "wq": ((slots, 3 * part, width), BF16),
        "wo": ((slots, part, width), BF16),
        "wu": ((slots, width, units), BF16),
        "wd": ((slots, width, units), BF16),
        "bc": ((slots, 2 * part, 128), BF16),
        "ub": ((slots, 16, units), BF16),
        "xbuf": ((blocks, rows, width), BF16),
        "cotb": ((blocks, rows, width), BF16),
        "hop": ((blocks, rows, width), BF16),
        "resb": ((blocks, rows, width), BF16),
        "pool": ((max(2 * length, chunks * CHUNK), width), F32),
        "nrm": ((blocks, rows, width), BF16),
        "n2t": ((width, length), BF16),
        "qt": ((blocks, heads, HD, rows), BF16),
        "kt": ((heads, HD, length), BF16),
        "vt": ((heads, HD, length), BF16),
        "ctx": ((heads, HD, length), BF16),
        "lse": ((blocks, heads, 1, rows), F32),
        "gp": ((slots, blocks, rows, units), BF16),
        "hid": ((slots, blocks, rows, units), BF16),
        "gpre": ((slots, blocks, rows, units), BF16),
        "gmt": ((width, length), BF16),
        "gat": ((blocks, rows, width), BF16),
        "dot": ((blocks, heads, HD, rows), BF16),
        "dqkv": ((slots, 3, hs, HD, length), BF16),
        "dk": ((HD, length), F32),
        "dv": ((HD, length), F32),
        "ex": ((4 * length, width), BF16),
        "xrec": ((chunks, CHUNK, width), BF16),
        "cin": ((chunks, CHUNK, width), BF16),
        "fin": ((chunks, CHUNK, width), BF16),
        "sown": ((8, width), F32),
        "soth": ((8, width), F32),
        "srec": ((8, width), F32),
        "scin": ((8, width), F32),
        "sfin": ((8, width), F32),
    }
    dma = pltpu.SemaphoreType.DMA
    semaphores = {
        "sl": dma((10,)),
        "sg": dma((2, 16)),
        "se": dma((2, 2, blocks)),
        "sh": dma((2, 2, blocks)),
        "so": dma((2, 2 + chunks)),
        "sr": dma((2, chunks)),
        "sc": dma((2, 4, chunks)),
        "ss": dma((2, 5)),
        "credit": pltpu.SemaphoreType.REGULAR,
    }
    in_vmem = {"vec", "segc", "segr", "small"}

    def spec(name):
        return pl.BlockSpec(memory_space=pltpu.VMEM if name in in_vmem else pl.ANY)

    names = [*inputs, *outputs, *scratch, *semaphores]
    act, eg, grads, small = pl.pallas_call(
        make_kernel(names, count),
        out_shape=[jax.ShapeDtypeStruct(*item) for item in outputs.values()],
        in_specs=[spec(name) for name in inputs],
        out_specs=[spec(name) for name in outputs],
        scratch_shapes=[pltpu.VMEM(*item) for item in scratch.values()] + list(semaphores.values()),
        compiler_params=pltpu.CompilerParams(
            collective_id=0, has_side_effects=True, vmem_limit_bytes=63 * 1024 * 1024
        ),
        name="layers",
    )(*inputs.values())

    grads = grads.reshape(chunks * CHUNK, width).astype(F32)
    down, up, qkv, out = jnp.split(grads, [width, 2 * width, 2 * width + 3 * part])
    qv = small[5, : 3 * part].reshape(3, part)
    return (
        act[None, :, :, None, :kept],
        eg[None, :, :, None, :kept].astype(F32),
        small[0:1],
        qkv.reshape(3, part, width).transpose(2, 0, 1)[None],
        qv[0::2][None],
        out[None],
        small[1:2],
        small[2:3],
        up[None],
        small[4:5, :units],
        down[None],
        small[3:4],
    )


def solution(mesh):
    in_specs = (
        P(None, "tensor", "dp", None),
        P(None, "dp", None),
        P(None, "tensor", "dp", None),
        P("section", None),
        P("section", None, None, "tensor"),
        P("section", None, "tensor"),
        P("section", "tensor", None),
        P("section", None),
        P("section", None),
        P("section", None, "tensor"),
        P("section", "tensor"),
        P("section", None, "tensor"),
        P("section", None),
    )
    out_specs = (
        P("section", None, "tensor", "dp", None),
        P("section", None, "tensor", "dp", None),
        P("section", None),
        P("section", None, None, "tensor"),
        P("section", None, "tensor"),
        P("section", "tensor", None),
        P("section", None),
        P("section", None),
        P("section", None, "tensor"),
        P("section", "tensor"),
        P("section", None, "tensor"),
        P("section", None),
    )
    return jax.shard_map(
        per_device, mesh=mesh, in_specs=in_specs, out_specs=out_specs, check_vma=False
    )
```

time: 1230 us -> 359 us (0.29)
  waiting for transfers between devices: 685 us -> 0 us
  Pallas kernels: 0 us -> 334 us
  matrix products: 243 us -> 0 us
  other arithmetic: 119 us -> 3.6 us
  blocking collectives: 74.1 us -> 0 us
  local copies, waits for them, and re-layouts: 67.5 us -> 20.5 us
  between operations: 17.5 us -> 0.8 us
  starting transfers between devices: 14.6 us -> 0 us
    reduce_scatter x15 -> x0, waiting for transfers between devices: 358 us -> none  [the longest x9 220 us: sum_branch(): lax.psum_scatter(term(jnp.int32(0), lax.axis_size('tensor') * row_count)....]
    pallas_call x0 -> x1, Pallas kernels: none -> 334 us  [per_device(): pl.pallas_call(make_kernel(names, count), out_shape=[jax.ShapeDtypeStruct...]
    all_gather x18 -> x0, waiting for transfers between devices: 225 us -> none  [the longest x12 119 us: gather_rows(): return lax.all_gather(normed, 'tensor', axis=0, tiled=True)]
    dot_general x54 -> x0, matrix products: 189 us -> none  [the longest x6 25.1 us: run_layer(): jnp.einsum('shqk,kshd->qshd', probs.astype(jnp.bfloat16), values.reshape(...]
    psum x2 -> x0, blocking collectives: 74.1 us -> none  [the longest x1 62.3 us: per_device(): lax.psum((gain_one, out_bias_total, gain_two, down_bias_total), ('tensor'...]
    psum x1 -> x0, waiting for transfers between devices: 66.4 us -> none  [per_device(): lax.psum(qkv_total.astype(jnp.bfloat16), 'dp').astype(jnp.float32)]
    reduce_sum x49 -> x0, other arithmetic: 49.5 us -> none  [the longest x6 9.74 us: crms(): return full * factor * gain]
    unnamed x386 -> x28, local copies, waits for them, and re-layouts: 52.5 us -> 9.33 us
  transfers between devices with their start and end apart: 38 -> 0, of which waited for: 34 -> 0; matrix products, arithmetic and copies ran while one was open for 15% -> 0% of each run, Pallas kernels for 0% -> 0%
where the time goes in v1:
time: 359 us
  Pallas kernels  334 us (93%)
  local copies, waits for them, and re-layouts  20.5 us (6%)
  other arithmetic  3.6 us (1%)
    pallas_call x1, Pallas kernels, per_device(): pl.pallas_call(make_kernel(names, count), out_shape=[jax.ShapeDtypeStruct...  334 us
    unnamed x28, local copies, waits for them, and re-layouts  9.33 us

profile of v1, /device:TPU:0, one launch (start us, length us, event | category | flops | bytes accessed | tf_op | source)
XLA Modules:
  0.0 358.5 jit_solution(9424622315871656803)
XLA Ops:
  0.7 0.7 copy-done
  1.3 1.0 broadcast_in_dim.52.refs_9_
  2.3 0.6 broadcast_in_dim.53.refs_10_
  3.0 2.2 copy.25
  5.3 1.0 pad.7.refs_0_
  6.2 1.2 copy.26
  7.4 1.0 pad.8.refs_1_
  8.4 0.1 broadcast_in_dim.47
  8.4 0.8 broadcast_in_dim.48.refs_6_
  9.2 0.1 concatenate.3
  9.3 0.6 convert_element_type.18.refs_8_
  9.9 0.6 broadcast_in_dim.50.refs_7_
  10.5 333.6 %layers.1 = (bf16[2,256,768]{2,1,0:T(8,128)(2,1)}, bf16[2,256,768]{2,1,0:T(8,128)(2,1)}, bf16[18,128,768]{2,1,0:T(8,128)(2,1)}, f32[8,768]{1,0:T(8,128)}) custom-call(bf16[2,256,768]{2,1,0:T(8,128)(2,1)} %pad.7.refs_0_, bf16[2,256,768]{2,1,0:T(8,128)(2,1)} %pad.8.refs_1_, bf16[576,768]{1,0:T(8,128)(2,1)} %bitcast.36, bf16[192,768]{1,0:T(8,128)(2,1)} %bitcast.37, ...), custom_call_target="tpu_custom_call" | custom-call | tf_op jit(solution)/shard_map/layers/pallas_call | solution.py:823
  344.2 2.8 convert_element_type.21
  347.0 1.3 split.16
  348.3 0.9 slice_bitcast_fusion.1
  349.2 0.7 copy-done.1
  349.8 2.6 fusion
  352.5 0.2 bitcast_convert_fusion
  352.7 2.8 copy.28
  355.4 1.8 copy.27
  357.2 0.6 fusion.1
  357.8 0.1 reshape_squeeze.4
  357.9 0.6 slice.33
  (25 shorter events, 0.1 us)
Async XLA Ops:
  0.6 0.7 copy-start
  0.7 5.6 %copy-start.4 = (bf16[2,256,1,767]{1,0,3,2:T(2,128)(2,1)S(1)}, bf16[2,256,1,767]{1,0,3,2:T(2,128)(2,1)}, u32[]{:S(2)}) copy-start(bf16[2,256,1,767]{1,0,3,2:T(2,128)(2,1)} %param.15) | copy-start | bytes 2356228
  5.2 3.2 copy-start.11
  5.2 4.0 %copy-start.6 = (bf16[1,768]{1,0:T(2,128)(2,1)S(1)}, bf16[1,768]{1,0:T(2,128)(2,1)}, u32[]{:S(2)}) copy-start(bf16[1,768]{1,0:T(2,128)(2,1)} %param.16) | copy-start | bytes 4612
  5.2 4.0 %copy-start.7 = (bf16[1,768]{1,0:T(2,128)(2,1)S(1)}, bf16[1,768]{1,0:T(2,128)(2,1)}, u32[]{:S(2)}) copy-start(bf16[1,768]{1,0:T(2,128)(2,1)} %param.21) | copy-start | bytes 4612
  5.2 4.0 %copy-start.8 = (bf16[1,768]{1,0:T(2,128)(2,1)S(1)}, bf16[1,768]{1,0:T(2,128)(2,1)}, u32[]{:S(2)}) copy-start(bf16[1,768]{1,0:T(2,128)(2,1)} %param.20) | copy-start | bytes 4612
  5.3 4.0 %copy-start.9 = (bf16[1,768]{1,0:T(2,128)(2,1)S(1)}, bf16[1,768]{1,0:T(2,128)(2,1)}, u32[]{:S(2)}) copy-start(bf16[1,768]{1,0:T(2,128)(2,1)} %param.25) | copy-start | bytes 4612
  5.3 4.6 %copy-start.10 = (bf16[1,768]{1,0:T(2,128)(2,1)S(1)}, bf16[1,768]{1,0:T(2,128)(2,1)}, u32[]{:S(2)}) copy-start(bf16[1,768]{1,0:T(2,128)(2,1)} %param.23) | copy-start | bytes 4612
  347.0 2.9 copy-start.1
  349.8 2.7 copy-start.2
  349.8 2.7 copy-start.3
  352.7 4.5 %copy-start.5 = (f32[8,768]{1,0:T(8,128)S(1)}, f32[8,768]{1,0:T(8,128)}, u32[]{:S(2)}) copy-start(f32[8,768]{1,0:T(8,128)} %get-tuple-element.18) | copy-start | bytes 73732

commit v2 on v1

v2 whole, which is shorter than its diff:
```python
import jax
import jax.numpy as jnp
from jax import lax
from jax.experimental import pallas as pl
from jax.experimental.pallas import tpu as pltpu
from jax.sharding import PartitionSpec as P

HD = 64
EPS = 1e-05
SCALE = 0.125
NEGATIVE = -1e30
CHUNK = 64
MESH = pl.DeviceIdType.MESH
F32 = jnp.float32
BF16 = jnp.bfloat16
NN = (((1,), (0,)), ((), ()))
NT = (((1,), (1,)), ((), ()))
TN = (((0,), (0,)), ((), ()))
GELU_C = 0.7978845608028654
GELU_A = 0.044715


def dot(left, right, dims=NN):
    return lax.dot_general(left, right, dims, preferred_element_type=F32)


def lane_sum(value):
    return jnp.sum(value, axis=-1, keepdims=True)


def row_sum(value):
    return jnp.sum(value, axis=0, keepdims=True)


def expanded(block):
    value = block.astype(F32)
    lane = lax.broadcasted_iota(jnp.int32, value.shape, 1)
    return jnp.where(lane == value.shape[1] - 1, -lane_sum(value), value)


def norm_factor(full):
    return lax.rsqrt(lane_sum(full * full) * (1.0 / full.shape[1]) + EPS)


def centred(value):
    return value - lane_sum(value) * (1.0 / value.shape[1])


def norm_back(grad, full, gain):
    factor = norm_factor(full)
    weighted = grad * gain
    inner = lane_sum(weighted * full) * (1.0 / full.shape[1])
    gain_grad = row_sum(grad * full * factor)
    return centred(factor * weighted - full * (factor * factor * factor * inner)), gain_grad


def make_kernel(names, count):
    def kernel(*refs):
        r = dict(zip(names, refs, strict=True))
        xin, cot, misc, seg = r["xin"], r["cot"], r["misc"], r["seg"]
        act, eg, small = r["act"], r["eg"], r["small"]
        wq, wo, wu, wd, mc = r["wq"], r["wo"], r["wu"], r["wd"], r["mc"]
        xbuf, cotb, resb, outt = r["xbuf"], r["cotb"], r["resb"], r["outt"]
        pool, nrm, n2t = r["pool"], r["nrm"], r["n2t"]
        qt, kt, vt, kn, vn = r["qt"], r["kt"], r["vt"], r["kn"], r["vn"]
        ctx, lse, segc = r["ctx"], r["lse"], r["segc"]
        gp, hid, gmt, gat = r["gp"], r["hid"], r["gmt"], r["gat"]
        dot_, dqkv, dk, dv = r["dot"], r["dqkv"], r["dk"], r["dv"]
        ex, xrec, cin, fin = r["ex"], r["xrec"], r["cin"], r["fin"]
        sown, soth, srec, scin, sfin = r["sown"], r["soth"], r["srec"], r["scin"], r["sfin"]
        sl, sg, sw, se, sh, so, sr, sc, ss = (
            r[name] for name in ("sl", "sg", "sw", "se", "sh", "so", "sr", "sc", "ss"))
        blocks, rows, width = xbuf.shape
        length = blocks * rows
        slots, hs = wq.shape[0], wo.shape[1] // HD
        heads = slots * hs
        part = wo.shape[1]
        units = wu.shape[2]
        chunks = xrec.shape[0]

        s = lax.axis_index("section")
        t = lax.axis_index("tensor")
        d = lax.axis_index("dp")
        core, xh = lax.rem(t, 2), lax.div(t, 2)
        t_core = 2 * xh + 1 - core
        t_x = 2 * (1 - xh) + core
        to_core = (s, t_core, d)
        to_x = (s, t_x, d)
        to_y = (1 - s, t, d)
        to_xy = (1 - s, t_x, d)
        parity = lax.rem(d, 2)
        to_pair = (s, t, d + 1 - 2 * parity)
        left, right = (s, t, d - 1), (s, t, d + 1)
        first_section, last_section = s == 0, s == 1

        def send(src, dst, sems, at, device):
            return pltpu.make_async_remote_copy(
                src_ref=src, dst_ref=dst, send_sem=sems.at[(0, *at)], recv_sem=sems.at[(1, *at)],
                device_id=device, device_id_type=MESH)

        def loop(stop, body):
            def step(i, carry):
                body(i)
                return carry

            lax.fori_loop(0, stop, step, 0)

        barrier = pltpu.get_barrier_semaphore()
        for device in (to_core, to_x, to_y, to_xy):
            pl.semaphore_signal(barrier, inc=1, device_id=device, device_id_type=MESH)

        @pl.when(d > 0)
        def _():
            pl.semaphore_signal(barrier, inc=1, device_id=left, device_id_type=MESH)

        @pl.when(d < count - 1)
        def _():
            pl.semaphore_signal(barrier, inc=1, device_id=right, device_id_type=MESH)

        ends = jnp.where(d > 0, 1, 0) + jnp.where(d < count - 1, 1, 0)
        pl.semaphore_wait(barrier, 4 + ends)

        def at_row(i):
            return pl.ds(pl.multiple_of(i * rows, rows), rows)

        mid_at = at_row

        def grad_at(i):
            return pl.ds(pl.multiple_of(length + i * rows, rows), rows)

        def rows_in(source, device):
            mine, other = gmt.at[:, at_row(t)], gmt.at[:, at_row(t_x)]
            return (
                pltpu.make_async_copy(source.at[xh], mine, sl.at[0]),
                send(source.at[xh], mine, sg, (1,), to_core),
                send(source.at[1 - xh], mine, sg, (0,), device),
                send(other, other, sg, (2,), to_core),
            )

        def rows_wait(copies, target):
            local, core_own, across, core_other = copies
            across.wait_recv()
            core_other.start()
            local.wait()
            core_own.wait()
            core_other.wait()

            def turn(i):
                target[i] = gmt[:, at_row(i)].astype(F32).T.astype(BF16)

            loop(blocks, turn)

        @pl.when(first_section)
        def _():
            for copy in rows_in(xin, to_xy)[:2]:
                copy.start()

        @pl.when(last_section)
        def _():
            rows_in(xin, to_xy)[2].start()

        misc_local = pltpu.make_async_copy(misc, mc.at[0], sl.at[1])
        misc_x = send(misc, mc.at[1], sg, (3,), to_x)
        misc_local.start()
        misc_x.start()
        locals_, pieces = [], []
        for which, (name, target, cuts) in enumerate((("wqh", wq, 2), ("woh", wo, 1), ("wuh", wu, 2), ("wdh", wd, 3))):
            source = r[name]
            locals_.append(pltpu.make_async_copy(source, target.at[0], sl.at[4 + which]))
            half = source.shape[0] // 2
            step = half // cuts
            group = []
            for cut in range(cuts):
                at = pl.ds(pl.multiple_of(parity * half + cut * step, 16), step)
                place = 3 * which + cut
                group.append((
                    send(source.at[at], target.at[1, at], sw, (0, place), to_x),
                    send(target.at[1, at], target.at[1, at], sw, (1, place), to_pair),
                ))
            pieces.append(group)
        for local, group in zip(locals_, pieces, strict=True):
            local.start()
            for across, _ in group:
                across.start()

        @pl.when(last_section)
        def _():
            for copy in rows_in(cot, to_x)[:3]:
                copy.start()

        def pass_on(which, *cuts):
            for cut in cuts:
                across, pair = pieces[which][cut]
                across.wait_recv()
                pair.start()

        def have(which):
            locals_[which].wait()
            for across, pair in pieces[which]:
                across.wait_send()
                pair.wait()

        sown[...] = jnp.zeros_like(sown)
        soth[...] = jnp.zeros_like(soth)
        segment = seg[pl.ds(xh, 1), :]
        segc[...] = jnp.broadcast_to(segment.astype(F32), (128, length)).T

        def ex_at(kind, i):
            return pl.ds(pl.multiple_of(kind * length + i * rows, rows), rows)

        def pair_copy(kind, i):
            return send(ex.at[ex_at(2 * kind, i)], ex.at[ex_at(2 * kind + 1, i)], se, (kind, i), to_core)

        def pair_send(kind, i, value):
            ex[ex_at(2 * kind, i), :] = value.astype(BF16)
            pair_copy(kind, i).start()

        def pair_sum(kind, i):
            pair_copy(kind, i).wait()
            return ex[ex_at(2 * kind, i), :].astype(F32) + ex[ex_at(2 * kind + 1, i), :].astype(F32)

        half_rows = rows // 2
        own_half = pl.ds(pl.multiple_of(core * half_rows, half_rows), half_rows)

        def hop_copy(i, target):
            return send(resb.at[lax.rem(i, 2), own_half], target.at[i, own_half], sh, (0, i), to_y)

        def hop_core(i, target):
            return send(target.at[i, own_half], target.at[i, own_half], sh, (1, i), to_core)

        pass_on(0, 0, 1)

        @pl.when(first_section)
        def _():
            rows_wait(rows_in(xin, to_xy), xbuf)
            pass_on(1, 0)

        @pl.when(last_section)
        def _():
            pass_on(1, 0)
            pass_on(2, 0, 1)
            pass_on(3, 0, 1, 2)
            copies = rows_in(cot, to_x)
            rows_wait(copies, cotb)
            copies[2].wait_send()
            rows_in(xin, to_xy)[2].wait_send()

        misc_local.wait()
        misc_x.wait()
        attn_gain, mlp_gain, out_bias, down_bias = (mc[0, i : i + 1, :] for i in range(4))
        have(0)

        def masked(scores, i, j0, j1, diagonal):
            same = segc[j0:j1, :]
            same = jnp.concatenate([same] * (rows // same.shape[1]), axis=1)
            cols = slice(i * rows, (i + 1) * rows)
            allowed = same == seg[pl.ds(xh, 1), cols].astype(F32)
            if diagonal:
                key = lax.broadcasted_iota(jnp.int32, scores.shape, 0)
                query = lax.broadcasted_iota(jnp.int32, scores.shape, 1)
                allowed = allowed & (key <= query)
            return jnp.where(allowed, scores, NEGATIVE)

        def key_parts(i):
            parts = [(i * rows, (i + 1) * rows, True)]
            if i > 0:
                parts.append((0, i * rows, False))
            return parts

        def project(i):
            full = expanded(xbuf[i])
            normed = (full * norm_factor(full) * attn_gain).astype(BF16)
            nrm[i] = normed
            cols = at_row(i)
            for slot in range(slots):
                three = dot(wq[slot], normed, NT)
                bias = jnp.broadcast_to(mc[slot, 5:6, : 2 * part], (8, 2 * part)).T[:, 0:1]
                query = (three[:part] + bias[:part]).astype(BF16) * SCALE
                key = three[part : 2 * part]
                value = (three[2 * part :] + bias[part:]).astype(BF16).astype(F32)
                for h in range(hs):
                    at = slice(h * HD, (h + 1) * HD)
                    head = slot * hs + h
                    qt[i, head] = query[at].astype(BF16)
                    kt[head, :, cols] = key[at].astype(BF16)
                    vt[head, :, cols] = value[at].astype(BF16)
                    kn[head, cols, :] = key[at].T.astype(BF16)
                    vn[head, cols, :] = value[at].T.astype(BF16)

        def attend(i, h):
            cols = slice(i * rows, (i + 1) * rows)
            parts = key_parts(i)
            query = qt[i, h]
            scores = [masked(dot(kn[h, a:b], query), i, a, b, g) for a, b, g in parts]
            highest = scores[0].max(axis=0, keepdims=True)
            for score in scores[1:]:
                highest = jnp.maximum(highest, score.max(axis=0, keepdims=True))
            total, context = 0.0, 0.0
            for score, (a, b, _) in zip(scores, parts, strict=True):
                power = jnp.exp(score - highest)
                total = total + row_sum(power)
                context = context + dot(vt[h, :, a:b], power.astype(BF16))
            ctx[h, :, cols] = (context / total).astype(BF16)
            lse[i, h] = highest + jnp.log(total)

        def each_block(i, body):
            for block in range(blocks):

                @pl.when(i == block)
                def _():
                    loop(heads, lambda h: body(block, h))

        def attention_rows(i):
            @pl.when(last_section & (i == 0))
            def _():
                hop_copy(0, xbuf).wait_recv()
                hop_core(0, xbuf).start()

            @pl.when(last_section)
            def _():
                hop_core(i, xbuf).wait()

            project(i)
            each_block(i, attend)

            @pl.when(i == 0)
            def _():
                have(1)

            context = ctx[:, :, at_row(i)].reshape(heads * HD, rows)
            pair_send(0, i, dot(context, wo[...].reshape(heads * HD, width), TN))

            for step, (which, cut) in enumerate(((2, 0), (2, 1), (3, 0), (3, 1))):

                @pl.when((i == step) & first_section)
                def _():
                    pass_on(which, cut)

            @pl.when(last_section & (i < blocks - 1))
            def _():
                hop_copy(i + 1, xbuf).wait_recv()
                hop_core(i + 1, xbuf).start()

        def mlp_rows(i):
            @pl.when(i == 0)
            def _():
                have(2)

            branch = pair_sum(0, i) + out_bias
            middle = expanded(xbuf[i]) + centred(branch)
            pool[mid_at(i), :] = middle
            normed = middle * norm_factor(middle) * mlp_gain
            n2t[:, at_row(i)] = normed.T.astype(BF16)
            normed = normed.astype(BF16)
            for slot in range(slots):
                pre = dot(normed, wu[slot]) + mc[slot, 4:5, :]
                square = pre * pre
                bend = jnp.tanh(GELU_C * pre * (1.0 + GELU_A * square))
                grow = 0.5 * (1.0 + bend)
                hid[slot, i] = (pre * grow).astype(BF16)
                slope = GELU_C * (1.0 + 3.0 * GELU_A * square)
                gp[slot, i] = (grow + 0.5 * pre * (1.0 - bend * bend) * slope).astype(BF16)

            @pl.when(i == 0)
            def _():
                @pl.when(first_section)
                def _():
                    pass_on(3, 2)

                have(3)

            branch = dot(hid[0, i], wd[0], NT)
            for slot in range(1, slots):
                branch = branch + dot(hid[slot, i], wd[slot], NT)
            pair_send(1, i, branch)

        def keep_out(i, value):
            @pl.when((i == t) | (i == t_x))
            def _():
                outt[jnp.where(i == t, 0, 1)] = value.T.astype(BF16)

        def result_rows(i):
            result = pool[mid_at(i), :] + centred(pair_sum(1, i) + down_bias)
            keep_out(i, result)

            @pl.when(first_section)
            def _():
                @pl.when(i >= 2)
                def _():
                    hop_copy(i - 2, xbuf).wait_send()

                lane = lax.broadcasted_iota(jnp.int32, result.shape, 1)
                resb[lax.rem(i, 2)] = jnp.where(lane == width - 1, 0.0, result).astype(BF16)
                hop_copy(i, xbuf).start()

        def forward(step):
            i_mlp = jnp.where(first_section, step - blocks, step - 1)
            i_res = i_mlp - 1
            some_res = (i_res >= 0) & (i_res < blocks)

            @pl.when(step < blocks)
            def _():
                attention_rows(step)

            @pl.when(last_section & some_res)
            def _():
                result_rows(i_res)

            @pl.when((i_mlp >= 0) & (i_mlp < blocks))
            def _():
                mlp_rows(i_mlp)

            @pl.when(first_section & some_res)
            def _():
                result_rows(i_res)

        loop(2 * blocks + 1, forward)

        def rows_out(target, which):
            return (
                pltpu.make_async_copy(outt.at[0], target.at[xh], sl.at[2]),
                send(outt.at[1], target.at[xh], so, (which,), to_x),
            )

        act_copies = rows_out(act, 0)
        for copy in act_copies:
            copy.start()

        @pl.when(first_section)
        def _():
            loop(2, lambda i: hop_copy(blocks - 2 + i, xbuf).wait_send())

        def other_at(k):
            row = k * CHUNK
            early = lax.div(row, 2 * rows) * length + 2 * rows + lax.rem(row, 2 * rows)
            return pl.ds(pl.multiple_of(jnp.where(row < 8 * rows, early, row - 8 * rows), CHUNK), CHUNK)

        def own_at(k):
            row = k * CHUNK
            late = jnp.where(row < 7 * rows, row - 6 * rows, row - 3 * rows)
            late = jnp.where(row < 6 * rows, row + 3 * rows, late)
            return pl.ds(pl.multiple_of(jnp.where(row < 3 * rows, row + rows, late), CHUNK), CHUNK)

        def x_copy(k):
            return send(ex.at[other_at(k)], xrec.at[k], sr, (k,), to_x)

        def put(turn, first, value):
            @pl.when(turn == 0)
            def _():
                for k in range(value.shape[0] // CHUNK):
                    ex[other_at(first + k), :] = value[k * CHUNK : (k + 1) * CHUNK].astype(BF16)

            @pl.when(turn == 1)
            def _():
                for k in range(value.shape[0] // CHUNK):
                    pool[own_at(first + k), :] = value[k * CHUNK : (k + 1) * CHUNK]

        def start(turn, first, number):
            @pl.when(turn == 0)
            def _():
                loop(number, lambda k: x_copy(first + k).start())

        def mlp_grads(turn):
            slot = 1 - turn
            tile = 256
            tiles = width // tile

            def down_part(k):
                at = pl.ds(pl.multiple_of(k * tile, tile), tile)
                put(turn, k * (tile // CHUNK), dot(gmt[at, :], hid[slot].reshape(length, units)))

            loop(tiles, down_part)
            start(turn, 0, width // CHUNK)

            def up_part(k):
                at = pl.ds(pl.multiple_of(k * tile, tile), tile)
                first = width // CHUNK + k * (tile // CHUNK)
                put(turn, first, dot(n2t[at, :], gp[slot].reshape(length, units)))

            loop(tiles, up_part)
            start(turn, width // CHUNK, width // CHUNK)

        def down_back(i):
            @pl.when(first_section)
            def _():
                hop_copy(i, cotb).wait_recv()
                hop_core(i, cotb).start()
                hop_core(i, cotb).wait()

            grad = centred(cotb[i].astype(F32))
            pool[grad_at(i), :] = grad
            gmt[:, at_row(i)] = grad.T.astype(BF16)
            grad = grad.astype(BF16)
            sown[3:4, :] += row_sum(grad.astype(F32))
            branch = 0.0
            for slot, sums in ((0, sown), (1, soth)):
                before = (dot(grad, wd[slot]) * gp[slot, i].astype(F32)).astype(BF16)
                gp[slot, i] = before
                sums[4:5, :] += row_sum(before.astype(F32))
                branch = branch + dot(before, wu[slot], NT)
            pair_send(0, i, branch)

        def out_back(i):
            grad, gain_grad = norm_back(pair_sum(0, i), pool[mid_at(i), :], mlp_gain)
            sown[2:3, :] += gain_grad
            grad = grad + pool[grad_at(i), :]
            pool[grad_at(i), :] = grad
            grad = grad.astype(BF16)
            gat[i] = grad
            sown[1:2, :] += row_sum(grad.astype(F32))
            back = dot(wo[...].reshape(heads * HD, width), grad, NT).astype(BF16)
            for h in range(heads):
                dot_[i, h] = back[h * HD : (h + 1) * HD]

        def attend_back(i, h):
            slot, place = lax.div(h, hs), lax.rem(h, hs)
            query, back = qt[i, h], dot_[i, h]
            parts = key_parts(i)
            cols = slice(i * rows, (i + 1) * rows)
            probs, g_probs = [], []
            centre = 0.0
            for a, b, g in parts:
                prob = jnp.exp(masked(dot(kn[h, a:b], query), i, a, b, g) - lse[i, h])
                g_prob = dot(vn[h, a:b], back)
                centre = centre + row_sum(prob * g_prob)
                probs.append(prob)
                g_probs.append(g_prob)
            g_query = 0.0
            for prob, g_prob, (a, b, _) in zip(probs, g_probs, parts, strict=True):
                g_score = (prob * (g_prob - centre)).astype(BF16)
                g_value = dot(back, prob.astype(BF16), NT)
                g_key = dot(query, g_score, NT)
                g_query = g_query + dot(kt[h, :, a:b], g_score)
                if i == blocks - 1:
                    dv[h, :, a:b] = g_value
                    dk[h, :, a:b] = g_key
                else:
                    dv[h, :, a:b] += g_value
                    dk[h, :, a:b] += g_key
            dqkv[slot, 0, place, :, cols] = (g_query * SCALE).astype(BF16)
            dqkv[slot, 1, place, :, cols] = dk[h, :, cols].astype(BF16)
            dqkv[slot, 2, place, :, cols] = dv[h, :, cols].astype(BF16)

        def qkv_back(i):
            branch = 0.0
            for slot in range(slots):
                three = dqkv[slot, :, :, :, at_row(i)].reshape(3 * part, rows)
                branch = branch + dot(three, wq[slot], TN)
            pair_send(1, i, branch)

        def in_back(i):
            grad, gain_grad = norm_back(pair_sum(1, i), expanded(xbuf[i]), attn_gain)
            sown[0:1, :] += gain_grad
            grad = grad + pool[grad_at(i), :]
            grad = grad - grad[:, width - 1 :]
            keep_out(i, grad)

            @pl.when(last_section)
            def _():
                @pl.when(i < blocks - 2)
                def _():
                    hop_copy(i + 2, cotb).wait_send()

                resb[lax.rem(i, 2)] = grad.astype(BF16)
                hop_copy(i, cotb).start()

        def backward(step):
            behind = jnp.where(first_section, 0, 1)
            n_rest = step - behind
            n_in = n_rest - 1
            last = blocks - 1

            @pl.when(step < blocks)
            def _():
                down_back(last - step)

            @pl.when(step == jnp.where(first_section, blocks - 1, blocks + 2))
            def _():
                loop(2, mlp_grads)

            @pl.when(n_in == 0)
            def _():
                for copy in act_copies:
                    copy.wait()

            @pl.when((n_in >= 0) & (n_in < blocks))
            def _():
                in_back(last - n_in)

            @pl.when((n_rest >= 0) & (n_rest < blocks))
            def _():
                i = last - n_rest
                out_back(i)
                each_block(i, attend_back)
                qkv_back(i)

        loop(blocks + 3, backward)

        ones = jnp.ones((8, length), BF16)
        sown[5:6, : 3 * part] = dot(ones, dqkv[0].reshape(3 * part, length), NT)[0:1]
        soth[5:6, : 3 * part] = dot(ones, dqkv[1].reshape(3 * part, length), NT)[0:1]
        soth[0:4, :] = sown[0:4, :]
        small_x = send(soth, srec, ss, (0,), to_x)
        small_x.start()

        def attention_grads(turn):
            slot = 1 - turn

            def qkv_part(k):
                first = (2 * width) // CHUNK + k * (part // CHUNK)
                put(turn, first, dot(dqkv[slot, k].reshape(part, length), nrm[...].reshape(length, width)))

            loop(3, qkv_part)
            first = (2 * width + 3 * part) // CHUNK
            context = ctx[pl.ds(slot * hs, hs)].reshape(part, length)
            put(turn, first, dot(context, gat[...].reshape(length, width)))
            start(turn, 2 * (width // CHUNK), chunks - 2 * (width // CHUNK))

        loop(2, attention_grads)
        eg_copies = rows_out(eg, 1)
        for copy in eg_copies:
            copy.start()

        middle = count // 2
        on_left = d < middle
        depth = jnp.where(on_left, d, count - 1 - d)
        has_outer = depth > 0
        is_mid = depth == middle - 1
        side = jnp.where(on_left, 0, 1)
        inner = (s, t, jnp.where(on_left, d + 1, d - 1))
        outer = (s, t, jnp.where(on_left, d - 1, d + 1))
        lag = 3
        lag_in = lag * depth
        lag_mid = lag * middle
        lag_out = lag_mid + lag * (middle - depth)
        lag_all = lag_mid + lag * middle

        def in_copy(k):
            return send(xrec.at[k], cin.at[k], sc, (0, k), inner)

        def cross_copy(k):
            return send(xrec.at[k], fin.at[k], sc, (1, k), inner)

        def back_copy(k):
            return send(fin.at[k], fin.at[k], sc, (2, k), inner)

        def out_copy(k):
            return send(fin.at[k], fin.at[k], sc, (3, k), outer)

        def chunk_out(k):
            place = 0
            for name in ("down", "up", "qkv", "out"):
                number = r[name].shape[0] // CHUNK

                @pl.when((k >= place) & (k < place + number))
                def _():
                    at = pl.ds(pl.multiple_of((k - place) * CHUNK, CHUNK), CHUNK)
                    pltpu.make_async_copy(fin.at[k], r[name].at[at], so.at[0, 2 + k]).start()

                place += number

        s_in = send(sown, scin, ss, (1,), inner)
        s_cross = send(sown, sfin, ss, (2,), inner)
        s_back = send(sfin, sfin, ss, (3,), inner)
        s_out = send(sfin, sfin, ss, (4,), outer)

        def reduce_small(it):
            small_owner = side == 0
            begin = chunks - 4

            @pl.when(it == begin)
            def _():
                small_x.wait()
                sown[...] = sown[...] + srec[...]

            @pl.when(it == begin + lag_in)
            def _():
                @pl.when(has_outer)
                def _():
                    s_in.wait_recv()
                    sown[...] = sown[...] + scin[...]

                @pl.when(jnp.logical_not(is_mid))
                def _():
                    s_in.start()

                @pl.when(is_mid & jnp.logical_not(small_owner))
                def _():
                    s_cross.start()

            @pl.when((it == begin + lag_mid) & is_mid & small_owner)
            def _():
                s_cross.wait_recv()
                sfin[...] = sfin[...] + sown[...]
                s_back.start()

            @pl.when(it == begin + lag_out)
            def _():
                @pl.when(is_mid & jnp.logical_not(small_owner))
                def _():
                    s_back.wait_recv()

                @pl.when(jnp.logical_not(is_mid))
                def _():
                    s_out.wait_recv()

                @pl.when(has_outer)
                def _():
                    s_out.start()

        def reduce(it):
            @pl.when(it < chunks)
            def _():
                k = it
                x_copy(k).wait()
                xrec[k] = (pool[own_at(k), :] + xrec[k].astype(F32)).astype(BF16)

            k_in = it - lag_in

            @pl.when((k_in >= 0) & (k_in < chunks))
            def _():
                k = k_in
                owner = lax.rem(k, 2) == side

                @pl.when(has_outer)
                def _():
                    in_copy(k).wait_recv()
                    xrec[k] = (xrec[k].astype(F32) + cin[k].astype(F32)).astype(BF16)

                @pl.when(jnp.logical_not(is_mid))
                def _():
                    in_copy(k).start()

                @pl.when(is_mid & jnp.logical_not(owner))
                def _():
                    cross_copy(k).start()

            k_mid = it - lag_mid

            @pl.when((k_mid >= 0) & (k_mid < chunks) & is_mid)
            def _():
                k = k_mid

                @pl.when(lax.rem(k, 2) == side)
                def _():
                    cross_copy(k).wait_recv()
                    fin[k] = (xrec[k].astype(F32) + fin[k].astype(F32)).astype(BF16)
                    back_copy(k).start()

                    @pl.when(has_outer)
                    def _():
                        out_copy(k).start()

                    chunk_out(k)

            k_out = it - lag_out

            @pl.when((k_out >= 0) & (k_out < chunks))
            def _():
                k = k_out
                owner = lax.rem(k, 2) == side

                @pl.when(is_mid & jnp.logical_not(owner))
                def _():
                    back_copy(k).wait_recv()

                @pl.when(jnp.logical_not(is_mid))
                def _():
                    out_copy(k).wait_recv()

                @pl.when(jnp.logical_not(is_mid & owner))
                def _():
                    @pl.when(has_outer)
                    def _():
                        out_copy(k).start()

                    chunk_out(k)

            reduce_small(it)

        loop(chunks + lag_all, reduce)
        small[...] = sfin[...]

        @pl.when(jnp.logical_not(is_mid))
        def _():
            s_in.wait_send()

        @pl.when(is_mid & (side == 1))
        def _():
            s_cross.wait_send()

        @pl.when(is_mid & (side == 0))
        def _():
            s_back.wait_send()

        @pl.when(has_outer)
        def _():
            s_out.wait_send()

        def drain(k):
            owner = lax.rem(k, 2) == side

            @pl.when(jnp.logical_not(is_mid))
            def _():
                in_copy(k).wait_send()

            @pl.when(is_mid & jnp.logical_not(owner))
            def _():
                cross_copy(k).wait_send()

            @pl.when(is_mid & owner)
            def _():
                back_copy(k).wait_send()

            @pl.when(has_outer)
            def _():
                out_copy(k).wait_send()

            pltpu.make_async_copy(fin.at[k], r["down"].at[pl.ds(0, CHUNK)], so.at[0, 2 + k]).wait()

        loop(chunks, drain)

        @pl.when(last_section)
        def _():
            loop(2, lambda i: hop_copy(i, cotb).wait_send())

        for copy in eg_copies:
            copy.wait()

    return kernel


def per_device(
    block_input,
    segments,
    cotangent,
    attn_gain,
    qkv_weight,
    qv_bias,
    out_weight,
    out_bias,
    mlp_gain,
    up_projection_weight,
    up_bias,
    down_projection_weight,
    down_bias,
):
    micros, rows, _, kept = block_input.shape
    width = qkv_weight.shape[1]
    part = qkv_weight.shape[3]
    units = up_projection_weight.shape[2]
    blocks = lax.axis_size("tensor")
    count = lax.axis_size("dp")
    length = blocks * rows
    slots = 2
    hs = part // HD
    heads = slots * hs
    chunks = (2 * width + 4 * part) // CHUNK

    def features_first(array):
        return jnp.pad(array[:, :, 0, :].transpose(0, 2, 1), ((0, 0), (0, width - kept), (0, 0)))

    qv_row = jnp.pad(qv_bias.reshape(1, 2 * part), ((0, 0), (0, width - 2 * part)))
    rows_of = [attn_gain, mlp_gain, out_bias, down_bias, up_bias, qv_row, up_bias, qv_row]
    inputs = {
        "xin": features_first(block_input),
        "cot": features_first(cotangent),
        "wqh": qkv_weight[0].transpose(1, 2, 0).reshape(3 * part, width),
        "woh": out_weight[0],
        "wuh": up_projection_weight[0],
        "wdh": down_projection_weight[0],
        "misc": jnp.concatenate(rows_of).astype(F32),
        "seg": segments[:, 0, :],
    }
    outputs = {
        "act": ((micros, width, rows), BF16),
        "eg": ((micros, width, rows), BF16),
        "down": ((width, units), BF16),
        "up": ((width, units), BF16),
        "qkv": ((3 * part, width), BF16),
        "out": ((part, width), BF16),
        "small": ((8, width), F32),
    }
    scratch = {
        "wq": ((slots, 3 * part, width), BF16),
        "wo": ((slots, part, width), BF16),
        "wu": ((slots, width, units), BF16),
        "wd": ((slots, width, units), BF16),
        "mc": ((slots, 8, width), F32),
        "xbuf": ((blocks, rows, width), BF16),
        "cotb": ((blocks, rows, width), BF16),
        "resb": ((2, rows, width), BF16),
        "outt": ((2, width, rows), BF16),
        "pool": ((max(2 * length, chunks * CHUNK), width), F32),
        "nrm": ((blocks, rows, width), BF16),
        "n2t": ((width, length), BF16),
        "qt": ((blocks, heads, HD, rows), BF16),
        "kt": ((heads, HD, length), BF16),
        "vt": ((heads, HD, length), BF16),
        "kn": ((heads, length, HD), BF16),
        "vn": ((heads, length, HD), BF16),
        "ctx": ((heads, HD, length), BF16),
        "lse": ((blocks, heads, 1, rows), F32),
        "segc": ((length, 128), F32),
        "gp": ((slots, blocks, rows, units), BF16),
        "hid": ((slots, blocks, rows, units), BF16),
        "gmt": ((width, length), BF16),
        "gat": ((blocks, rows, width), BF16),
        "dot": ((blocks, heads, HD, rows), BF16),
        "dqkv": ((slots, 3, hs, HD, length), BF16),
        "dk": ((heads, HD, length), F32),
        "dv": ((heads, HD, length), F32),
        "ex": ((4 * length, width), BF16),
        "xrec": ((chunks, CHUNK, width), BF16),
        "cin": ((chunks, CHUNK, width), BF16),
        "fin": ((chunks, CHUNK, width), BF16),
        "sown": ((8, width), F32),
        "soth": ((8, width), F32),
        "srec": ((8, width), F32),
        "scin": ((8, width), F32),
        "sfin": ((8, width), F32),
    }
    dma = pltpu.SemaphoreType.DMA
    semaphores = {
        "sl": dma((8,)),
        "sg": dma((2, 4)),
        "sw": dma((2, 2, 12)),
        "se": dma((2, 2, blocks)),
        "sh": dma((2, 2, blocks)),
        "so": dma((2, 2 + chunks)),
        "sr": dma((2, chunks)),
        "sc": dma((2, 4, chunks)),
        "ss": dma((2, 5)),
    }
    in_vmem = {"seg", "small"}

    def spec(name):
        return pl.BlockSpec(memory_space=pltpu.VMEM if name in in_vmem else pl.ANY)

    names = [*inputs, *outputs, *scratch, *semaphores]
    act, eg, down, up, qkv, out, small = pl.pallas_call(
        make_kernel(names, count),
        out_shape=[jax.ShapeDtypeStruct(*item) for item in outputs.values()],
        in_specs=[spec(name) for name in inputs],
        out_specs=[spec(name) for name in outputs],
        scratch_shapes=[pltpu.VMEM(*item) for item in scratch.values()] + list(semaphores.values()),
        compiler_params=pltpu.CompilerParams(
            collective_id=0, has_side_effects=True, vmem_limit_bytes=63 * 1024 * 1024
        ),
        name="layers",
    )(*inputs.values())

    def positions_first(array):
        return array[:, :kept, :].transpose(0, 2, 1)[None, :, :, None, :]

    qv = small[5, : 3 * part].reshape(3, part)
    return (
        positions_first(act),
        positions_first(eg).astype(F32),
        small[0:1],
        qkv.reshape(3, part, width).transpose(2, 0, 1).astype(F32)[None],
        qv[0::2][None],
        out.astype(F32)[None],
        small[1:2],
        small[2:3],
        up.astype(F32)[None],
        small[4:5, :units],
        down.astype(F32)[None],
        small[3:4],
    )


def solution(mesh):
    in_specs = (
        P(None, "tensor", "dp", None),
        P(None, "dp", None),
        P(None, "tensor", "dp", None),
        P("section", None),
        P("section", None, None, "tensor"),
        P("section", None, "tensor"),
        P("section", "tensor", None),
        P("section", None),
        P("section", None),
        P("section", None, "tensor"),
        P("section", "tensor"),
        P("section", None, "tensor"),
        P("section", None),
    )
    out_specs = (
        P("section", None, "tensor", "dp", None),
        P("section", None, "tensor", "dp", None),
        P("section", None),
        P("section", None, None, "tensor"),
        P("section", None, "tensor"),
        P("section", "tensor", None),
        P("section", None),
        P("section", None),
        P("section", None, "tensor"),
        P("section", "tensor"),
        P("section", None, "tensor"),
        P("section", None),
    )
    return jax.shard_map(
        per_device, mesh=mesh, in_specs=in_specs, out_specs=out_specs, check_vma=False
    )
```

time: 359 us -> 300 us (0.84)
  Pallas kernels: 334 us -> 282 us
  local copies, waits for them, and re-layouts: 20.5 us -> 9.83 us
  other arithmetic: 3.6 us -> 7.27 us
    pallas_call x1, Pallas kernels: 334 us -> 282 us  [per_device(): pl.pallas_call(make_kernel(names, count), out_shape=[jax.ShapeDtypeStruct...]
    broadcast_in_dim x0 -> x3, other arithmetic: none -> 6.49 us  [the longest x1 4.29 us: per_device(): down.astype(F32)[None]]
    split x2 -> x0, local copies, waits for them, and re-layouts: 3.97 us -> none  [per_device(): jnp.split(grads, [width, 2 * width, 2 * width + 3 * part])]
    broadcast_in_dim x6 -> x0, local copies, waits for them, and re-layouts: 3.93 us -> none  [the longest x1 1 us: per_device(): jnp.broadcast_to(segment[:, None], (length, 128))]
    unnamed x28 -> x31, local copies, waits for them, and re-layouts: 9.33 us -> 6.52 us
where the time goes in v2:
time: 300 us
  Pallas kernels  282 us (94%)
  local copies, waits for them, and re-layouts  9.83 us (3%)
  other arithmetic  7.27 us (2%)
    pallas_call x1, Pallas kernels, per_device(): pl.pallas_call(make_kernel(names, count), out_shape=[jax.ShapeDtypeStruct...  282 us
    unnamed x31, local copies, waits for them, and re-layouts  6.52 us

profile of v2, /device:TPU:0, one launch (start us, length us, event | category | flops | bytes accessed | tf_op | source)
XLA Modules:
  0.0 299.7 jit_solution(17120824621849411111)
XLA Ops:
  0.7 1.3 copy.34
  2.0 0.9 pad.11.refs_0_
  2.9 0.0 copy-start.9
  2.9 0.0 copy-start.10
  2.9 0.0 copy-start.11
  3.0 0.0 copy-start.7
  3.0 0.1 copy.33
  3.1 0.9 pad.12.refs_1_
  4.0 0.0 copy-done.12
  4.0 0.1 reshape.36
  4.1 0.0 copy-done.8
  4.2 0.1 concatenate.3
  4.2 0.6 convert_element_type.27.refs_6_
  4.8 0.6 copy.35
  5.4 281.8 %layers.1 = (bf16[2,768,256]{2,1,0:T(8,128)(2,1)}, bf16[2,768,256]{2,1,0:T(8,128)(2,1)}, bf16[768,768]{1,0:T(8,128)(2,1)}, bf16[768,768]{1,0:T(8,128)(2,1)}, bf1...) custom-call(bf16[2,768,256]{2,1,0:T(8,128)(2,1)} %pad.11.refs_0_, ...), custom_call_target="tpu_custom_call" | custom-call | tf_op jit(solution)/shard_map/layers/pallas_call | solution.py:941
  287.2 4.3 %bitcast_convert_fusion = (f32[1,768,768]{2,1,0:T(8,128)}, f32[1,768,768]{2,1,0:T(8,128)}) fusion(bf16[768,768]{1,0:T(8,128)(2,1)} %get-tuple-element.25, bf16[768,768]{1,0:T(8,128)(2,1)} %get-tuple-element.24), kind=kLoop, calls=%fused_computation.2 | loop fusion | flops 1179648 | bytes 7077888 | tf_op jit(solution)/shard_map/broadcast_in_dim | solution.py:968
  291.5 0.2 convert_bitcast_fusion.1
  291.7 2.8 copy.28
  294.5 1.7 copy.27
  296.2 0.6 fusion
  296.8 0.1 reshape_squeeze.3
  296.9 0.6 slice.31
  297.5 1.4 convert_bitcast_fusion
  298.8 0.9 bitcast_convert_fusion.2
  (22 shorter events, 0.1 us)
Async XLA Ops:
  0.6 2.3 copy-start.3
  2.9 1.1 copy-start.12
  2.9 1.2 copy-start.6
  2.9 1.2 copy-start.8
  2.9 1.2 copy-start.9
  2.9 1.2 copy-start.10
  2.9 1.2 copy-start.11
  3.0 1.9 copy-start.7
  287.2 4.3 %copy-start.1 = (bf16[2,768,256]{2,1,0:T(8,128)(2,1)S(1)}, bf16[2,768,256]{2,1,0:T(8,128)(2,1)}, u32[]{:S(2)}) copy-start(bf16[2,768,256]{2,1,0:T(8,128)(2,1)} %get-tuple-element.19) | copy-start | bytes 2359300
  287.2 4.3 %copy-start.2 = (bf16[2,768,256]{2,1,0:T(8,128)(2,1)S(1)}, bf16[2,768,256]{2,1,0:T(8,128)(2,1)}, u32[]{:S(2)}) copy-start(bf16[2,768,256]{2,1,0:T(8,128)(2,1)} %get-tuple-element.20) | copy-start | bytes 2359300
  294.5 1.7 copy-start.5
  294.5 3.0 copy-start
  296.2 2.7 copy-start.4

commit v3 on v2

--- a/solution.py
+++ b/solution.py
@@ -10,6 +10,7 @@
 SCALE = 0.125
 NEGATIVE = -1e30
 CHUNK = 64
+EARLY = ({3: (0, 1), 4: (5, 6)}, {3: (1, 4), 4: (6, 7)}, {3: (4, 5), 4: (7, 8)})
 MESH = pl.DeviceIdType.MESH
 F32 = jnp.float32
 BF16 = jnp.bfloat16
@@ -437,9 +438,9 @@
 
         def own_at(k):
             row = k * CHUNK
-            late = jnp.where(row < 7 * rows, row - 6 * rows, row - 3 * rows)
-            late = jnp.where(row < 6 * rows, row + 3 * rows, late)
-            return pl.ds(pl.multiple_of(jnp.where(row < 3 * rows, row + rows, late), CHUNK), CHUNK)
+            late = jnp.where(row < 7 * rows, row - 5 * rows, row - 3 * rows)
+            late = jnp.where(row < 5 * rows, row + 4 * rows, late)
+            return pl.ds(pl.multiple_of(jnp.where(row < 2 * rows, row + 2 * rows, late), CHUNK), CHUNK)
 
         def x_copy(k):
             return send(ex.at[other_at(k)], xrec.at[k], sr, (k,), to_x)
@@ -460,25 +461,182 @@
             def _():
                 loop(number, lambda k: x_copy(first + k).start())
 
+        tile = 256
+        tiles = width // tile
+
+        def down_part(turn, k):
+            at = pl.ds(pl.multiple_of(k * tile, tile), tile)
+            first = k * (tile // CHUNK)
+            put(turn, first, dot(gmt[at, :], hid[1 - turn].reshape(length, units)))
+            start(turn, first, tile // CHUNK)
+
+        def up_part(turn, k):
+            at = pl.ds(pl.multiple_of(k * tile, tile), tile)
+            first = width // CHUNK + k * (tile // CHUNK)
+            put(turn, first, dot(n2t[at, :], gp[1 - turn].reshape(length, units)))
+            start(turn, first, tile // CHUNK)
+
         def mlp_grads(turn):
-            slot = 1 - turn
-            tile = 256
-            tiles = width // tile
-
-            def down_part(k):
-                at = pl.ds(pl.multiple_of(k * tile, tile), tile)
-                put(turn, k * (tile // CHUNK), dot(gmt[at, :], hid[slot].reshape(length, units)))
-
-            loop(tiles, down_part)
-            start(turn, 0, width // CHUNK)
-
-            def up_part(k):
-                at = pl.ds(pl.multiple_of(k * tile, tile), tile)
-                first = width // CHUNK + k * (tile // CHUNK)
-                put(turn, first, dot(n2t[at, :], gp[slot].reshape(length, units)))
-
-            loop(tiles, up_part)
-            start(turn, width // CHUNK, width // CHUNK)
+            loop(tiles, lambda k: down_part(turn, k))
+            loop(tiles - 1, lambda k: up_part(turn, k))
+
+        middle = count // 2
+        on_left = d < middle
+        depth = jnp.where(on_left, d, count - 1 - d)
+        has_outer = depth > 0
+        is_mid = depth == middle - 1
+        side = jnp.where(on_left, 0, 1)
+        inner = (s, t, jnp.where(on_left, d + 1, d - 1))
+        outer = (s, t, jnp.where(on_left, d - 1, d + 1))
+        lag = 3
+        lag_in = lag * depth
+        lag_mid = lag * middle
+        lag_out = lag_mid + lag * (middle - depth)
+        lag_all = lag_mid + lag * middle
+
+        def in_copy(k):
+            return send(xrec.at[k], cin.at[k], sc, (0, k), inner)
+
+        def cross_copy(k):
+            return send(xrec.at[k], fin.at[k], sc, (1, k), inner)
+
+        def back_copy(k):
+            return send(fin.at[k], fin.at[k], sc, (2, k), inner)
+
+        def out_copy(k):
+            return send(fin.at[k], fin.at[k], sc, (3, k), outer)
+
+        def chunk_out(k):
+            place = 0
+            for name in ("down", "up", "qkv", "out"):
+                number = r[name].shape[0] // CHUNK
+
+                @pl.when((k >= place) & (k < place + number))
+                def _():
+                    at = pl.ds(pl.multiple_of((k - place) * CHUNK, CHUNK), CHUNK)
+                    pltpu.make_async_copy(fin.at[k], r[name].at[at], so.at[0, 2 + k]).start()
+
+                place += number
+
+        small_x = send(soth, srec, ss, (0,), to_x)
+        s_in = send(sown, scin, ss, (1,), inner)
+        s_cross = send(sown, sfin, ss, (2,), inner)
+        s_back = send(sfin, sfin, ss, (3,), inner)
+        s_out = send(sfin, sfin, ss, (4,), outer)
+
+        def reduce_small(it):
+            small_owner = side == 0
+            begin = chunks - 4
+
+            @pl.when(it == begin)
+            def _():
+                small_x.wait()
+                sown[...] = sown[...] + srec[...]
+
+            @pl.when(it == begin + lag_in)
+            def _():
+                @pl.when(has_outer)
+                def _():
+                    s_in.wait_recv()
+                    sown[...] = sown[...] + scin[...]
+
+                @pl.when(jnp.logical_not(is_mid))
+                def _():
+                    s_in.start()
+
+                @pl.when(is_mid & jnp.logical_not(small_owner))
+                def _():
+                    s_cross.start()
+
+            @pl.when((it == begin + lag_mid) & is_mid & small_owner)
+            def _():
+                s_cross.wait_recv()
+                sfin[...] = sfin[...] + sown[...]
+                s_back.start()
+
+            @pl.when(it == begin + lag_out)
+            def _():
+                @pl.when(is_mid & jnp.logical_not(small_owner))
+                def _():
+                    s_back.wait_recv()
+
+                @pl.when(jnp.logical_not(is_mid))
+                def _():
+                    s_out.wait_recv()
+
+                @pl.when(has_outer)
+                def _():
+                    s_out.start()
+
+        def reduce(it):
+            @pl.when(it < chunks)
+            def _():
+                k = it
+                x_copy(k).wait()
+                xrec[k] = (pool[own_at(k), :] + xrec[k].astype(F32)).astype(BF16)
+
+            k_in = it - lag_in
+
+            @pl.when((k_in >= 0) & (k_in < chunks))
+            def _():
+                k = k_in
+                owner = lax.rem(k, 2) == side
+
+                @pl.when(has_outer)
+                def _():
+                    in_copy(k).wait_recv()
+                    xrec[k] = (xrec[k].astype(F32) + cin[k].astype(F32)).astype(BF16)
+
+                @pl.when(jnp.logical_not(is_mid))
+                def _():
+                    in_copy(k).start()
+
+                @pl.when(is_mid & jnp.logical_not(owner))
+                def _():
+                    cross_copy(k).start()
+
+            k_mid = it - lag_mid
+
+            @pl.when((k_mid >= 0) & (k_mid < chunks) & is_mid)
+            def _():
+                k = k_mid
+
+                @pl.when(lax.rem(k, 2) == side)
+                def _():
+                    cross_copy(k).wait_recv()
+                    fin[k] = (xrec[k].astype(F32) + fin[k].astype(F32)).astype(BF16)
+                    back_copy(k).start()
+
+                    @pl.when(has_outer)
+                    def _():
+                        out_copy(k).start()
+
+                    chunk_out(k)
+
+            k_out = it - lag_out
+
+            @pl.when((k_out >= 0) & (k_out < chunks))
+            def _():
+                k = k_out
+                owner = lax.rem(k, 2) == side
+
+                @pl.when(is_mid & jnp.logical_not(owner))
+                def _():
+                    back_copy(k).wait_recv()
+
+                @pl.when(jnp.logical_not(is_mid))
+                def _():
+                    out_copy(k).wait_recv()
+
+                @pl.when(jnp.logical_not(is_mid & owner))
+                def _():
+                    @pl.when(has_outer)
+                    def _():
+                        out_copy(k).start()
+
+                    chunk_out(k)
+
+            reduce_small(it)
 
         def down_back(i):
             @pl.when(first_section)
@@ -564,21 +722,34 @@
                 resb[lax.rem(i, 2)] = grad.astype(BF16)
                 hop_copy(i, cotb).start()
 
+        def advance(step, place):
+            def body(it, carry):
+                reduce(it)
+                return carry
+
+            first, stop = 0, 0
+            for at, (lo, hi) in EARLY[place].items():
+                first = jnp.where(first_section & (step == at), lo, first)
+                stop = jnp.where(first_section & (step == at), hi, stop)
+            lax.fori_loop(first, stop, body, 0)
+
         def backward(step):
-            behind = jnp.where(first_section, 0, 1)
-            n_rest = step - behind
-            n_in = n_rest - 1
+            later = jnp.where(step >= blocks - 1, 1, 0)
+            idle = first_section & (step == blocks - 2)
+            n_rest = jnp.where(first_section, jnp.where(idle, -1, step - later), step)
+            idle_in = first_section & (step == blocks - 1)
+            n_in = jnp.where(first_section, jnp.where(idle_in, -1, step - 1 - later), step - 1)
             last = blocks - 1
 
             @pl.when(step < blocks)
             def _():
                 down_back(last - step)
 
-            @pl.when(step == jnp.where(first_section, blocks - 1, blocks + 2))
+            @pl.when(step == jnp.where(first_section, blocks - 1, blocks + 1))
             def _():
                 loop(2, mlp_grads)
 
-            @pl.when(n_in == 0)
+            @pl.when(step == 1)
             def _():
                 for copy in act_copies:
                     copy.wait()
@@ -591,20 +762,22 @@
             def _():
                 i = last - n_rest
                 out_back(i)
+                advance(step, 0)
                 each_block(i, attend_back)
+                advance(step, 1)
                 qkv_back(i)
-
-        loop(blocks + 3, backward)
-
+                advance(step, 2)
+
+        loop(blocks + 2, backward)
         ones = jnp.ones((8, length), BF16)
         sown[5:6, : 3 * part] = dot(ones, dqkv[0].reshape(3 * part, length), NT)[0:1]
         soth[5:6, : 3 * part] = dot(ones, dqkv[1].reshape(3 * part, length), NT)[0:1]
         soth[0:4, :] = sown[0:4, :]
-        small_x = send(soth, srec, ss, (0,), to_x)
         small_x.start()
 
         def attention_grads(turn):
             slot = 1 - turn
+            up_part(turn, tiles - 1)
 
             def qkv_part(k):
                 first = (2 * width) // CHUNK + k * (part // CHUNK)
@@ -621,164 +794,12 @@
         for copy in eg_copies:
             copy.start()
 
-        middle = count // 2
-        on_left = d < middle
-        depth = jnp.where(on_left, d, count - 1 - d)
-        has_outer = depth > 0
-        is_mid = depth == middle - 1
-        side = jnp.where(on_left, 0, 1)
-        inner = (s, t, jnp.where(on_left, d + 1, d - 1))
-        outer = (s, t, jnp.where(on_left, d - 1, d + 1))
-        lag = 3
-        lag_in = lag * depth
-        lag_mid = lag * middle
-        lag_out = lag_mid + lag * (middle - depth)
-        lag_all = lag_mid + lag * middle
-
-        def in_copy(k):
-            return send(xrec.at[k], cin.at[k], sc, (0, k), inner)
-
-        def cross_copy(k):
-            return send(xrec.at[k], fin.at[k], sc, (1, k), inner)
-
-        def back_copy(k):
-            return send(fin.at[k], fin.at[k], sc, (2, k), inner)
-
-        def out_copy(k):
-            return send(fin.at[k], fin.at[k], sc, (3, k), outer)
-
-        def chunk_out(k):
-            place = 0
-            for name in ("down", "up", "qkv", "out"):
-                number = r[name].shape[0] // CHUNK
-
-                @pl.when((k >= place) & (k < place + number))
-                def _():
-                    at = pl.ds(pl.multiple_of((k - place) * CHUNK, CHUNK), CHUNK)
-                    pltpu.make_async_copy(fin.at[k], r[name].at[at], so.at[0, 2 + k]).start()
-
-                place += number
-
-        s_in = send(sown, scin, ss, (1,), inner)
-        s_cross = send(sown, sfin, ss, (2,), inner)
-        s_back = send(sfin, sfin, ss, (3,), inner)
-        s_out = send(sfin, sfin, ss, (4,), outer)
-
-        def reduce_small(it):
-            small_owner = side == 0
-            begin = chunks - 4
-
-            @pl.when(it == begin)
-            def _():
-                small_x.wait()
-                sown[...] = sown[...] + srec[...]
-
-            @pl.when(it == begin + lag_in)
-            def _():
-                @pl.when(has_outer)
-                def _():
-                    s_in.wait_recv()
-                    sown[...] = sown[...] + scin[...]
-
-                @pl.when(jnp.logical_not(is_mid))
-                def _():
-                    s_in.start()
-
-                @pl.when(is_mid & jnp.logical_not(small_owner))
-                def _():
-                    s_cross.start()
-
-            @pl.when((it == begin + lag_mid) & is_mid & small_owner)
-            def _():
-                s_cross.wait_recv()
-                sfin[...] = sfin[...] + sown[...]
-                s_back.start()
-
-            @pl.when(it == begin + lag_out)
-            def _():
-                @pl.when(is_mid & jnp.logical_not(small_owner))
-                def _():
-                    s_back.wait_recv()
-
-                @pl.when(jnp.logical_not(is_mid))
-                def _():
-                    s_out.wait_recv()
-
-                @pl.when(has_outer)
-                def _():
-                    s_out.start()
-
-        def reduce(it):
-            @pl.when(it < chunks)
-            def _():
-                k = it
-                x_copy(k).wait()
-                xrec[k] = (pool[own_at(k), :] + xrec[k].astype(F32)).astype(BF16)
-
-            k_in = it - lag_in
-
-            @pl.when((k_in >= 0) & (k_in < chunks))
-            def _():
-                k = k_in
-                owner = lax.rem(k, 2) == side
-
-                @pl.when(has_outer)
-                def _():
-                    in_copy(k).wait_recv()
-                    xrec[k] = (xrec[k].astype(F32) + cin[k].astype(F32)).astype(BF16)
-
-                @pl.when(jnp.logical_not(is_mid))
-                def _():
-                    in_copy(k).start()
-
-                @pl.when(is_mid & jnp.logical_not(owner))
-                def _():
-                    cross_copy(k).start()
-
-            k_mid = it - lag_mid
-
-            @pl.when((k_mid >= 0) & (k_mid < chunks) & is_mid)
-            def _():
-                k = k_mid
-
-                @pl.when(lax.rem(k, 2) == side)
-                def _():
-                    cross_copy(k).wait_recv()
-                    fin[k] = (xrec[k].astype(F32) + fin[k].astype(F32)).astype(BF16)
-                    back_copy(k).start()
-
-                    @pl.when(has_outer)
-                    def _():
-                        out_copy(k).start()
-
-                    chunk_out(k)
-
-            k_out = it - lag_out
-
-            @pl.when((k_out >= 0) & (k_out < chunks))
-            def _():
-                k = k_out
-                owner = lax.rem(k, 2) == side
-
-                @pl.when(is_mid & jnp.logical_not(owner))
-                def _():
-                    back_copy(k).wait_recv()
-
-                @pl.when(jnp.logical_not(is_mid))
-                def _():
-                    out_copy(k).wait_recv()
-
-                @pl.when(jnp.logical_not(is_mid & owner))
-                def _():
-                    @pl.when(has_outer)
-                    def _():
-                        out_copy(k).start()
-
-                    chunk_out(k)
-
-            reduce_small(it)
-
-        loop(chunks + lag_all, reduce)
+        def rest(it, carry):
+            reduce(it)
+            return carry
+
+        begun = max(hi for place in EARLY for _, hi in place.values())
+        lax.fori_loop(jnp.where(first_section, begun, 0), chunks + lag_all, rest, 0)
         small[...] = sfin[...]
 
         @pl.when(jnp.logical_not(is_mid))

time: 300 us -> 286 us (0.953)
  Pallas kernels: 282 us -> 268 us
    pallas_call x1, Pallas kernels: 282 us -> 268 us  [per_device(): pl.pallas_call(make_kernel(names, count), out_shape=[jax.ShapeDtypeStruct...]
where the time goes in v3:
time: 286 us
  Pallas kernels  268 us (94%)
  local copies, waits for them, and re-layouts  9.83 us (3%)
  other arithmetic  7.27 us (3%)
    pallas_call x1, Pallas kernels, per_device(): pl.pallas_call(make_kernel(names, count), out_shape=[jax.ShapeDtypeStruct...  268 us
    unnamed x31, local copies, waits for them, and re-layouts  6.52 us

profile of v3, /device:TPU:0, one launch (start us, length us, event | category | flops | bytes accessed | tf_op | source)
XLA Modules:
  0.0 286.2 jit_solution(6540355063005971213)
XLA Ops:
  0.7 1.3 copy.34
  2.0 0.9 pad.11.refs_0_
  2.9 0.0 copy-start.9
  2.9 0.0 copy-start.10
  2.9 0.0 copy-start.11
  3.0 0.0 copy-start.7
  3.0 0.1 copy.33
  3.1 0.9 pad.12.refs_1_
  4.0 0.0 copy-done.12
  4.0 0.1 reshape.36
  4.1 0.0 copy-done.8
  4.2 0.1 concatenate.3
  4.2 0.6 convert_element_type.27.refs_6_
  4.8 0.6 copy.35
  5.4 268.3 %layers.1 = (bf16[2,768,256]{2,1,0:T(8,128)(2,1)}, bf16[2,768,256]{2,1,0:T(8,128)(2,1)}, bf16[768,768]{1,0:T(8,128)(2,1)}, bf16[768,768]{1,0:T(8,128)(2,1)}, bf1...) custom-call(bf16[2,768,256]{2,1,0:T(8,128)(2,1)} %pad.11.refs_0_, ...), custom_call_target="tpu_custom_call" | custom-call | tf_op jit(solution)/shard_map/layers/pallas_call | solution.py:962
  273.8 4.3 %bitcast_convert_fusion = (f32[1,768,768]{2,1,0:T(8,128)}, f32[1,768,768]{2,1,0:T(8,128)}) fusion(bf16[768,768]{1,0:T(8,128)(2,1)} %get-tuple-element.25, bf16[768,768]{1,0:T(8,128)(2,1)} %get-tuple-element.24), kind=kLoop, calls=%fused_computation.2 | loop fusion | flops 1179648 | bytes 7077888 | tf_op jit(solution)/shard_map/broadcast_in_dim | solution.py:989
  278.1 0.2 convert_bitcast_fusion.1
  278.3 2.8 copy.28
  281.0 1.7 copy.27
  282.7 0.6 fusion
  283.3 0.1 reshape_squeeze.3
  283.4 0.6 slice.31
  284.0 1.4 convert_bitcast_fusion
  285.4 0.9 bitcast_convert_fusion.2
  (22 shorter events, 0.1 us)
Async XLA Ops:
  0.6 2.3 copy-start.3
  2.9 1.1 copy-start.12
  2.9 1.2 copy-start.6
  2.9 1.2 copy-start.8
  2.9 1.2 copy-start.9
  2.9 1.2 copy-start.10
  2.9 1.2 copy-start.11
  3.0 1.9 copy-start.7
  273.8 4.3 %copy-start.1 = (bf16[2,768,256]{2,1,0:T(8,128)(2,1)S(1)}, bf16[2,768,256]{2,1,0:T(8,128)(2,1)}, u32[]{:S(2)}) copy-start(bf16[2,768,256]{2,1,0:T(8,128)(2,1)} %get-tuple-element.19) | copy-start | bytes 2359300
  273.8 4.3 %copy-start.2 = (bf16[2,768,256]{2,1,0:T(8,128)(2,1)S(1)}, bf16[2,768,256]{2,1,0:T(8,128)(2,1)}, u32[]{:S(2)}) copy-start(bf16[2,768,256]{2,1,0:T(8,128)(2,1)} %get-tuple-element.20) | copy-start | bytes 2359300
  281.0 1.7 copy-start.5
  281.0 3.0 %copy-start = (bf16[576,768]{1,0:T(8,128)(2,1)S(1)}, bf16[576,768]{1,0:T(8,128)(2,1)}, u32[]{:S(2)}) copy-start(bf16[576,768]{1,0:T(8,128)(2,1)} %get-tuple-element.22) | copy-start | bytes 2654212
  282.7 2.7 copy-start.4

commit v4 on v3

--- a/solution.py
+++ b/solution.py
@@ -9,8 +9,17 @@
 EPS = 1e-05
 SCALE = 0.125
 NEGATIVE = -1e30
-CHUNK = 64
-EARLY = ({3: (0, 1), 4: (5, 6)}, {3: (1, 4), 4: (6, 7)}, {3: (4, 5), 4: (7, 8)})
+CHUNK = 32
+LAG = 4
+HEADS_FORWARD = 3
+HEADS_BACKWARD = 3
+EARLY = ({3: (0, 2), 4: (8, 12), 5: (16, 21)}, {3: (2, 7), 4: (12, 15), 5: (21, 23)}, {3: (7, 8), 4: (15, 16), 5: (23, 26)})
+PLAN = {
+    "down": ((0, 1, 2, 3, -1, -1, -1, -1), (0, 1, 2, 3, -1, -1, -1, -1)),
+    "rest": ((0, -1, -1, 1, 2, 3, -1, -1), (-1, 0, 1, 2, 3, -1, -1, -1)),
+    "in": ((-1, 0, -1, -1, 1, 2, 3, -1), (-1, -1, 0, 1, -1, 2, 3, -1)),
+    "grads": ((-1, -1, -1, 0, 1, -1, -1, -1), (-1, -1, -1, -1, -1, -1, -1, 2)),
+}
 MESH = pl.DeviceIdType.MESH
 F32 = jnp.float32
 BF16 = jnp.bfloat16
@@ -60,14 +69,14 @@
         r = dict(zip(names, refs, strict=True))
         xin, cot, misc, seg = r["xin"], r["cot"], r["misc"], r["seg"]
         act, eg, small = r["act"], r["eg"], r["small"]
-        wq, wo, wu, wd, mc = r["wq"], r["wo"], r["wu"], r["wd"], r["mc"]
+        wq, wo, wud, mc = r["wq"], r["wo"], r["wud"], r["mc"]
         xbuf, cotb, resb, outt = r["xbuf"], r["cotb"], r["resb"], r["outt"]
         pool, nrm, n2t = r["pool"], r["nrm"], r["n2t"]
         qt, kt, vt, kn, vn = r["qt"], r["kt"], r["vt"], r["kn"], r["vn"]
         ctx, lse, segc = r["ctx"], r["lse"], r["segc"]
         gp, hid, gmt, gat = r["gp"], r["hid"], r["gmt"], r["gat"]
         dot_, dqkv, dk, dv = r["dot"], r["dqkv"], r["dk"], r["dv"]
-        ex, xrec, cin, fin = r["ex"], r["xrec"], r["cin"], r["fin"]
+        ex, xrec, cin, ready = r["ex"], r["xrec"], r["cin"], r["ready"]
         sown, soth, srec, scin, sfin = r["sown"], r["soth"], r["srec"], r["scin"], r["sfin"]
         sl, sg, sw, se, sh, so, sr, sc, ss = (
             r[name] for name in ("sl", "sg", "sw", "se", "sh", "so", "sr", "sc", "ss"))
@@ -76,8 +85,10 @@
         slots, hs = wq.shape[0], wo.shape[1] // HD
         heads = slots * hs
         part = wo.shape[1]
-        units = wu.shape[2]
+        units = wud.shape[1]
         chunks = xrec.shape[0]
+        wu = [wud.at[pl.ds(slot * width, width)] for slot in range(slots)]
+        wd = [wud.at[pl.ds((slots + slot) * width, width)] for slot in range(slots)]
 
         s = lax.axis_index("section")
         t = lax.axis_index("tensor")
@@ -165,9 +176,9 @@
         misc_local.start()
         misc_x.start()
         locals_, pieces = [], []
-        for which, (name, target, cuts) in enumerate((("wqh", wq, 2), ("woh", wo, 1), ("wuh", wu, 2), ("wdh", wd, 3))):
+        for which, (name, target, cuts) in enumerate((("wqh", [wq.at[0], wq.at[1]], 2), ("woh", [wo.at[0], wo.at[1]], 1), ("wuh", wu, 2), ("wdh", wd, 3))):
             source = r[name]
-            locals_.append(pltpu.make_async_copy(source, target.at[0], sl.at[4 + which]))
+            locals_.append(pltpu.make_async_copy(source, target[0], sl.at[4 + which]))
             half = source.shape[0] // 2
             step = half // cuts
             group = []
@@ -175,8 +186,8 @@
                 at = pl.ds(pl.multiple_of(parity * half + cut * step, 16), step)
                 place = 3 * which + cut
                 group.append((
-                    send(source.at[at], target.at[1, at], sw, (0, place), to_x),
-                    send(target.at[1, at], target.at[1, at], sw, (1, place), to_pair),
+                    send(source.at[at], target[1].at[at], sw, (0, place), to_x),
+                    send(target[1].at[at], target[1].at[at], sw, (1, place), to_pair),
                 ))
             pieces.append(group)
         for local, group in zip(locals_, pieces, strict=True):
@@ -208,6 +219,9 @@
 
         def ex_at(kind, i):
             return pl.ds(pl.multiple_of(kind * length + i * rows, rows), rows)
+
+        def shifted(i):
+            return lax.rem(i + 1, blocks)
 
         def pair_copy(kind, i):
             return send(ex.at[ex_at(2 * kind, i)], ex.at[ex_at(2 * kind + 1, i)], se, (kind, i), to_core)
@@ -251,16 +265,19 @@
         attn_gain, mlp_gain, out_bias, down_bias = (mc[0, i : i + 1, :] for i in range(4))
         have(0)
 
-        def masked(scores, i, j0, j1, diagonal):
+        def allowed(i, j0, j1, diagonal):
             same = segc[j0:j1, :]
             same = jnp.concatenate([same] * (rows // same.shape[1]), axis=1)
             cols = slice(i * rows, (i + 1) * rows)
-            allowed = same == seg[pl.ds(xh, 1), cols].astype(F32)
+            keep = same == seg[pl.ds(xh, 1), cols].astype(F32)
             if diagonal:
-                key = lax.broadcasted_iota(jnp.int32, scores.shape, 0)
-                query = lax.broadcasted_iota(jnp.int32, scores.shape, 1)
-                allowed = allowed & (key <= query)
-            return jnp.where(allowed, scores, NEGATIVE)
+                key = lax.broadcasted_iota(jnp.int32, keep.shape, 0)
+                query = lax.broadcasted_iota(jnp.int32, keep.shape, 1)
+                keep = keep & (key <= query)
+            return keep
+
+        def masked(scores, i, j0, j1, diagonal):
+            return jnp.where(allowed(i, j0, j1, diagonal), scores, NEGATIVE)
 
         def key_parts(i):
             parts = [(i * rows, (i + 1) * rows, True)]
@@ -288,28 +305,32 @@
                     kn[head, cols, :] = key[at].T.astype(BF16)
                     vn[head, cols, :] = value[at].T.astype(BF16)
 
-        def attend(i, h):
+        def attend(i, group):
             cols = slice(i * rows, (i + 1) * rows)
             parts = key_parts(i)
-            query = qt[i, h]
-            scores = [masked(dot(kn[h, a:b], query), i, a, b, g) for a, b, g in parts]
-            highest = scores[0].max(axis=0, keepdims=True)
-            for score in scores[1:]:
-                highest = jnp.maximum(highest, score.max(axis=0, keepdims=True))
-            total, context = 0.0, 0.0
-            for score, (a, b, _) in zip(scores, parts, strict=True):
-                power = jnp.exp(score - highest)
-                total = total + row_sum(power)
-                context = context + dot(vt[h, :, a:b], power.astype(BF16))
-            ctx[h, :, cols] = (context / total).astype(BF16)
-            lse[i, h] = highest + jnp.log(total)
-
-        def each_block(i, body):
+            scores = [[masked(dot(kn[h, a:b], qt[i, h]), i, a, b, g) for a, b, g in parts] for h in group]
+            tops = []
+            for score in scores:
+                top = score[0].max(axis=0, keepdims=True)
+                for more in score[1:]:
+                    top = jnp.maximum(top, more.max(axis=0, keepdims=True))
+                tops.append(top)
+            powers = [[jnp.exp(one - top) for one in score] for score, top in zip(scores, tops, strict=True)]
+            totals = [sum(row_sum(one) for one in power) for power in powers]
+            contexts = [
+                sum(dot(vt[h, :, a:b], one.astype(BF16)) for one, (a, b, _) in zip(power, parts, strict=True))
+                for h, power in zip(group, powers, strict=True)
+            ]
+            for h, top, total, context in zip(group, tops, totals, contexts, strict=True):
+                ctx[h, :, cols] = (context / total).astype(BF16)
+                lse[i, h] = top + jnp.log(total)
+
+        def each_block(i, body, number):
             for block in range(blocks):
 
                 @pl.when(i == block)
                 def _():
-                    loop(heads, lambda h: body(block, h))
+                    loop(heads // number, lambda n: body(block, [n * number + k for k in range(number)]))
 
         def attention_rows(i):
             @pl.when(last_section & (i == 0))
@@ -322,14 +343,14 @@
                 hop_core(i, xbuf).wait()
 
             project(i)
-            each_block(i, attend)
+            each_block(i, attend, HEADS_FORWARD)
 
             @pl.when(i == 0)
             def _():
                 have(1)
 
             context = ctx[:, :, at_row(i)].reshape(heads * HD, rows)
-            pair_send(0, i, dot(context, wo[...].reshape(heads * HD, width), TN))
+            pair_send(0, shifted(i), dot(context, wo[...].reshape(heads * HD, width), TN))
 
             for step, (which, cut) in enumerate(((2, 0), (2, 1), (3, 0), (3, 1))):
 
@@ -342,19 +363,19 @@
                 hop_copy(i + 1, xbuf).wait_recv()
                 hop_core(i + 1, xbuf).start()
 
-        def mlp_rows(i):
+        def up_rows(i):
             @pl.when(i == 0)
             def _():
                 have(2)
 
-            branch = pair_sum(0, i) + out_bias
+            branch = pair_sum(0, shifted(i)) + out_bias
             middle = expanded(xbuf[i]) + centred(branch)
             pool[mid_at(i), :] = middle
             normed = middle * norm_factor(middle) * mlp_gain
             n2t[:, at_row(i)] = normed.T.astype(BF16)
             normed = normed.astype(BF16)
             for slot in range(slots):
-                pre = dot(normed, wu[slot]) + mc[slot, 4:5, :]
+                pre = dot(normed, wu[slot][...]) + mc[slot, 4:5, :]
                 square = pre * pre
                 bend = jnp.tanh(GELU_C * pre * (1.0 + GELU_A * square))
                 grow = 0.5 * (1.0 + bend)
@@ -362,6 +383,7 @@
                 slope = GELU_C * (1.0 + 3.0 * GELU_A * square)
                 gp[slot, i] = (grow + 0.5 * pre * (1.0 - bend * bend) * slope).astype(BF16)
 
+        def down_rows(i):
             @pl.when(i == 0)
             def _():
                 @pl.when(first_section)
@@ -370,10 +392,10 @@
 
                 have(3)
 
-            branch = dot(hid[0, i], wd[0], NT)
+            branch = dot(hid[0, i], wd[0][...], NT)
             for slot in range(1, slots):
-                branch = branch + dot(hid[slot, i], wd[slot], NT)
-            pair_send(1, i, branch)
+                branch = branch + dot(hid[slot, i], wd[slot][...], NT)
+            pair_send(1, shifted(i), branch)
 
         def keep_out(i, value):
             @pl.when((i == t) | (i == t_x))
@@ -381,7 +403,7 @@
                 outt[jnp.where(i == t, 0, 1)] = value.T.astype(BF16)
 
         def result_rows(i):
-            result = pool[mid_at(i), :] + centred(pair_sum(1, i) + down_bias)
+            result = pool[mid_at(i), :] + centred(pair_sum(1, shifted(i)) + down_bias)
             keep_out(i, result)
 
             @pl.when(first_section)
@@ -395,27 +417,32 @@
                 hop_copy(i, xbuf).start()
 
         def forward(step):
-            i_mlp = jnp.where(first_section, step - blocks, step - 1)
-            i_res = i_mlp - 1
+            i_up = jnp.where(first_section, step - blocks, step - 1)
+            i_down = jnp.where(first_section, step - 2 * blocks, step - 1)
+            i_res = i_down - 1
             some_res = (i_res >= 0) & (i_res < blocks)
 
             @pl.when(step < blocks)
             def _():
                 attention_rows(step)
 
-            @pl.when(last_section & some_res)
+            @pl.when(last_section & some_res & (i_res < blocks - 1))
             def _():
                 result_rows(i_res)
 
-            @pl.when((i_mlp >= 0) & (i_mlp < blocks))
-            def _():
-                mlp_rows(i_mlp)
+            @pl.when((i_up >= 0) & (i_up < blocks))
+            def _():
+                up_rows(i_up)
+
+            @pl.when((i_down >= 0) & (i_down < blocks))
+            def _():
+                down_rows(i_down)
 
             @pl.when(first_section & some_res)
             def _():
                 result_rows(i_res)
 
-        loop(2 * blocks + 1, forward)
+        loop(3 * blocks + 1, forward)
 
         def rows_out(target, which):
             return (
@@ -424,8 +451,6 @@
             )
 
         act_copies = rows_out(act, 0)
-        for copy in act_copies:
-            copy.start()
 
         @pl.when(first_section)
         def _():
@@ -433,14 +458,21 @@
 
         def other_at(k):
             row = k * CHUNK
-            early = lax.div(row, 2 * rows) * length + 2 * rows + lax.rem(row, 2 * rows)
-            return pl.ds(pl.multiple_of(jnp.where(row < 8 * rows, early, row - 8 * rows), CHUNK), CHUNK)
+            third = jnp.where(row < 3 * rows, 0, jnp.where(row < 6 * rows, 1, 2))
+            place = row - third * 3 * rows
+            kind = jnp.where(place < rows, 0, jnp.where(place < 2 * rows, 1, 2))
+            row = kind * (length - rows) + (blocks - 1 - third) * rows + place
+            return pl.ds(pl.multiple_of(row, CHUNK), CHUNK)
 
         def own_at(k):
             row = k * CHUNK
-            late = jnp.where(row < 7 * rows, row - 5 * rows, row - 3 * rows)
-            late = jnp.where(row < 5 * rows, row + 4 * rows, late)
-            return pl.ds(pl.multiple_of(jnp.where(row < 2 * rows, row + 2 * rows, late), CHUNK), CHUNK)
+            third = jnp.where(row < 3 * rows, 0, jnp.where(row < 6 * rows, 1, 2))
+            place = row - third * 3 * rows
+            down = jnp.where(place < rows, place + 3 * rows, place + 6 * rows)
+            up = jnp.where(place < 2 * rows, place + rows, place + 4 * rows)
+            rest = jnp.where(place < rows, place, place + 3 * rows)
+            row = jnp.where(third == 0, down, jnp.where(third == 1, up, rest))
+            return pl.ds(pl.multiple_of(row, CHUNK), CHUNK)
 
         def x_copy(k):
             return send(ex.at[other_at(k)], xrec.at[k], sr, (k,), to_x)
@@ -476,57 +508,57 @@
             put(turn, first, dot(n2t[at, :], gp[1 - turn].reshape(length, units)))
             start(turn, first, tile // CHUNK)
 
-        def mlp_grads(turn):
+        def down_grads(turn):
             loop(tiles, lambda k: down_part(turn, k))
-            loop(tiles - 1, lambda k: up_part(turn, k))
+
+        def up_grads(turn):
+            loop(tiles, lambda k: up_part(turn, k))
 
         middle = count // 2
         on_left = d < middle
         depth = jnp.where(on_left, d, count - 1 - d)
         has_outer = depth > 0
         is_mid = depth == middle - 1
-        side = jnp.where(on_left, 0, 1)
         inner = (s, t, jnp.where(on_left, d + 1, d - 1))
         outer = (s, t, jnp.where(on_left, d - 1, d + 1))
-        lag = 3
-        lag_in = lag * depth
-        lag_mid = lag * middle
-        lag_out = lag_mid + lag * (middle - depth)
-        lag_all = lag_mid + lag * middle
+        lag_in = LAG * depth
+        lag_mid = LAG * middle
+        lag_out = lag_mid + LAG * (middle - 1 - depth)
+        lag_all = lag_mid + LAG * (middle - 1)
+
+        def fin_at(k):
+            return pl.ds(pl.multiple_of(k * CHUNK, CHUNK), CHUNK)
 
         def in_copy(k):
             return send(xrec.at[k], cin.at[k], sc, (0, k), inner)
 
         def cross_copy(k):
-            return send(xrec.at[k], fin.at[k], sc, (1, k), inner)
-
-        def back_copy(k):
-            return send(fin.at[k], fin.at[k], sc, (2, k), inner)
+            return send(xrec.at[k], wud.at[fin_at(k)], sc, (1, k), inner)
 
         def out_copy(k):
-            return send(fin.at[k], fin.at[k], sc, (3, k), outer)
-
-        def chunk_out(k):
-            place = 0
-            for name in ("down", "up", "qkv", "out"):
-                number = r[name].shape[0] // CHUNK
-
-                @pl.when((k >= place) & (k < place + number))
-                def _():
-                    at = pl.ds(pl.multiple_of((k - place) * CHUNK, CHUNK), CHUNK)
-                    pltpu.make_async_copy(fin.at[k], r[name].at[at], so.at[0, 2 + k]).start()
-
-                place += number
+            return send(wud.at[fin_at(k)], wud.at[fin_at(k)], sc, (2, k), outer)
+
+        outs, place = [], 0
+        for which, name in enumerate(("down", "up", "qkv", "out")):
+            number = r[name].shape[0]
+            copy = pltpu.make_async_copy(wud.at[pl.ds(place, number)], r[name], so.at[0, 2 + which])
+            place += number
+            outs.append((place // CHUNK - 1, copy))
+
+        def matrix_out(k):
+            for final, copy in outs:
+
+                @pl.when(k == final)
+                def _():
+                    copy.start()
 
         small_x = send(soth, srec, ss, (0,), to_x)
         s_in = send(sown, scin, ss, (1,), inner)
         s_cross = send(sown, sfin, ss, (2,), inner)
-        s_back = send(sfin, sfin, ss, (3,), inner)
-        s_out = send(sfin, sfin, ss, (4,), outer)
+        s_out = send(sfin, sfin, ss, (3,), outer)
 
         def reduce_small(it):
-            small_owner = side == 0
-            begin = chunks - 4
+            begin = chunks - 8
 
             @pl.when(it == begin)
             def _():
@@ -544,21 +576,16 @@
                 def _():
                     s_in.start()
 
-                @pl.when(is_mid & jnp.logical_not(small_owner))
+                @pl.when(is_mid)
                 def _():
                     s_cross.start()
 
-            @pl.when((it == begin + lag_mid) & is_mid & small_owner)
-            def _():
-                s_cross.wait_recv()
-                sfin[...] = sfin[...] + sown[...]
-                s_back.start()
-
             @pl.when(it == begin + lag_out)
             def _():
-                @pl.when(is_mid & jnp.logical_not(small_owner))
-                def _():
-                    s_back.wait_recv()
+                @pl.when(is_mid)
+                def _():
+                    s_cross.wait()
+                    sfin[...] = sfin[...] + sown[...]
 
                 @pl.when(jnp.logical_not(is_mid))
                 def _():
@@ -569,6 +596,10 @@
                     s_out.start()
 
         def reduce(it):
+            @pl.when((it == 0) & is_mid)
+            def _():
+                pl.semaphore_signal(ready, inc=1, device_id=inner, device_id_type=MESH)
+
             @pl.when(it < chunks)
             def _():
                 k = it
@@ -580,7 +611,6 @@
             @pl.when((k_in >= 0) & (k_in < chunks))
             def _():
                 k = k_in
-                owner = lax.rem(k, 2) == side
 
                 @pl.when(has_outer)
                 def _():
@@ -591,50 +621,34 @@
                 def _():
                     in_copy(k).start()
 
-                @pl.when(is_mid & jnp.logical_not(owner))
-                def _():
+                @pl.when(is_mid)
+                def _():
+                    @pl.when(k == 0)
+                    def _():
+                        pl.semaphore_wait(ready, 1)
+
                     cross_copy(k).start()
 
-            k_mid = it - lag_mid
-
-            @pl.when((k_mid >= 0) & (k_mid < chunks) & is_mid)
-            def _():
-                k = k_mid
-
-                @pl.when(lax.rem(k, 2) == side)
+            k_out = it - lag_out
+
+            @pl.when((k_out >= 0) & (k_out < chunks))
+            def _():
+                k = k_out
+
+                @pl.when(is_mid)
                 def _():
                     cross_copy(k).wait_recv()
-                    fin[k] = (xrec[k].astype(F32) + fin[k].astype(F32)).astype(BF16)
-                    back_copy(k).start()
-
-                    @pl.when(has_outer)
-                    def _():
-                        out_copy(k).start()
-
-                    chunk_out(k)
-
-            k_out = it - lag_out
-
-            @pl.when((k_out >= 0) & (k_out < chunks))
-            def _():
-                k = k_out
-                owner = lax.rem(k, 2) == side
-
-                @pl.when(is_mid & jnp.logical_not(owner))
-                def _():
-                    back_copy(k).wait_recv()
+                    wud[fin_at(k), :] = (xrec[k].astype(F32) + wud[fin_at(k), :].astype(F32)).astype(BF16)
 
                 @pl.when(jnp.logical_not(is_mid))
                 def _():
                     out_copy(k).wait_recv()
 
-                @pl.when(jnp.logical_not(is_mid & owner))
-                def _():
-                    @pl.when(has_outer)
-                    def _():
-                        out_copy(k).start()
-
-                    chunk_out(k)
+                @pl.when(has_outer)
+                def _():
+                    out_copy(k).start()
+
+                matrix_out(k)
 
             reduce_small(it)
 
@@ -652,10 +666,10 @@
             sown[3:4, :] += row_sum(grad.astype(F32))
             branch = 0.0
             for slot, sums in ((0, sown), (1, soth)):
-                before = (dot(grad, wd[slot]) * gp[slot, i].astype(F32)).astype(BF16)
+                before = (dot(grad, wd[slot][...]) * gp[slot, i].astype(F32)).astype(BF16)
                 gp[slot, i] = before
                 sums[4:5, :] += row_sum(before.astype(F32))
-                branch = branch + dot(before, wu[slot], NT)
+                branch = branch + dot(before, wu[slot][...], NT)
             pair_send(0, i, branch)
 
         def out_back(i):
@@ -670,34 +684,41 @@
             for h in range(heads):
                 dot_[i, h] = back[h * HD : (h + 1) * HD]
 
-        def attend_back(i, h):
-            slot, place = lax.div(h, hs), lax.rem(h, hs)
-            query, back = qt[i, h], dot_[i, h]
+        def attend_back(i, group):
             parts = key_parts(i)
             cols = slice(i * rows, (i + 1) * rows)
+            masks = [jnp.where(allowed(i, a, b, g), 0.0, NEGATIVE) for a, b, g in parts]
             probs, g_probs = [], []
-            centre = 0.0
-            for a, b, g in parts:
-                prob = jnp.exp(masked(dot(kn[h, a:b], query), i, a, b, g) - lse[i, h])
-                g_prob = dot(vn[h, a:b], back)
-                centre = centre + row_sum(prob * g_prob)
-                probs.append(prob)
-                g_probs.append(g_prob)
-            g_query = 0.0
-            for prob, g_prob, (a, b, _) in zip(probs, g_probs, parts, strict=True):
-                g_score = (prob * (g_prob - centre)).astype(BF16)
-                g_value = dot(back, prob.astype(BF16), NT)
-                g_key = dot(query, g_score, NT)
-                g_query = g_query + dot(kt[h, :, a:b], g_score)
-                if i == blocks - 1:
-                    dv[h, :, a:b] = g_value
-                    dk[h, :, a:b] = g_key
-                else:
-                    dv[h, :, a:b] += g_value
-                    dk[h, :, a:b] += g_key
-            dqkv[slot, 0, place, :, cols] = (g_query * SCALE).astype(BF16)
-            dqkv[slot, 1, place, :, cols] = dk[h, :, cols].astype(BF16)
-            dqkv[slot, 2, place, :, cols] = dv[h, :, cols].astype(BF16)
+            for h in group:
+                less = [mask - lse[i, h] for mask in masks]
+                probs.append([jnp.exp(dot(kn[h, a:b], qt[i, h]) + one) for one, (a, b, _) in zip(less, parts, strict=True)])
+                g_probs.append([dot(vn[h, a:b], dot_[i, h]) for a, b, _ in parts])
+            centres = [
+                sum(row_sum(x * y) for x, y in zip(prob, g_prob, strict=True))
+                for prob, g_prob in zip(probs, g_probs, strict=True)
+            ]
+            g_scores = [
+                [(x * (y - centre)).astype(BF16) for x, y in zip(prob, g_prob, strict=True)]
+                for prob, g_prob, centre in zip(probs, g_probs, centres, strict=True)
+            ]
+            g_values = [[dot(dot_[i, h], x.astype(BF16), NT) for x in prob] for h, prob in zip(group, probs, strict=True)]
+            g_keys = [[dot(qt[i, h], x, NT) for x in g_score] for h, g_score in zip(group, g_scores, strict=True)]
+            g_queries = [
+                sum(dot(kt[h, :, a:b], x) for x, (a, b, _) in zip(g_score, parts, strict=True))
+                for h, g_score in zip(group, g_scores, strict=True)
+            ]
+            for h, g_value, g_key, g_query in zip(group, g_values, g_keys, g_queries, strict=True):
+                slot, place = lax.div(h, hs), lax.rem(h, hs)
+                for (a, b, _), value, key in zip(parts, g_value, g_key, strict=True):
+                    if i == blocks - 1:
+                        dv[h, :, a:b] = value
+                        dk[h, :, a:b] = key
+                    else:
+                        dv[h, :, a:b] += value
+                        dk[h, :, a:b] += key
+                dqkv[slot, 0, place, :, cols] = (g_query * SCALE).astype(BF16)
+                dqkv[slot, 1, place, :, cols] = dk[h, :, cols].astype(BF16)
+                dqkv[slot, 2, place, :, cols] = dv[h, :, cols].astype(BF16)
 
         def qkv_back(i):
             branch = 0.0
@@ -733,42 +754,58 @@
                 stop = jnp.where(first_section & (step == at), hi, stop)
             lax.fori_loop(first, stop, body, 0)
 
+        def planned(step, name):
+            found = -1
+            for at, (first, last) in enumerate(zip(*PLAN[name], strict=True)):
+                found = jnp.where(step == at, jnp.where(first_section, first, last), found)
+            return found
+
         def backward(step):
-            later = jnp.where(step >= blocks - 1, 1, 0)
-            idle = first_section & (step == blocks - 2)
-            n_rest = jnp.where(first_section, jnp.where(idle, -1, step - later), step)
-            idle_in = first_section & (step == blocks - 1)
-            n_in = jnp.where(first_section, jnp.where(idle_in, -1, step - 1 - later), step - 1)
+            n_down, n_in, n_rest = (planned(step, name) for name in ("down", "in", "rest"))
+            n_grad = planned(step, "grads")
             last = blocks - 1
 
-            @pl.when(step < blocks)
-            def _():
-                down_back(last - step)
-
-            @pl.when(step == jnp.where(first_section, blocks - 1, blocks + 1))
-            def _():
-                loop(2, mlp_grads)
-
-            @pl.when(step == 1)
+            @pl.when(n_down >= 0)
+            def _():
+                down_back(last - n_down)
+
+            @pl.when(step == 0)
+            def _():
+                @pl.when(last_section)
+                def _():
+                    result_rows(last)
+
+                for copy in act_copies:
+                    copy.start()
+
+            @pl.when((n_grad == 0) | (n_grad == 2))
+            def _():
+                loop(2, down_grads)
+
+            @pl.when(n_in == 0)
             def _():
                 for copy in act_copies:
                     copy.wait()
 
-            @pl.when((n_in >= 0) & (n_in < blocks))
+            @pl.when(n_in >= 0)
             def _():
                 in_back(last - n_in)
 
-            @pl.when((n_rest >= 0) & (n_rest < blocks))
+            @pl.when(n_rest >= 0)
             def _():
                 i = last - n_rest
                 out_back(i)
                 advance(step, 0)
-                each_block(i, attend_back)
+                each_block(i, attend_back, HEADS_BACKWARD)
                 advance(step, 1)
                 qkv_back(i)
                 advance(step, 2)
 
-        loop(blocks + 2, backward)
+            @pl.when(n_grad >= 1)
+            def _():
+                loop(2, up_grads)
+
+        loop(len(PLAN["in"][0]), backward)
         ones = jnp.ones((8, length), BF16)
         sown[5:6, : 3 * part] = dot(ones, dqkv[0].reshape(3 * part, length), NT)[0:1]
         soth[5:6, : 3 * part] = dot(ones, dqkv[1].reshape(3 * part, length), NT)[0:1]
@@ -777,7 +814,6 @@
 
         def attention_grads(turn):
             slot = 1 - turn
-            up_part(turn, tiles - 1)
 
             def qkv_part(k):
                 first = (2 * width) // CHUNK + k * (part // CHUNK)
@@ -806,40 +842,26 @@
         def _():
             s_in.wait_send()
 
-        @pl.when(is_mid & (side == 1))
-        def _():
-            s_cross.wait_send()
-
-        @pl.when(is_mid & (side == 0))
-        def _():
-            s_back.wait_send()
-
         @pl.when(has_outer)
         def _():
             s_out.wait_send()
 
         def drain(k):
-            owner = lax.rem(k, 2) == side
-
             @pl.when(jnp.logical_not(is_mid))
             def _():
                 in_copy(k).wait_send()
 
-            @pl.when(is_mid & jnp.logical_not(owner))
+            @pl.when(is_mid)
             def _():
                 cross_copy(k).wait_send()
 
-            @pl.when(is_mid & owner)
-            def _():
-                back_copy(k).wait_send()
-
             @pl.when(has_outer)
             def _():
                 out_copy(k).wait_send()
 
-            pltpu.make_async_copy(fin.at[k], r["down"].at[pl.ds(0, CHUNK)], so.at[0, 2 + k]).wait()
-
         loop(chunks, drain)
+        for _, copy in outs:
+            copy.wait()
 
         @pl.when(last_section)
         def _():
@@ -905,8 +927,7 @@
     scratch = {
         "wq": ((slots, 3 * part, width), BF16),
         "wo": ((slots, part, width), BF16),
-        "wu": ((slots, width, units), BF16),
-        "wd": ((slots, width, units), BF16),
+        "wud": ((2 * slots * width, units), BF16),
         "mc": ((slots, 8, width), F32),
         "xbuf": ((blocks, rows, width), BF16),
         "cotb": ((blocks, rows, width), BF16),
@@ -934,7 +955,6 @@
         "ex": ((4 * length, width), BF16),
         "xrec": ((chunks, CHUNK, width), BF16),
         "cin": ((chunks, CHUNK, width), BF16),
-        "fin": ((chunks, CHUNK, width), BF16),
         "sown": ((8, width), F32),
         "soth": ((8, width), F32),
         "srec": ((8, width), F32),
@@ -948,10 +968,11 @@
         "sw": dma((2, 2, 12)),
         "se": dma((2, 2, blocks)),
         "sh": dma((2, 2, blocks)),
-        "so": dma((2, 2 + chunks)),
+        "so": dma((2, 6)),
         "sr": dma((2, chunks)),
-        "sc": dma((2, 4, chunks)),
-        "ss": dma((2, 5)),
+        "sc": dma((2, 3, chunks)),
+        "ss": dma((2, 4)),
+        "ready": pltpu.SemaphoreType.REGULAR,
     }
     in_vmem = {"seg", "small"}
 

time: 286 us -> 267 us (0.934)
  Pallas kernels: 268 us -> 248 us
    pallas_call x1, Pallas kernels: 268 us -> 248 us  [per_device(): pl.pallas_call(make_kernel(names, count), out_shape=[jax.ShapeDtypeStruct...]
where the time goes in v4:
time: 267 us; the launch traced here: 266 us
  Pallas kernels  248 us (93%)
  local copies, waits for them, and re-layouts  9.83 us (4%)
  other arithmetic  7.27 us (3%)
    pallas_call x1, Pallas kernels, per_device(): pl.pallas_call(make_kernel(names, count), out_shape=[jax.ShapeDtypeStruct...  248 us
    unnamed x31, local copies, waits for them, and re-layouts  6.52 us

profile of v4, /device:TPU:0, one launch (start us, length us, event | category | flops | bytes accessed | tf_op | source)
XLA Modules:
  0.0 266.4 jit_solution(12471067621100090626)
XLA Ops:
  0.6 0.0 copy-start.3
  0.7 1.3 copy.34
  2.0 0.9 pad.11.refs_0_
  2.9 0.0 copy-start.9
  2.9 0.0 copy-start.10
  2.9 0.0 copy-start.11
  3.0 0.0 copy-start.7
  3.0 0.1 copy.33
  3.1 0.9 pad.12.refs_1_
  4.0 0.1 reshape.36
  4.2 0.1 concatenate.3
  4.2 0.6 convert_element_type.27.refs_6_
  4.8 0.0 copy-done.7
  4.8 0.6 copy.35
  5.4 248.5 %layers.1 = (bf16[2,768,256]{2,1,0:T(8,128)(2,1)}, bf16[2,768,256]{2,1,0:T(8,128)(2,1)}, bf16[768,768]{1,0:T(8,128)(2,1)}, bf16[768,768]{1,0:T(8,128)(2,1)}, bf1...) custom-call(bf16[2,768,256]{2,1,0:T(8,128)(2,1)} %pad.11.refs_0_, ...), custom_call_target="tpu_custom_call" | custom-call | tf_op jit(solution)/shard_map/layers/pallas_call | solution.py:983
  253.9 4.3 %bitcast_convert_fusion = (f32[1,768,768]{2,1,0:T(8,128)}, f32[1,768,768]{2,1,0:T(8,128)}) fusion(bf16[768,768]{1,0:T(8,128)(2,1)} %get-tuple-element.25, bf16[768,768]{1,0:T(8,128)(2,1)} %get-tuple-element.24), kind=kLoop, calls=%fused_computation.2 | loop fusion | flops 1179648 | bytes 7077888 | tf_op jit(solution)/shard_map/broadcast_in_dim | solution.py:1010
  258.2 0.2 convert_bitcast_fusion.1
  258.4 2.8 %copy.28 = f32[1,2,256,1,767]{2,3,4,1,0:T(1,128)} copy(f32[1,2,256,1,767]{2,4,1,3,0:T(8,128)S(1)} %get-tuple-element.43) | data formatting | bytes 3141632
  261.2 1.7 copy.27
  262.9 0.6 fusion
  263.5 0.1 reshape_squeeze.3
  263.6 0.6 slice.31
  264.2 1.4 convert_bitcast_fusion
  265.5 0.9 bitcast_convert_fusion.2
  (22 shorter events, 0.1 us)
Async XLA Ops:
  0.6 2.3 copy-start.3
  2.9 1.1 copy-start.12
  2.9 1.2 copy-start.6
  2.9 1.2 copy-start.8
  2.9 1.2 copy-start.9
  2.9 1.2 copy-start.10
  2.9 1.2 copy-start.11
  3.0 1.9 copy-start.7
  253.9 4.3 %copy-start.1 = (bf16[2,768,256]{2,1,0:T(8,128)(2,1)S(1)}, bf16[2,768,256]{2,1,0:T(8,128)(2,1)}, u32[]{:S(2)}) copy-start(bf16[2,768,256]{2,1,0:T(8,128)(2,1)} %get-tuple-element.19) | copy-start | bytes 2359300
  253.9 4.3 %copy-start.2 = (bf16[2,768,256]{2,1,0:T(8,128)(2,1)S(1)}, bf16[2,768,256]{2,1,0:T(8,128)(2,1)}, u32[]{:S(2)}) copy-start(bf16[2,768,256]{2,1,0:T(8,128)(2,1)} %get-tuple-element.20) | copy-start | bytes 2359300
  261.2 1.7 copy-start.5
  261.2 3.0 %copy-start = (bf16[576,768]{1,0:T(8,128)(2,1)S(1)}, bf16[576,768]{1,0:T(8,128)(2,1)}, u32[]{:S(2)}) copy-start(bf16[576,768]{1,0:T(8,128)(2,1)} %get-tuple-element.22) | copy-start | bytes 2654212
  262.9 2.7 copy-start.4

commit v5 on v4

--- a/solution.py
+++ b/solution.py
@@ -11,13 +11,20 @@
 NEGATIVE = -1e30
 CHUNK = 32
 LAG = 4
-HEADS_FORWARD = 3
+HEADS_FORWARD = 6
 HEADS_BACKWARD = 3
-EARLY = ({3: (0, 2), 4: (8, 12), 5: (16, 21)}, {3: (2, 7), 4: (12, 15), 5: (21, 23)}, {3: (7, 8), 4: (15, 16), 5: (23, 26)})
+EARLY = (
+    {3: (2, 4), 4: (9, 12), 5: (18, 21)},
+    {3: (4, 8), 4: (12, 17), 5: (21, 23)},
+    {3: (8, 9), 4: (17, 18), 5: (23, 24)},
+    {6: (24, 27)},
+    {3: (0, 2)},
+)
 PLAN = {
     "down": ((0, 1, 2, 3, -1, -1, -1, -1), (0, 1, 2, 3, -1, -1, -1, -1)),
     "rest": ((0, -1, -1, 1, 2, 3, -1, -1), (-1, 0, 1, 2, 3, -1, -1, -1)),
-    "in": ((-1, 0, -1, -1, 1, 2, 3, -1), (-1, -1, 0, 1, -1, 2, 3, -1)),
+    "in": ((-1, 0, -1, -1, -1, -1, 3, -1), (-1, -1, 0, 1, -1, 2, 3, -1)),
+    "late": ((-1, -1, -1, -1, 1, 2, -1, -1), (-1,) * 8),
     "grads": ((-1, -1, -1, 0, 1, -1, -1, -1), (-1, -1, -1, -1, -1, -1, -1, 2)),
 }
 MESH = pl.DeviceIdType.MESH
@@ -67,7 +74,7 @@
 def make_kernel(names, count):
     def kernel(*refs):
         r = dict(zip(names, refs, strict=True))
-        xin, cot, misc, seg = r["xin"], r["cot"], r["misc"], r["seg"]
+        xin, cot, seg = r["xin"], r["cot"], r["seg"]
         act, eg, small = r["act"], r["eg"], r["small"]
         wq, wo, wud, mc = r["wq"], r["wo"], r["wud"], r["mc"]
         xbuf, cotb, resb, outt = r["xbuf"], r["cotb"], r["resb"], r["outt"]
@@ -171,12 +178,15 @@
         def _():
             rows_in(xin, to_xy)[2].start()
 
-        misc_local = pltpu.make_async_copy(misc, mc.at[0], sl.at[1])
-        misc_x = send(misc, mc.at[1], sg, (3,), to_x)
-        misc_local.start()
+        mc[0] = jnp.zeros_like(mc[0])
+        for row, name in enumerate(("attn_gain", "mlp_gain", "out_bias", "down_bias", "up_bias")):
+            mc[0, row : row + 1, :] = r[name][...].astype(F32)
+        for row in range(2):
+            mc[0, 5 + row : 6 + row, : wo.shape[1]] = r["qv_bias"][0, row : row + 1, :].astype(F32)
+        misc_x = send(mc.at[0], mc.at[1], sg, (3,), to_x)
         misc_x.start()
         locals_, pieces = [], []
-        for which, (name, target, cuts) in enumerate((("wqh", [wq.at[0], wq.at[1]], 2), ("woh", [wo.at[0], wo.at[1]], 1), ("wuh", wu, 2), ("wdh", wd, 3))):
+        for which, (name, target, cuts) in enumerate((("wqh", [wq.at[0], wq.at[1]], 2), ("woh", [wo.at[0], wo.at[1]], 1), ("wuh", wu, 2), ("wdh", wd, 4))):
             source = r[name]
             locals_.append(pltpu.make_async_copy(source, target[0], sl.at[4 + which]))
             half = source.shape[0] // 2
@@ -184,21 +194,23 @@
             group = []
             for cut in range(cuts):
                 at = pl.ds(pl.multiple_of(parity * half + cut * step, 16), step)
-                place = 3 * which + cut
+                place = 4 * which + cut
                 group.append((
                     send(source.at[at], target[1].at[at], sw, (0, place), to_x),
                     send(target[1].at[at], target[1].at[at], sw, (1, place), to_pair),
                 ))
             pieces.append(group)
-        for local, group in zip(locals_, pieces, strict=True):
+        for which, (local, group) in enumerate(zip(locals_, pieces, strict=True)):
+            if which == 3:
+
+                @pl.when(last_section)
+                def _():
+                    for copy in rows_in(cot, to_x)[:3]:
+                        copy.start()
+
             local.start()
             for across, _ in group:
                 across.start()
-
-        @pl.when(last_section)
-        def _():
-            for copy in rows_in(cot, to_x)[:3]:
-                copy.start()
 
         def pass_on(which, *cuts):
             for cut in cuts:
@@ -214,7 +226,7 @@
 
         sown[...] = jnp.zeros_like(sown)
         soth[...] = jnp.zeros_like(soth)
-        segment = seg[pl.ds(xh, 1), :]
+        segment = seg[xh]
         segc[...] = jnp.broadcast_to(segment.astype(F32), (128, length)).T
 
         def ex_at(kind, i):
@@ -254,13 +266,12 @@
         def _():
             pass_on(1, 0)
             pass_on(2, 0, 1)
-            pass_on(3, 0, 1, 2)
             copies = rows_in(cot, to_x)
             rows_wait(copies, cotb)
+            pass_on(3, 0, 1, 2, 3)
             copies[2].wait_send()
             rows_in(xin, to_xy)[2].wait_send()
 
-        misc_local.wait()
         misc_x.wait()
         attn_gain, mlp_gain, out_bias, down_bias = (mc[0, i : i + 1, :] for i in range(4))
         have(0)
@@ -269,7 +280,7 @@
             same = segc[j0:j1, :]
             same = jnp.concatenate([same] * (rows // same.shape[1]), axis=1)
             cols = slice(i * rows, (i + 1) * rows)
-            keep = same == seg[pl.ds(xh, 1), cols].astype(F32)
+            keep = same == seg[xh, :, cols].astype(F32)
             if diagonal:
                 key = lax.broadcasted_iota(jnp.int32, keep.shape, 0)
                 query = lax.broadcasted_iota(jnp.int32, keep.shape, 1)
@@ -292,10 +303,10 @@
             cols = at_row(i)
             for slot in range(slots):
                 three = dot(wq[slot], normed, NT)
-                bias = jnp.broadcast_to(mc[slot, 5:6, : 2 * part], (8, 2 * part)).T[:, 0:1]
-                query = (three[:part] + bias[:part]).astype(BF16) * SCALE
+                bias = mc[slot, :, :part].T
+                query = (three[:part] + bias[:, 5:6]).astype(BF16) * SCALE
                 key = three[part : 2 * part]
-                value = (three[2 * part :] + bias[part:]).astype(BF16).astype(F32)
+                value = (three[2 * part :] + bias[:, 6:7]).astype(BF16).astype(F32)
                 for h in range(hs):
                     at = slice(h * HD, (h + 1) * HD)
                     head = slot * hs + h
@@ -377,19 +388,22 @@
             for slot in range(slots):
                 pre = dot(normed, wu[slot][...]) + mc[slot, 4:5, :]
                 square = pre * pre
-                bend = jnp.tanh(GELU_C * pre * (1.0 + GELU_A * square))
-                grow = 0.5 * (1.0 + bend)
-                hid[slot, i] = (pre * grow).astype(BF16)
-                slope = GELU_C * (1.0 + 3.0 * GELU_A * square)
-                gp[slot, i] = (grow + 0.5 * pre * (1.0 - bend * bend) * slope).astype(BF16)
+                bend = jnp.tanh(pre * (GELU_C + (GELU_C * GELU_A) * square))
+                grow = 0.5 + 0.5 * bend
+                value = pre * grow
+                hid[slot, i] = value.astype(BF16)
+                slope = GELU_C + (3.0 * GELU_C * GELU_A) * square
+                gp[slot, i] = (grow + value * (1.0 - bend) * slope).astype(BF16)
+
+            for step, cut in ((0, 2), (1, 3)):
+
+                @pl.when((i == step) & first_section)
+                def _():
+                    pass_on(3, cut)
 
         def down_rows(i):
             @pl.when(i == 0)
             def _():
-                @pl.when(first_section)
-                def _():
-                    pass_on(3, 2)
-
                 have(3)
 
             branch = dot(hid[0, i], wd[0][...], NT)
@@ -761,9 +775,10 @@
             return found
 
         def backward(step):
-            n_down, n_in, n_rest = (planned(step, name) for name in ("down", "in", "rest"))
+            n_down, n_in, n_rest, n_late = (planned(step, name) for name in ("down", "in", "rest", "late"))
             n_grad = planned(step, "grads")
             last = blocks - 1
+            advance(step, 3)
 
             @pl.when(n_down >= 0)
             def _():
@@ -781,6 +796,7 @@
             @pl.when((n_grad == 0) | (n_grad == 2))
             def _():
                 loop(2, down_grads)
+                advance(step, 4)
 
             @pl.when(n_in == 0)
             def _():
@@ -796,12 +812,21 @@
                 i = last - n_rest
                 out_back(i)
                 advance(step, 0)
+
+                @pl.when(n_late >= 0)
+                def _():
+                    in_back(last - n_late)
+
+                @pl.when(n_grad == 1)
+                def _():
+                    loop(2, up_grads)
+
                 each_block(i, attend_back, HEADS_BACKWARD)
                 advance(step, 1)
                 qkv_back(i)
                 advance(step, 2)
 
-            @pl.when(n_grad >= 1)
+            @pl.when(n_grad == 2)
             def _():
                 loop(2, up_grads)
 
@@ -903,8 +928,6 @@
     def features_first(array):
         return jnp.pad(array[:, :, 0, :].transpose(0, 2, 1), ((0, 0), (0, width - kept), (0, 0)))
 
-    qv_row = jnp.pad(qv_bias.reshape(1, 2 * part), ((0, 0), (0, width - 2 * part)))
-    rows_of = [attn_gain, mlp_gain, out_bias, down_bias, up_bias, qv_row, up_bias, qv_row]
     inputs = {
         "xin": features_first(block_input),
         "cot": features_first(cotangent),
@@ -912,8 +935,13 @@
         "woh": out_weight[0],
         "wuh": up_projection_weight[0],
         "wdh": down_projection_weight[0],
-        "misc": jnp.concatenate(rows_of).astype(F32),
-        "seg": segments[:, 0, :],
+        "attn_gain": attn_gain,
+        "mlp_gain": mlp_gain,
+        "out_bias": out_bias,
+        "down_bias": down_bias,
+        "up_bias": up_bias,
+        "qv_bias": qv_bias,
+        "seg": segments,
     }
     outputs = {
         "act": ((micros, width, rows), BF16),
@@ -965,7 +993,7 @@
     semaphores = {
         "sl": dma((8,)),
         "sg": dma((2, 4)),
-        "sw": dma((2, 2, 12)),
+        "sw": dma((2, 2, 16)),
         "se": dma((2, 2, blocks)),
         "sh": dma((2, 2, blocks)),
         "so": dma((2, 6)),
@@ -974,7 +1002,7 @@
         "ss": dma((2, 4)),
         "ready": pltpu.SemaphoreType.REGULAR,
     }
-    in_vmem = {"seg", "small"}
+    in_vmem = {"attn_gain", "mlp_gain", "out_bias", "down_bias", "up_bias", "qv_bias", "seg", "small"}
 
     def spec(name):
         return pl.BlockSpec(memory_space=pltpu.VMEM if name in in_vmem else pl.ANY)

time: 267 us -> 262 us (0.981)
  Pallas kernels: 248 us -> 245 us
    pallas_call x1, Pallas kernels: 248 us -> 245 us  [per_device(): pl.pallas_call(make_kernel(names, count), out_shape=[jax.ShapeDtypeStruct...]
    unnamed x31 -> x16, local copies, waits for them, and re-layouts: 6.52 us -> 5.88 us
where the time goes in v5:
time: 262 us
  Pallas kernels  245 us (94%)
  local copies, waits for them, and re-layouts  9.05 us (3%)
  other arithmetic  6.66 us (3%)
    pallas_call x1, Pallas kernels, per_device(): pl.pallas_call(make_kernel(names, count), out_shape=[jax.ShapeDtypeStruct...  245 us
    unnamed x16, local copies, waits for them, and re-layouts  5.88 us

profile of v5, /device:TPU:0, one launch (start us, length us, event | category | flops | bytes accessed | tf_op | source)
XLA Modules:
  0.0 261.5 jit_solution(4655586367311130532)
XLA Ops:
  0.6 0.0 copy-start.3
  0.7 1.3 copy.32
  2.0 0.9 pad.7.refs_0_
  2.9 0.0 copy-done.3
  2.9 0.1 copy.31
  3.0 0.9 pad.8.refs_1_
  4.0 245.1 %layers.1 = (bf16[2,768,256]{2,1,0:T(8,128)(2,1)}, bf16[2,768,256]{2,1,0:T(8,128)(2,1)}, bf16[768,768]{1,0:T(8,128)(2,1)}, bf16[768,768]{1,0:T(8,128)(2,1)}, bf1...) custom-call(bf16[2,768,256]{2,1,0:T(8,128)(2,1)} %pad.7.refs_0_, ...), custom_call_target="tpu_custom_call" | custom-call | tf_op jit(solution)/shard_map/layers/pallas_call | solution.py:1011
  249.1 0.0 copy-start.1
  249.1 0.0 copy-start.2
  249.1 4.3 %bitcast_convert_fusion = (f32[1,768,768]{2,1,0:T(8,128)}, f32[1,768,768]{2,1,0:T(8,128)}) fusion(bf16[768,768]{1,0:T(8,128)(2,1)} %get-tuple-element.25, bf16[768,768]{1,0:T(8,128)(2,1)} %get-tuple-element.24), kind=kLoop, calls=%fused_computation.2 | loop fusion | flops 1179648 | bytes 7077888 | tf_op jit(solution)/shard_map/broadcast_in_dim | solution.py:1038
  253.4 0.0 copy-done.1
  253.4 0.0 copy-done.2
  253.4 0.2 convert_bitcast_fusion.1
  253.6 2.8 %copy.28 = f32[1,2,256,1,767]{2,3,4,1,0:T(1,128)} copy(f32[1,2,256,1,767]{2,4,1,3,0:T(8,128)S(1)} %get-tuple-element.43) | data formatting | bytes 3141632
  256.3 0.0 copy-start.5
  256.3 1.7 copy.27
  258.0 0.0 copy-done.5
  258.0 0.6 fusion
  258.6 0.1 reshape_squeeze.3
  258.7 0.6 slice.31
  259.3 0.0 copy-done
  259.3 1.4 convert_bitcast_fusion
  260.7 0.0 copy-done.4
  260.7 0.9 bitcast_convert_fusion.2
  (3 shorter events, 0.0 us)
Async XLA Ops:
  0.6 2.3 copy-start.3
  249.1 4.3 %copy-start.1 = (bf16[2,768,256]{2,1,0:T(8,128)(2,1)S(1)}, bf16[2,768,256]{2,1,0:T(8,128)(2,1)}, u32[]{:S(2)}) copy-start(bf16[2,768,256]{2,1,0:T(8,128)(2,1)} %get-tuple-element.19) | copy-start | bytes 2359300
  249.1 4.3 %copy-start.2 = (bf16[2,768,256]{2,1,0:T(8,128)(2,1)S(1)}, bf16[2,768,256]{2,1,0:T(8,128)(2,1)}, u32[]{:S(2)}) copy-start(bf16[2,768,256]{2,1,0:T(8,128)(2,1)} %get-tuple-element.20) | copy-start | bytes 2359300
  256.3 1.7 copy-start.5
  256.3 3.0 %copy-start = (bf16[576,768]{1,0:T(8,128)(2,1)S(1)}, bf16[576,768]{1,0:T(8,128)(2,1)}, u32[]{:S(2)}) copy-start(bf16[576,768]{1,0:T(8,128)(2,1)} %get-tuple-element.22) | copy-start | bytes 2654212
  258.0 2.7 %copy-start.4 = (bf16[192,768]{1,0:T(8,128)(2,1)S(1)}, bf16[192,768]{1,0:T(8,128)(2,1)}, u32[]{:S(2)}) copy-start(bf16[192,768]{1,0:T(8,128)(2,1)} %get-tuple-element.23) | copy-start | bytes 884740

commit v6 on v5

--- a/solution.py
+++ b/solution.py
@@ -9,16 +9,16 @@
 EPS = 1e-05
 SCALE = 0.125
 NEGATIVE = -1e30
-CHUNK = 32
-LAG = 4
+CHUNK = 64
+LAG = 3
 HEADS_FORWARD = 6
 HEADS_BACKWARD = 3
 EARLY = (
-    {3: (2, 4), 4: (9, 12), 5: (18, 21)},
-    {3: (4, 8), 4: (12, 17), 5: (21, 23)},
-    {3: (8, 9), 4: (17, 18), 5: (23, 24)},
-    {6: (24, 27)},
-    {3: (0, 2)},
+    {3: (1, 3), 4: (7, 9), 5: (14, 16)},
+    {3: (3, 6), 4: (9, 13), 5: (16, 17)},
+    {3: (6, 7), 4: (13, 14), 5: (17, 18)},
+    {6: (18, 20)},
+    {3: (0, 1)},
 )
 PLAN = {
     "down": ((0, 1, 2, 3, -1, -1, -1, -1), (0, 1, 2, 3, -1, -1, -1, -1)),
@@ -383,7 +383,6 @@
             middle = expanded(xbuf[i]) + centred(branch)
             pool[mid_at(i), :] = middle
             normed = middle * norm_factor(middle) * mlp_gain
-            n2t[:, at_row(i)] = normed.T.astype(BF16)
             normed = normed.astype(BF16)
             for slot in range(slots):
                 pre = dot(normed, wu[slot][...]) + mc[slot, 4:5, :]
@@ -521,6 +520,10 @@
             first = width // CHUNK + k * (tile // CHUNK)
             put(turn, first, dot(n2t[at, :], gp[1 - turn].reshape(length, units)))
             start(turn, first, tile // CHUNK)
+
+        def turn_normed(i):
+            middle = pool[mid_at(i), :]
+            n2t[:, at_row(i)] = (middle * norm_factor(middle) * mlp_gain).T.astype(BF16)
 
         def down_grads(turn):
             loop(tiles, lambda k: down_part(turn, k))
@@ -572,7 +575,7 @@
         s_out = send(sfin, sfin, ss, (3,), outer)
 
         def reduce_small(it):
-            begin = chunks - 8
+            begin = chunks - 4
 
             @pl.when(it == begin)
             def _():
@@ -666,16 +669,20 @@
 
             reduce_small(it)
 
-        def down_back(i):
+        def grad_rows(i):
             @pl.when(first_section)
             def _():
                 hop_copy(i, cotb).wait_recv()
                 hop_core(i, cotb).start()
                 hop_core(i, cotb).wait()
-
+                turn_grad(i)
+
+        def turn_grad(i):
+            gmt[:, at_row(i)] = centred(cotb[i].astype(F32)).T.astype(BF16)
+
+        def down_back(i):
             grad = centred(cotb[i].astype(F32))
             pool[grad_at(i), :] = grad
-            gmt[:, at_row(i)] = grad.T.astype(BF16)
             grad = grad.astype(BF16)
             sown[3:4, :] += row_sum(grad.astype(F32))
             branch = 0.0
@@ -774,12 +781,34 @@
                 found = jnp.where(step == at, jnp.where(first_section, first, last), found)
             return found
 
+        def turns(first, stop, body):
+            def one(turn, carry):
+                body(turn)
+                return carry
+
+            lax.fori_loop(first, stop, one, 0)
+
         def backward(step):
             n_down, n_in, n_rest, n_late = (planned(step, name) for name in ("down", "in", "rest", "late"))
             n_grad = planned(step, "grads")
             last = blocks - 1
             advance(step, 3)
 
+            @pl.when(step == jnp.where(first_section, blocks - 2, 2 * blocks - 1))
+            def _():
+                loop(blocks, turn_normed)
+
+            @pl.when(last_section & (step == 2 * blocks - 1))
+            def _():
+                loop(blocks, turn_grad)
+
+            @pl.when(n_down >= 0)
+            def _():
+                grad_rows(last - n_down)
+
+            early = jnp.where(n_grad == 0, 1, 0)
+            turns(0, early, down_grads)
+
             @pl.when(n_down >= 0)
             def _():
                 down_back(last - n_down)
@@ -795,7 +824,7 @@
 
             @pl.when((n_grad == 0) | (n_grad == 2))
             def _():
-                loop(2, down_grads)
+                turns(early, 2, down_grads)
                 advance(step, 4)
 
             @pl.when(n_in == 0)
@@ -926,7 +955,8 @@
     chunks = (2 * width + 4 * part) // CHUNK
 
     def features_first(array):
-        return jnp.pad(array[:, :, 0, :].transpose(0, 2, 1), ((0, 0), (0, width - kept), (0, 0)))
+        first = array[:, :, 0, :].transpose(2, 0, 1)
+        return jnp.pad(first, ((0, width - kept), (0, 0), (0, 0))).transpose(1, 0, 2)
 
     inputs = {
         "xin": features_first(block_input),

time: 262 us -> 256 us (0.977)
  Pallas kernels: 245 us -> 240 us
    pallas_call x1, Pallas kernels: 245 us -> 240 us  [per_device(): pl.pallas_call(make_kernel(names, count), out_shape=[jax.ShapeDtypeStruct...]
where the time goes in v6:
time: 256 us
  Pallas kernels  240 us (94%)
  local copies, waits for them, and re-layouts  9.04 us (4%)
  other arithmetic  6.66 us (3%)
    pallas_call x1, Pallas kernels, per_device(): pl.pallas_call(make_kernel(names, count), out_shape=[jax.ShapeDtypeStruct...  240 us
    unnamed x16, local copies, waits for them, and re-layouts  5.88 us

profile of v6, /device:TPU:0, one launch (start us, length us, event | category | flops | bytes accessed | tf_op | source)
XLA Modules:
  0.0 256.1 jit_solution(432016570309963688)
XLA Ops:
  0.6 0.0 copy-start.3
  0.7 1.3 copy.31
  2.0 0.9 pad_bitcast_fusion.refs_1_
  2.9 0.0 copy-done.3
  2.9 0.1 copy.32
  3.0 0.9 pad_bitcast_fusion.1.refs_0_
  3.9 239.7 %layers.1 = (bf16[2,768,256]{2,1,0:T(8,128)(2,1)}, bf16[2,768,256]{2,1,0:T(8,128)(2,1)}, bf16[768,768]{1,0:T(8,128)(2,1)}, bf16[768,768]{1,0:T(8,128)(2,1)}, bf1...) custom-call(bf16[2,768,256]{2,1,0:T(8,128)(2,1)} %pad_bitcast_fusion.1.refs_0_, ...), custom_call_target="tpu_custom_call" | custom-call | tf_op jit(solution)/shard_map/layers/pallas_call | solution.py:1041
  243.6 0.0 copy-start.1
  243.6 0.0 copy-start.2
  243.6 4.3 %bitcast_convert_fusion = (f32[1,768,768]{2,1,0:T(8,128)}, f32[1,768,768]{2,1,0:T(8,128)}) fusion(bf16[768,768]{1,0:T(8,128)(2,1)} %get-tuple-element.25, bf16[768,768]{1,0:T(8,128)(2,1)} %get-tuple-element.24), kind=kLoop, calls=%fused_computation.2 | loop fusion | flops 1179648 | bytes 7077888 | tf_op jit(solution)/shard_map/broadcast_in_dim | solution.py:1068
  247.9 0.0 copy-done.1
  247.9 0.0 copy-done.2
  247.9 0.2 convert_bitcast_fusion.1
  248.1 2.8 %copy.28 = f32[1,2,256,1,767]{2,3,4,1,0:T(1,128)} copy(f32[1,2,256,1,767]{2,4,1,3,0:T(8,128)S(1)} %get-tuple-element.43) | data formatting | bytes 3141632
  250.9 0.0 copy-start.5
  250.9 1.7 copy.27
  252.6 0.0 copy-done.5
  252.6 0.6 fusion
  253.2 0.1 reshape_squeeze.3
  253.3 0.6 slice.31
  253.9 0.0 copy-done
  253.9 1.4 convert_bitcast_fusion
  255.2 0.0 copy-done.4
  255.2 0.9 bitcast_convert_fusion.2
  (3 shorter events, 0.0 us)
Async XLA Ops:
  0.6 2.3 copy-start.3
  243.6 4.3 %copy-start.1 = (bf16[2,768,256]{2,1,0:T(8,128)(2,1)S(1)}, bf16[2,768,256]{2,1,0:T(8,128)(2,1)}, u32[]{:S(2)}) copy-start(bf16[2,768,256]{2,1,0:T(8,128)(2,1)} %get-tuple-element.19) | copy-start | bytes 2359300
  243.6 4.3 %copy-start.2 = (bf16[2,768,256]{2,1,0:T(8,128)(2,1)S(1)}, bf16[2,768,256]{2,1,0:T(8,128)(2,1)}, u32[]{:S(2)}) copy-start(bf16[2,768,256]{2,1,0:T(8,128)(2,1)} %get-tuple-element.20) | copy-start | bytes 2359300
  250.9 1.7 copy-start.5
  250.9 3.0 %copy-start = (bf16[576,768]{1,0:T(8,128)(2,1)S(1)}, bf16[576,768]{1,0:T(8,128)(2,1)}, u32[]{:S(2)}) copy-start(bf16[576,768]{1,0:T(8,128)(2,1)} %get-tuple-element.22) | copy-start | bytes 2654212
  252.6 2.7 %copy-start.4 = (bf16[192,768]{1,0:T(8,128)(2,1)S(1)}, bf16[192,768]{1,0:T(8,128)(2,1)}, u32[]{:S(2)}) copy-start(bf16[192,768]{1,0:T(8,128)(2,1)} %get-tuple-element.23) | copy-start | bytes 884740

commit v7 on v6

--- a/solution.py
+++ b/solution.py
@@ -14,10 +14,10 @@
 HEADS_FORWARD = 6
 HEADS_BACKWARD = 3
 EARLY = (
-    {3: (1, 3), 4: (7, 9), 5: (14, 16)},
-    {3: (3, 6), 4: (9, 13), 5: (16, 17)},
-    {3: (6, 7), 4: (13, 14), 5: (17, 18)},
-    {6: (18, 20)},
+    {3: (1, 4), 4: (8, 10), 5: (16, 18)},
+    {3: (4, 7), 4: (10, 15), 5: (18, 19)},
+    {3: (7, 8), 4: (15, 16), 5: (19, 20)},
+    {6: (20, 23)},
     {3: (0, 1)},
 )
 PLAN = {
@@ -685,13 +685,14 @@
             pool[grad_at(i), :] = grad
             grad = grad.astype(BF16)
             sown[3:4, :] += row_sum(grad.astype(F32))
-            branch = 0.0
+            befores = []
             for slot, sums in ((0, sown), (1, soth)):
                 before = (dot(grad, wd[slot][...]) * gp[slot, i].astype(F32)).astype(BF16)
                 gp[slot, i] = before
                 sums[4:5, :] += row_sum(before.astype(F32))
-                branch = branch + dot(before, wu[slot][...], NT)
-            pair_send(0, i, branch)
+                befores.append(before)
+            both = jnp.concatenate([wu[slot][...] for slot in range(slots)], axis=1)
+            pair_send(0, i, dot(jnp.concatenate(befores, axis=1), both, NT))
 
         def out_back(i):
             grad, gain_grad = norm_back(pair_sum(0, i), pool[mid_at(i), :], mlp_gain)
@@ -742,11 +743,8 @@
                 dqkv[slot, 2, place, :, cols] = dv[h, :, cols].astype(BF16)
 
         def qkv_back(i):
-            branch = 0.0
-            for slot in range(slots):
-                three = dqkv[slot, :, :, :, at_row(i)].reshape(3 * part, rows)
-                branch = branch + dot(three, wq[slot], TN)
-            pair_send(1, i, branch)
+            three = dqkv[:, :, :, :, at_row(i)].reshape(slots * 3 * part, rows)
+            pair_send(1, i, dot(three, wq[...].reshape(slots * 3 * part, width), TN))
 
         def in_back(i):
             grad, gain_grad = norm_back(pair_sum(1, i), expanded(xbuf[i]), attn_gain)

time: 256 us -> 255 us (level)
  no operation moved by 1% of the time
where the time goes in v7:
time: 255 us
  Pallas kernels  239 us (94%)
  local copies, waits for them, and re-layouts  9.04 us (4%)
  other arithmetic  6.66 us (3%)
    pallas_call x1, Pallas kernels, per_device(): pl.pallas_call(make_kernel(names, count), out_shape=[jax.ShapeDtypeStruct...  239 us
    unnamed x16, local copies, waits for them, and re-layouts  5.88 us

profile of v7, /device:TPU:0, one launch (start us, length us, event | category | flops | bytes accessed | tf_op | source)
XLA Modules:
  0.0 255.0 jit_solution(12590322181756789763)
XLA Ops:
  0.6 0.0 copy-start.3
  0.7 1.3 copy.31
  2.0 0.9 pad_bitcast_fusion.refs_1_
  2.9 0.0 copy-done.3
  2.9 0.1 copy.32
  3.0 0.9 pad_bitcast_fusion.1.refs_0_
  3.9 238.6 %layers.1 = (bf16[2,768,256]{2,1,0:T(8,128)(2,1)}, bf16[2,768,256]{2,1,0:T(8,128)(2,1)}, bf16[768,768]{1,0:T(8,128)(2,1)}, bf16[768,768]{1,0:T(8,128)(2,1)}, bf1...) custom-call(bf16[2,768,256]{2,1,0:T(8,128)(2,1)} %pad_bitcast_fusion.1.refs_0_, ...), custom_call_target="tpu_custom_call" | custom-call | tf_op jit(solution)/shard_map/layers/pallas_call | solution.py:1039
  242.6 0.0 copy-start.1
  242.6 0.0 copy-start.2
  242.6 4.3 %bitcast_convert_fusion = (f32[1,768,768]{2,1,0:T(8,128)}, f32[1,768,768]{2,1,0:T(8,128)}) fusion(bf16[768,768]{1,0:T(8,128)(2,1)} %get-tuple-element.25, bf16[768,768]{1,0:T(8,128)(2,1)} %get-tuple-element.24), kind=kLoop, calls=%fused_computation.2 | loop fusion | flops 1179648 | bytes 7077888 | tf_op jit(solution)/shard_map/broadcast_in_dim | solution.py:1066
  246.9 0.0 copy-done.1
  246.9 0.0 copy-done.2
  246.9 0.2 convert_bitcast_fusion.1
  247.0 2.8 %copy.28 = f32[1,2,256,1,767]{2,3,4,1,0:T(1,128)} copy(f32[1,2,256,1,767]{2,4,1,3,0:T(8,128)S(1)} %get-tuple-element.43) | data formatting | bytes 3141632
  249.8 0.0 copy-start.5
  249.8 1.7 copy.27
  251.5 0.0 copy-done.5
  251.5 0.6 fusion
  252.1 0.1 reshape_squeeze.3
  252.2 0.6 slice.31
  252.8 0.0 copy-done
  252.8 1.4 convert_bitcast_fusion
  254.1 0.0 copy-done.4
  254.2 0.9 bitcast_convert_fusion.2
  (3 shorter events, 0.0 us)
Async XLA Ops:
  0.6 2.3 copy-start.3
  242.6 4.3 %copy-start.1 = (bf16[2,768,256]{2,1,0:T(8,128)(2,1)S(1)}, bf16[2,768,256]{2,1,0:T(8,128)(2,1)}, u32[]{:S(2)}) copy-start(bf16[2,768,256]{2,1,0:T(8,128)(2,1)} %get-tuple-element.19) | copy-start | bytes 2359300
  242.6 4.3 %copy-start.2 = (bf16[2,768,256]{2,1,0:T(8,128)(2,1)S(1)}, bf16[2,768,256]{2,1,0:T(8,128)(2,1)}, u32[]{:S(2)}) copy-start(bf16[2,768,256]{2,1,0:T(8,128)(2,1)} %get-tuple-element.20) | copy-start | bytes 2359300
  249.8 1.7 copy-start.5
  249.8 3.0 %copy-start = (bf16[576,768]{1,0:T(8,128)(2,1)S(1)}, bf16[576,768]{1,0:T(8,128)(2,1)}, u32[]{:S(2)}) copy-start(bf16[576,768]{1,0:T(8,128)(2,1)} %get-tuple-element.22) | copy-start | bytes 2654212
  251.5 2.7 %copy-start.4 = (bf16[192,768]{1,0:T(8,128)(2,1)S(1)}, bf16[192,768]{1,0:T(8,128)(2,1)}, u32[]{:S(2)}) copy-start(bf16[192,768]{1,0:T(8,128)(2,1)} %get-tuple-element.23) | copy-start | bytes 884740

commit v8 on v7

--- a/solution.py
+++ b/solution.py
@@ -341,7 +341,8 @@
 
                 @pl.when(i == block)
                 def _():
-                    loop(heads // number, lambda n: body(block, [n * number + k for k in range(number)]))
+                    for first in range(0, heads, number):
+                        body(block, range(first, first + number))
 
         def attention_rows(i):
             @pl.when(last_section & (i == 0))
@@ -405,10 +406,9 @@
             def _():
                 have(3)
 
-            branch = dot(hid[0, i], wd[0][...], NT)
-            for slot in range(1, slots):
-                branch = branch + dot(hid[slot, i], wd[slot][...], NT)
-            pair_send(1, shifted(i), branch)
+            units_all = jnp.concatenate([hid[slot, i] for slot in range(slots)], axis=1)
+            both = jnp.concatenate([wd[slot][...] for slot in range(slots)], axis=1)
+            pair_send(1, shifted(i), dot(units_all, both, NT))
 
         def keep_out(i, value):
             @pl.when((i == t) | (i == t_x))
@@ -730,7 +730,7 @@
                 for h, g_score in zip(group, g_scores, strict=True)
             ]
             for h, g_value, g_key, g_query in zip(group, g_values, g_keys, g_queries, strict=True):
-                slot, place = lax.div(h, hs), lax.rem(h, hs)
+                slot, place = h // hs, h % hs
                 for (a, b, _), value, key in zip(parts, g_value, g_key, strict=True):
                     if i == blocks - 1:
                         dv[h, :, a:b] = value

time: 255 us -> 255 us (level)
  no operation moved by 1% of the time
where the time goes in v8:
time: 255 us
  Pallas kernels  239 us (94%)
  local copies, waits for them, and re-layouts  9.04 us (4%)
  other arithmetic  6.66 us (3%)
    pallas_call x1, Pallas kernels, per_device(): pl.pallas_call(make_kernel(names, count), out_shape=[jax.ShapeDtypeStruct...  239 us
    unnamed x16, local copies, waits for them, and re-layouts  5.88 us

profile of v8, /device:TPU:0, one launch (start us, length us, event | category | flops | bytes accessed | tf_op | source)
XLA Modules:
  0.0 255.1 jit_solution(3785537226847484067)
XLA Ops:
  0.6 0.0 copy-start.3
  0.7 1.3 copy.31
  2.0 0.9 pad_bitcast_fusion.refs_1_
  2.9 0.0 copy-done.3
  2.9 0.1 copy.32
  3.0 0.9 pad_bitcast_fusion.1.refs_0_
  3.9 238.7 %layers.1 = (bf16[2,768,256]{2,1,0:T(8,128)(2,1)}, bf16[2,768,256]{2,1,0:T(8,128)(2,1)}, bf16[768,768]{1,0:T(8,128)(2,1)}, bf16[768,768]{1,0:T(8,128)(2,1)}, bf1...) custom-call(bf16[2,768,256]{2,1,0:T(8,128)(2,1)} %pad_bitcast_fusion.1.refs_0_, ...), custom_call_target="tpu_custom_call" | custom-call | tf_op jit(solution)/shard_map/layers/pallas_call | solution.py:1039
  242.6 0.0 copy-start.1
  242.6 0.0 copy-start.2
  242.7 4.3 %bitcast_convert_fusion = (f32[1,768,768]{2,1,0:T(8,128)}, f32[1,768,768]{2,1,0:T(8,128)}) fusion(bf16[768,768]{1,0:T(8,128)(2,1)} %get-tuple-element.25, bf16[768,768]{1,0:T(8,128)(2,1)} %get-tuple-element.24), kind=kLoop, calls=%fused_computation.2 | loop fusion | flops 1179648 | bytes 7077888 | tf_op jit(solution)/shard_map/broadcast_in_dim | solution.py:1066
  246.9 0.0 copy-done.1
  246.9 0.0 copy-done.2
  246.9 0.2 convert_bitcast_fusion.1
  247.1 2.8 %copy.28 = f32[1,2,256,1,767]{2,3,4,1,0:T(1,128)} copy(f32[1,2,256,1,767]{2,4,1,3,0:T(8,128)S(1)} %get-tuple-element.43) | data formatting | bytes 3141632
  249.9 0.0 copy-start.5
  249.9 1.7 copy.27
  251.6 0.0 copy-done.5
  251.6 0.6 fusion
  252.2 0.1 reshape_squeeze.3
  252.3 0.6 slice.31
  252.9 0.0 copy-done
  252.9 1.4 convert_bitcast_fusion
  254.2 0.0 copy-done.4
  254.2 0.9 bitcast_convert_fusion.2
  (3 shorter events, 0.0 us)
Async XLA Ops:
  0.6 2.3 copy-start.3
  242.6 4.3 %copy-start.1 = (bf16[2,768,256]{2,1,0:T(8,128)(2,1)S(1)}, bf16[2,768,256]{2,1,0:T(8,128)(2,1)}, u32[]{:S(2)}) copy-start(bf16[2,768,256]{2,1,0:T(8,128)(2,1)} %get-tuple-element.19) | copy-start | bytes 2359300
  242.6 4.3 %copy-start.2 = (bf16[2,768,256]{2,1,0:T(8,128)(2,1)S(1)}, bf16[2,768,256]{2,1,0:T(8,128)(2,1)}, u32[]{:S(2)}) copy-start(bf16[2,768,256]{2,1,0:T(8,128)(2,1)} %get-tuple-element.20) | copy-start | bytes 2359300
  249.9 1.7 copy-start.5
  249.9 3.0 %copy-start = (bf16[576,768]{1,0:T(8,128)(2,1)S(1)}, bf16[576,768]{1,0:T(8,128)(2,1)}, u32[]{:S(2)}) copy-start(bf16[576,768]{1,0:T(8,128)(2,1)} %get-tuple-element.22) | copy-start | bytes 2654212
  251.6 2.7 %copy-start.4 = (bf16[192,768]{1,0:T(8,128)(2,1)S(1)}, bf16[192,768]{1,0:T(8,128)(2,1)}, u32[]{:S(2)}) copy-start(bf16[192,768]{1,0:T(8,128)(2,1)} %get-tuple-element.23) | copy-start | bytes 884740
